TPU v7x, 512 devices: a whole 4x8x8 slice. The times are simulated.
512 devices in a mesh: resp: 128 (over z, y, core), section: 4 (over x).
Axes of the slice: x: 4, y: 8, z: 8, core: 2. Of those that a mesh axis runs over, the one named last changes fastest.
Arguments:
- queries: bfloat16 [4, 16384, 4096], P('section', 'resp'), may hold values from -6 to 6
- out_grad: bfloat16 [4, 16384, 4096], P('section', 'resp'), may hold values from -18 to 18
- resp_kv: bfloat16 [4, 16384, 1024], P('section', 'resp'), may hold values from -6 to 6
- prompt_kv: bfloat16 [4, 512, 128, 1024], P('section', 'resp'), may hold values from -6 to 6
- prompt_hidden: bfloat16 [4, 4096, 4096], P('section', 'resp'), may hold values from -6 to 6
- norm_gain: bfloat16 [4, 4096], P('section'), may hold values from 0.25 to 1.75
- kv_weight: bfloat16 [4, 4096, 1024], P('section', 'resp'), may hold values from -0.09375 to 0.09375
- upper_grad: bfloat16 [4096, 4096], P('resp'), may hold values from -3 to 3
- group_list: int32 [512], replicated, may hold values from 0 to 31, as said below
- lengths: int32 [512], P('resp'), may hold values from 1 to 32
- owner_map: int32 [32, 128], replicated, may hold values from 0 to 127, each once within a row
Outputs:
- query_grad: bfloat16 [4, 16384, 4096], P('section', 'resp')
- resp_kv_grad: bfloat16 [4, 16384, 1024], P('section', 'resp')
- prompt_grad: bfloat16 [4, 4096, 4096], P('section', 'resp')
Inputs may be any that keep to these rules, and one draw needn't show every extreme that they name: `group_list`: each of the 32 prompts is named by exactly 16 responses. `owner_map`: each row names every index of resp once.
All inputs are finite; a program needn't handle non-finite values.
Results may differ from a plain program's by a relative error of at most 0.025.
Values may be sent and summed in bfloat16 or wider, within the bound.
No kernel may reach another device: no remote copies, remote signals or barrier semaphores. Data moves between devices by JAX's collectives and lax.ppermute only.
A program may use at most 64 MiB of HBM per device.

v0:
```python
import jax
import jax.numpy as jnp
from jax import lax
from jax.sharding import PartitionSpec as P

QH = 32
KVH = 4
HD = 128


def entering(shard, axis, combine, identity):
    length, here = (lax.axis_size(axis), lax.axis_index(axis))
    everything = lax.all_gather(shard.astype(jnp.bfloat16), axis)
    start = jnp.broadcast_to(jnp.asarray(identity, shard.dtype), shard.shape)

    def turn(k, before):
        at = length - 1 - k
        reached = at > here
        new = combine(before, everything[at].astype(shard.dtype))
        return jnp.where(reached, new, before)

    return lax.fori_loop(0, length, turn, start)


def product(pattern, first_op, second_op):
    return jnp.einsum(pattern, first_op, second_op, preferred_element_type=jnp.float32)


def response_backward(resp_queries, resp_out_grad, own_kv, cached_kv, resp_lengths):
    batch_size = resp_queries.shape[0]
    resp_rows = resp_queries.shape[1]
    prompt_len = cached_kv.shape[1]
    per_group = QH // KVH
    kv_width = KVH * HD
    scaling = HD ** (-0.5)
    shaped = resp_queries.reshape(batch_size, resp_rows, KVH, per_group, HD)
    all_keys = jnp.concatenate([cached_kv[:, :, :kv_width], own_kv[:, :, :kv_width]], axis=1)
    all_keys = all_keys.reshape(batch_size, prompt_len + resp_rows, KVH, HD)
    all_values = jnp.concatenate([cached_kv[:, :, kv_width:], own_kv[:, :, kv_width:]], axis=1)
    all_values = all_values.reshape(batch_size, prompt_len + resp_rows, KVH, HD)
    scores = product("bqkgd,bckd->bkgqc", shaped, all_keys) * scaling
    query_pos = jnp.arange(resp_rows, dtype=jnp.int32)[:, None]
    key_pos = jnp.arange(prompt_len + resp_rows, dtype=jnp.int32)[None, :] - prompt_len
    allowed = (key_pos < 0)[None] | (key_pos <= query_pos)[None] & (
        key_pos[None] < resp_lengths[:, None, None]
    )
    scores = jnp.where(allowed[:, None, None], scores, -1e30)
    highest = jnp.max(scores, axis=-1, keepdims=True)
    expo_terms = jnp.exp(scores - highest)
    softmax = expo_terms / jnp.sum(expo_terms, axis=-1, keepdims=True)
    live_rows = (jnp.arange(resp_rows, dtype=jnp.int32)[None, :] < resp_lengths[:, None]).astype(
        resp_out_grad.dtype
    )
    masked = (
        resp_out_grad.reshape(batch_size, resp_rows, KVH, per_group, HD)
        * live_rows[:, :, None, None, None]
    )
    rounded = softmax.astype(jnp.bfloat16)
    attn_out = product("bkgqc,bckd->bqkgd", rounded, all_values)
    delta = jnp.einsum("bqkgd,bqkgd->bkgq", masked.astype(jnp.float32), attn_out)
    prob_grad = product("bqkgd,bckd->bkgqc", masked, all_values)
    score_grad = (scaling * softmax * (prob_grad - delta[..., None])).astype(jnp.bfloat16)
    query_part = product("bkgqc,bckd->bqkgd", score_grad, all_keys).reshape(
        batch_size, resp_rows, QH * HD
    )
    key_grad = product("bkgqc,bqkgd->bckd", score_grad, shaped).reshape(
        batch_size, prompt_len + resp_rows, kv_width
    )
    value_grad = product("bkgqc,bqkgd->bckd", rounded, masked).reshape(
        batch_size, prompt_len + resp_rows, kv_width
    )
    both_grads = jnp.concatenate([key_grad, value_grad], axis=-1)
    return (query_part, both_grads[:, prompt_len:], both_grads[:, :prompt_len])


def add_terms(earlier, later):
    return earlier + later


def body(
    queries,
    out_grad,
    resp_kv,
    prompt_kv,
    prompt_hidden,
    norm_gain,
    kv_weight,
    upper_grad,
    group_list,
    lengths,
    owner_map,
):
    resp_count = lengths.shape[0]
    resp_rows = queries.shape[1] // resp_count
    full_width = 2 * KVH * HD
    devices = lax.axis_size("resp")
    my_index = lax.axis_index("resp")
    prompt_count = owner_map.shape[0]
    query_part, own_part, prompt_part = response_backward(
        queries[0].reshape(resp_count, resp_rows, QH * HD),
        out_grad[0].reshape(resp_count, resp_rows, QH * HD),
        resp_kv[0].reshape(resp_count, resp_rows, full_width),
        prompt_kv[0],
        lengths,
    )
    block_rows = prompt_part.shape[1] // devices
    prompt_ids = jnp.arange(prompt_count, dtype=jnp.int32)
    my_groups = lax.dynamic_slice_in_dim(group_list, my_index * resp_count, resp_count)
    matches = my_groups[:, None] == prompt_ids[None, :]
    holders = jnp.sum(jnp.where(matches[:, :, None], owner_map[None, :, :], 0), axis=1)
    device_ids = jnp.arange(devices, dtype=jnp.int32)
    inverse = jnp.sum(
        jnp.where(holders[:, :, None] == device_ids[None, None, :], device_ids[None, :, None], 0),
        axis=1,
    )
    blocks = prompt_part.astype(jnp.bfloat16).reshape(resp_count, devices, block_rows, full_width)
    slot_ids = jnp.arange(resp_count, dtype=jnp.int32)
    outgoing = blocks[slot_ids[None, :], inverse.T]
    incoming = lax.all_to_all(outgoing, "resp", split_axis=0, concat_axis=0, tiled=True)
    select = (group_list[:, None] == prompt_ids[None, :]).astype(jnp.bfloat16)
    arrived = incoming.reshape(devices * resp_count, block_rows * full_width)
    summed = lax.dot_general(
        select, arrived, (((0,), (0,)), ((), ())), preferred_element_type=jnp.float32
    )
    page_grad = summed.astype(jnp.bfloat16)
    weight_rows = kv_weight[0]
    normed_grad = lax.dot_general(
        page_grad,
        lax.all_gather(weight_rows, "resp", axis=0, tiled=True),
        (((1,), (1,)), ((), ())),
        preferred_element_type=jnp.float32,
    )
    hidden = prompt_hidden[0].astype(jnp.float32)
    gain = norm_gain[0].astype(jnp.float32)
    inverse_rms = lax.rsqrt(jnp.mean(hidden * hidden, axis=-1, keepdims=True) + 1e-06)
    scaled = gain[None, :] * normed_grad
    term = inverse_rms * scaled - hidden * inverse_rms**3 * jnp.mean(
        hidden * scaled, axis=-1, keepdims=True
    )
    above = entering(term, "section", add_terms, jnp.zeros_like(term))
    total = above + term
    prompt_out = (upper_grad.astype(jnp.float32) + total).astype(jnp.bfloat16)
    query_out = query_part.astype(jnp.bfloat16).reshape(resp_count * resp_rows, QH * HD)
    own_out = own_part.astype(jnp.bfloat16).reshape(resp_count * resp_rows, full_width)
    return (query_out[None], own_out[None], prompt_out[None])


def solution(mesh):
    in_specs = (
        P("section", "resp", None),
        P("section", "resp", None),
        P("section", "resp", None),
        P("section", "resp", None, None),
        P("section", "resp", None),
        P("section", None),
        P("section", "resp", None),
        P("resp", None),
        P(),
        P("resp"),
        P(),
    )
    out_specs = (P("section", "resp", None), P("section", "resp", None), P("section", "resp", None))
    return jax.shard_map(body, mesh=mesh, in_specs=in_specs, out_specs=out_specs, check_vma=False)
```

profile of v0, /device:TPU:1, one launch (start us, length us, event | category | flops | bytes accessed | tf_op | source)
XLA Modules:
  0.0 171.7 jit_solution(6933962642008727432)
XLA Ops:
  7.2 0.7 all-gather.5.cloned.1.call-update
  7.9 1.4 copy.74
  9.4 1.0 fusion.41
  10.3 1.3 fusion.40
  12.1 1.5 copy.75
  13.7 0.7 fusion.17
  14.5 1.9 %fusion.42 = (f32[4,4,8,32]{3,2,1,0:T(8,128)S(1)}, f32[4,4,8,32,160]{4,3,2,1,0:T(8,128)S(1)}) fusion(f32[4,4,160,32,8]{2,3,4,1,0:T(8,128)S(1)} %fusion.17, pred[4,32,160]{2,1,0:T(8,128)(4,1)S(1)} %and_or_fusion), kind=kOutput, calls=%fused_computation.76 | output fusion | flops 3932319 | bytes 5279744 | tf_op jit(solution)/shard_map/sub | solution.py:49
  16.4 0.7 fusion.14
  17.2 0.9 convolution_bitcast_fusion
  18.1 0.9 fusion.10
  19.0 1.7 fusion.7
  20.7 0.8 convolution_bitcast_fusion.1
  22.2 0.8 dynamic_slice.13
  23.7 7.9 %gather_fusion = bf16[512,1024]{1,0:T(8,128)(2,1)} fusion(bf16[4,128,1024]{2,1,0:T(8,128)(2,1)S(1)} %fusion.9, s32[512]{0:T(512)S(1)} %reshape.185), kind=kCustom, calls=%fused_computation | custom fusion | bytes 2101248 | tf_op jit(solution)/shard_map/gather | solution.py:118
  31.6 2.3 %reshape.184 = bf16[128,4,1,1024]{3,1,0,2:T(4,128)(2,1)} reshape(bf16[512,1024]{1,0:T(8,128)(2,1)} %gather_fusion) | data formatting | bytes 2097152 | tf_op jit(solution)/shard_map/gather | solution.py:118
  33.9 18.9 %all-to-all-start = ((bf16[128,4,1,1024]{3,1,2,0:T(4,128)(2,1)}), bf16[128,4,1,1024]{3,1,2,0:T(4,128)(2,1)}, u32[]{:S(2)}, u32[]{:S(2)}) async-start(bf16[128,4,1,1024]{3,1,2,0:T(4,128)(2,1)} %bitcast.24), calls=%async_computation | async-start | bytes 2097152 | tf_op jit(solution)/shard_map/all_to_all | solution.py:119
  53.1 30.2 %all-to-all-done = bf16[128,4,1,1024]{3,1,2,0:T(4,128)(2,1)} async-done(((bf16[128,4,1,1024]{3,1,2,0:T(4,128)(2,1)}), bf16[128,4,1,1024]{3,1,2,0:T(4,128)(2,1)}, u32[]{:S(2)}, u32[]{:S(2)}) %all-to-all-start) | async-done | bytes 1048608 | tf_op jit(solution)/shard_map/all_to_all | solution.py:119
  83.3 1.3 reshape.179
  84.7 39.3 %all-gather.5.cloned.1.call-done = bf16[1,4096,1024]{2,1,0:T(8,128)(2,1)} async-done(((bf16[1,32,1024]{2,1,0:T(8,128)(2,1)}), bf16[1,4096,1024]{2,1,0:T(8,128)(2,1)}) %all-gather.5.cloned.1.call-update) | async-done | bytes 8388624 | tf_op jit(solution)/shard_map/all_gather | solution.py:129
  124.0 7.0 %fusion.23 = (f32[32]{0:T(128)}, f32[32]{0:T(128)}, f32[32,4096]{1,0:T(8,128)S(1)}) fusion(bf16[1,32,4096]{2,1,0:T(8,128)(2,1)} %param.17, bf16[1,4096,1024]{2,1,0:T(8,128)(2,1)} %all-gather.5.cloned.1.call-done, bf16[512,1024]{1,0:T(8,128)(2,1)S(1)} %reshape.179, s32[512]{0:T(512)} %param.21, f32[4096]{0:T(1024)S(1)} %bitcast.119), kind=kOutput, calls=%fused_computation.41 | convolution fusion | flops 302825408 | bytes 10242304 | tf_op jit(solution)/shard_map/dot_general | solution.py:127
  132.2 1.8 %fusion.29 = bf16[32,4096]{1,0:T(8,128)(2,1)} fusion(f32[32,4096]{1,0:T(8,128)S(1)} %get-tuple-element.147, bf16[1,32,4096]{2,1,0:T(8,128)(2,1)} %param.17, f32[32]{0:T(128)S(1)} %broadcast_multiply_fusion, f32[32]{0:T(128)S(1)} %get-tuple-element.144, f32[32]{0:T(128)S(1)} %get-tuple-element.143), kind=kLoop, calls=%fused_computation.49 | loop fusion | flops 786432 | bytes 1048960 | tf_op jit(solution)/shard_map/convert_element_type | solution.py:13
  134.1 2.3 %fusion.15 = bf16[4,32,4,8,128]{4,1,3,2,0:T(8,128)(2,1)S(1)} fusion(bf16[4,4,8,32,160]{4,3,2,1,0:T(8,128)(2,1)} %copy-done.1, bf16[4,160,4,128,1]{3,2,1,0,4:T(4,128)(2,1)S(1)} %bitcast.105), kind=kOutput, calls=%fused_computation.24 | convolution fusion | flops 168296448 | bytes 3014656 | tf_op jit(solution)/shard_map/bkgqc,bckd->bqkgd/dot_general | solution.py:26
  136.4 1.4 copy.45
  137.8 2.3 %convert_element_type.71 = bf16[1,128,4096]{2,1,0:T(8,128)(2,1)} reshape(bf16[4,32,4,8,128]{4,3,2,1,0:T(8,128)(2,1)} %copy.45) | data formatting | bytes 2097152 | tf_op jit(solution)/shard_map/convert_element_type | solution.py:143
  140.1 0.7 maximum_convert_fusion
  140.9 18.0 %all-gather.7.cloned.1.call-done = bf16[128,4096]{1,0:T(8,128)(2,1)} async-done(((bf16[32,4096]{1,0:T(8,128)(2,1)}), bf16[128,4096]{1,0:T(8,128)(2,1)}) %all-gather.7.cloned.1.call-update) | async-done | bytes 1048592 | tf_op jit(solution)/shard_map/all_gather | solution.py:13
  158.9 5.0 %while.16 = (s32[]{:T(128)}, f32[32,4096]{1,0:T(8,128)S(1)}, s32[]{:T(128)}, bf16[4,32,4096]{2,1,0:T(8,128)(2,1)}, s32[]{:T(128)}, /*index=5*/s32[]{:T(128)}, s32[]{:T(128)}, s32[]{:T(128)}) while((s32[]{:T(128)}, f32[32,4096]{1,0:T(8,128)S(1)}, s32[]{:T(128)}, bf16[4,32,4096]{2,1,0:T(8,128)(2,1)}, s32[]{:T(128)}, ...), condition=%wide.region_7.8_spmd.clone, body=%wide.region_6.7_spmd.clone.sunk | while | flops 524296 | bytes 1310883 | solution.py:22
  158.9 1.2 add_select_fusion.2
  160.2 1.2 add_select_fusion.2
  161.4 1.2 add_select_fusion.2
  162.7 1.2 add_select_fusion.2
  163.9 0.9 fusion.30
  (37 shorter events, 3.7 us)
Async XLA Ops:
  7.2 116.8 %all-gather.5.cloned.1.call-start = ((), (), s32[]{:S(2)}) async-start(), calls=%async_computation.1 | async-start | bytes 8454144 | tf_op jit(solution)/shard_map/all_gather | solution.py:129
  11.6 1.9 %copy-start.5 = (s32[4]{0:T(128)S(1)}, s32[4]{0:T(128)}, u32[]{:S(2)}) copy-start(s32[4]{0:T(128)} %param.22) | copy-start | bytes 52
  20.7 1.4 copy-start.1
  20.7 2.3 %copy-start.3 = (s32[32,128]{1,0:T(8,128)S(1)}, s32[32,128]{1,0:T(8,128)}, u32[]{:S(2)}) copy-start(s32[32,128]{1,0:T(8,128)} %param.23) | copy-start | bytes 49156
  31.6 21.4 %copy-start.4 = (bf16[1,4096]{1,0:T(2,128)(2,1)S(1)}, bf16[1,4096]{1,0:T(2,128)(2,1)}, u32[]{:S(2)}) copy-start(bf16[1,4096]{1,0:T(2,128)(2,1)} %param.18) | copy-start | bytes 24580
  33.9 49.4 %all-to-all-start = ((bf16[128,4,1,1024]{3,1,2,0:T(4,128)(2,1)}), bf16[128,4,1,1024]{3,1,2,0:T(4,128)(2,1)}, u32[]{:S(2)}, u32[]{:S(2)}) async-start(bf16[128,4,1,1024]{3,1,2,0:T(4,128)(2,1)} %bitcast.24), calls=%async_computation | async-start | bytes 2097152 | tf_op jit(solution)/shard_map/all_to_all | solution.py:119
  52.8 106.1 %all-gather.7.cloned.1.call-start = ((), (), s32[]{:S(2)}) async-start(), calls=%async_computation.2 | async-start | bytes 1310720 | tf_op jit(solution)/shard_map/all_gather | solution.py:13
  140.1 23.8 %copy-start = (bf16[1,32,4096]{2,1,0:T(8,128)(2,1)S(1)}, bf16[1,32,4096]{2,1,0:T(8,128)(2,1)}, u32[]{:S(2)}) copy-start(bf16[1,32,4096]{2,1,0:T(8,128)(2,1)} %param.17) | copy-start | bytes 786436
  140.1 23.8 %copy-start.2 = (bf16[32,4096]{1,0:T(8,128)(2,1)S(1)}, bf16[32,4096]{1,0:T(8,128)(2,1)}, u32[]{:S(2)}) copy-start(bf16[32,4096]{1,0:T(8,128)(2,1)} %param.20) | copy-start | bytes 786436
Sparse Core Ops, SparseCore 0:
  11.1 112.7 all-gather.4
  134.2 24.6 all-gather.6
where the time goes:
time: 172 us
  waiting for transfers between devices  88.3 us (51%)
  local copies, waits for them, and re-layouts  22.5 us (13%)
  starting transfers between devices  19.1 us (11%)
  between operations  14.3 us (8%)
  matrix products  14.2 us (8%)
  other arithmetic  13.1 us (8%)
    all_gather x1, waiting for transfers between devices, body(): lax.all_gather(weight_rows, 'resp', axis=0, tiled=True)  39.3 us
    all_to_all x1, waiting for transfers between devices, body(): lax.all_to_all(outgoing, 'resp', split_axis=0, concat_axis=0, tiled=True)  30.2 us
    all_to_all x1, starting transfers between devices, body(): lax.all_to_all(outgoing, 'resp', split_axis=0, concat_axis=0, tiled=True)  18.9 us
    all_gather x1, waiting for transfers between devices, entering(): everything = lax.all_gather(shard.astype(jnp.bfloat16), axis)  18 us
    gather x2, local copies, waits for them, and re-layouts, body(): outgoing = blocks[slot_ids[None, :], inverse.T]  10.2 us
    dot_general x6, matrix products, product(): jnp.einsum(pattern, first_op, second_op, preferred_element_type=jnp.float32)  7.29 us
    dot_general x1, matrix products, body(): lax.dot_general(page_grad, lax.all_gather(weight_rows, 'resp', axis=0, ti...  6.96 us
    select_n x4, other arithmetic, turn(): return jnp.where(reached, new, before)  4.92 us
  transfers between devices with their start and end apart: 3, of which 3 were waited for; matrix products, arithmetic and copies ran while one was open for 19% of the time, Pallas kernels for 0%

commit v1 on v0

v1 whole, which is shorter than its diff:
```python
import functools

import jax
import jax.numpy as jnp
from jax import lax
from jax.experimental import pallas as pl
from jax.experimental.pallas import tpu as pltpu
from jax.sharding import PartitionSpec as P

QH = 32
KVH = 4
HD = 128
PER = QH // KVH
RESP_DEV = 4
WIDE = 2 * KVH * HD
LOG2E = 1.4426950408889634
SMALL = pltpu.CompilerParams(vmem_limit_bytes=16 * 1024 * 1024)
F32 = jnp.float32
BF16 = jnp.bfloat16


def dot(a, b, dims):
    return lax.dot_general(a, b, (dims, ((), ())), preferred_element_type=F32)


RESP_AXES = ("z", "y", "core")
LANES = 128


def resp_index():
    index = 0
    for axis in RESP_AXES:
        index = index * lax.axis_size(axis) + lax.axis_index(axis)
    return index


def attention_kernel(groups, lengths, q_ref, do_ref, own_ref, cache_ref, owner_ref, dq_ref, down_ref, send_ref, mixed_ref):
    b = pl.program_id(0)
    count = RESP_DEV
    length = lengths[b]
    rows = q_ref.shape[0]
    plen = cache_ref.shape[0]
    scaling = HD ** (-0.5)
    lanes = PER * rows
    key_pos = lax.broadcasted_iota(jnp.int32, (rows, lanes), 0)
    query_pos = lax.broadcasted_iota(jnp.int32, (rows, lanes), 1) % rows
    allowed = (key_pos <= query_pos) & (key_pos < length)
    live = (lax.broadcasted_iota(jnp.int32, (rows, HD), 0) < length).astype(BF16)
    group = groups[resp_index() * count + b]
    owners = owner_ref[pl.ds(group, 1), :]
    devices = owner_ref.shape[1]
    place = (lax.broadcasted_iota(jnp.int32, (devices, devices), 0) == owners).astype(BF16)
    own_kv = own_ref[...]
    cached = cache_ref[...]
    heads = [slice(h * HD, (h + 1) * HD) for h in range(QH)]
    key_cols = heads[:KVH]
    value_cols = heads[KVH : 2 * KVH]
    each = range(KVH)
    q = [jnp.concatenate([q_ref[:, h] for h in heads[k * PER : (k + 1) * PER]], axis=0) for k in each]
    keys = [jnp.concatenate([cached[:, at], own_kv[:, at]], axis=0) for at in key_cols]
    scores = [dot(keys[k], q[k], ((1,), (1,))) for k in each]
    do = [jnp.concatenate([do_ref[:, h] * live for h in heads[k * PER : (k + 1) * PER]], axis=0) for k in each]
    values = [jnp.concatenate([cached[:, at], own_kv[:, at]], axis=0) for at in value_cols]
    prob_grad = [dot(values[k], do[k], ((1,), (1,))) for k in each]
    low, score_grad = [], []
    for k in each:
        masked = jnp.concatenate([scores[k][:plen], jnp.where(allowed, scores[k][plen:], -1e30)], axis=0)
        expo = jnp.exp2((masked - jnp.max(masked, axis=0, keepdims=True)) * (scaling * LOG2E))
        probs = expo * (1.0 / jnp.sum(expo, axis=0, keepdims=True))
        low.append(probs.astype(BF16))
        delta = jnp.sum(probs * prob_grad[k], axis=0, keepdims=True)
        score_grad.append((probs * ((prob_grad[k] - delta) * scaling)).astype(BF16))
    grads = []
    for k in each:
        grads.append((k, 1, value_cols[k], dot(low[k], do[k], ((1,), (0,)))))
        grads.append((k, 0, key_cols[k], dot(score_grad[k], q[k], ((1,), (0,)))))
    for k in each:
        dq = dot(score_grad[k], keys[k], ((0,), (0,)))
        for g, h in enumerate(heads[k * PER : (k + 1) * PER]):
            dq_ref[:, h] = dq[g * rows : (g + 1) * rows].astype(BF16)
    for k, half, at, grad in grads:
        down_ref[:, at] = grad[plen:].astype(BF16)
        part = dot(place, grad[:plen].astype(BF16), ((1,), (0,)))
        mixed_ref[k, pl.ds(2 * b + half, devices, stride=2 * count), :] = part

    @pl.when(b == count - 1)
    def _():
        for k in range(KVH):
            send_ref[:, k * HD : (k + 1) * HD] = mixed_ref[k].astype(BF16)


def attention(queries, out_grad, resp_kv, prompt_kv, group_list, lengths, owner_map):
    count, plen, _ = prompt_kv.shape
    total = queries.shape[0]
    rows = total // count
    width = queries.shape[1]
    by_resp = lambda w: pl.BlockSpec((rows, w), lambda b, *_: (b, 0))
    return pl.pallas_call(
        attention_kernel,
        grid_spec=pltpu.PrefetchScalarGridSpec(
            num_scalar_prefetch=2,
            grid=(count,),
            in_specs=[
                by_resp(width),
                by_resp(width),
                by_resp(WIDE),
                pl.BlockSpec((None, plen, WIDE), lambda b, *_: (b, 0, 0)),
                pl.BlockSpec(owner_map.shape, lambda b, *_: (0, 0)),
            ],
            out_specs=[
                by_resp(width),
                by_resp(WIDE),
                pl.BlockSpec((2 * count * plen, WIDE // 2), lambda b, *_: (0, 0)),
            ],
            scratch_shapes=[pltpu.VMEM((KVH, 2 * count * plen, HD), F32)],
        ),
        out_shape=[
            jax.ShapeDtypeStruct((total, width), BF16),
            jax.ShapeDtypeStruct((total, WIDE), BF16),
            jax.ShapeDtypeStruct((2 * count * plen, WIDE // 2), BF16),
        ],
        cost_estimate=pl.CostEstimate(flops=10**9, bytes_accessed=6 * 10**6, transcendentals=700000),
        name="attention_backward",
    )(group_list, lengths, queries, out_grad, resp_kv, prompt_kv, owner_map)


def page_kernel(groups_ref, arrived_ref, page_ref):
    copies, prompts, _ = page_ref.shape
    rows, half = arrived_ref.shape
    ids = lax.broadcasted_iota(jnp.int32, (2 * prompts, rows), 0)
    odd = lax.broadcasted_iota(jnp.int32, (2 * prompts, rows), 1) % 2
    select = (ids == groups_ref[...] + prompts * odd).astype(BF16)
    page = dot(select, arrived_ref[...], ((1,), (0,))).astype(BF16)
    for copy in range(copies):
        page_ref[copy, :, :half] = page[:prompts]
        page_ref[copy, :, half:] = page[prompts:]


def natural_order(transposed):
    span = 2 * LANES
    held = lax.broadcasted_iota(jnp.int32, (span, span), 1 if transposed else 0)
    model = lax.broadcasted_iota(jnp.int32, (span, span), 0 if transposed else 1)
    rows = 32
    core, rest = held // LANES, held % LANES
    return (model == rest // rows * (2 * rows) + core * rows + rest % rows).astype(BF16)


def collect_kernel(*refs):
    out_ref, pieces = refs[-1], refs[:-1]
    rows = len(pieces)
    for k, ref in enumerate(pieces):
        out_ref[lax.rem(lax.axis_index("y") + rows - k, rows)] = ref[...]


def project_kernel(pages_ref, own_ref, other_ref, gain_ref, out_ref, gain_rows):
    gain_rows[...] = dot(gain_ref[...], natural_order(True), ((1,), (0,)))
    pairs = out_ref.shape[1] // (2 * LANES)
    gain = [gain_rows[pl.ds(lax.axis_index("z") * pairs + pair, 1), :] for pair in range(pairs)]
    first = lax.axis_index("core") == 0
    own = dot(pages_ref[...], own_ref[...], ((1,), (1,)))
    other = dot(pages_ref[...], other_ref[...], ((1,), (1,)))
    for core in range(2):
        normed = jnp.where(first, own, other) if core == 0 else jnp.where(first, other, own)
        for pair in range(pairs):
            at = slice(pair * LANES, (pair + 1) * LANES)
            start = (core * pairs + pair) * LANES
            scale = gain[pair][:, core * LANES : (core + 1) * LANES]
            out_ref[:, start : start + LANES] = (normed[:, at] * scale).astype(BF16)


def term_kernel(scaled_ref, hidden_ref, *refs):
    got, (out_ref, term_ref, layers_ref) = refs[:-3], refs[-3:]
    blocks, rows, cols = scaled_ref.shape
    sections, step, width = layers_ref.shape
    here = lax.axis_index("section")
    layers_ref[here] = hidden_ref[here].astype(F32)
    for k, ref in enumerate(got, 1):
        layers_ref[lax.rem(here + sections - k, sections)] = ref[...].astype(F32)
    span = 2 * LANES
    pairs = cols // span
    mixed = []
    for block in range(blocks):
        for pair in range(pairs):
            low, high = pair * LANES, (pairs + pair) * LANES
            mixed.append(
                jnp.concatenate([scaled_ref[block, :, low : low + LANES], scaled_ref[block, :, high : high + LANES]], axis=1)
            )
    scaled = dot(jnp.concatenate(mixed, axis=0), natural_order(False), ((1,), (0,)))
    squares = jnp.zeros((rows, span), F32)
    cross = jnp.zeros((rows, span), F32)
    for n in range(len(mixed)):
        at = slice(n * span, (n + 1) * span)
        part = scaled[n * rows : (n + 1) * rows]
        term_ref[:, at] = part
        hidden = layers_ref[:, :, at].reshape(rows, span)
        squares += hidden * hidden
        cross += hidden * part
    inverse = lax.rsqrt(jnp.sum(squares, axis=-1, keepdims=True) / width + 1e-06)
    back = inverse**3 * (jnp.sum(cross, axis=-1, keepdims=True) / width)
    chunk = 4 * LANES
    for start in range(0, width, chunk):
        at = slice(start, start + chunk)
        term = inverse * term_ref[:, at] - layers_ref[:, :, at].reshape(rows, chunk) * back
        sums = [term[(sections - 1) * step :]]
        for s in reversed(range(sections - 1)):
            sums.insert(0, sums[0] + term[s * step : (s + 1) * step])
        out_ref[:, at] = jnp.concatenate(sums, axis=0).astype(BF16)


def finish(pages, weights, hidden, norm_gain, upper_grad):
    prompt_count, width = upper_grad.shape
    sections, quarter, _ = hidden[0].shape
    members = pages.shape[0]
    pages = lax.all_to_all(pages, "z", split_axis=0, concat_axis=0, tiled=True)
    scaled = pl.pallas_call(
        project_kernel,
        out_shape=jax.ShapeDtypeStruct((members * prompt_count, width // members), BF16),
        scratch_shapes=[pltpu.VMEM((width // (2 * LANES), 2 * LANES), F32)],
        compiler_params=SMALL,
        cost_estimate=pl.CostEstimate(flops=3 * 10**8, bytes_accessed=2 * 10**6, transcendentals=0),
        name="projection",
    )(pages.reshape(-1, WIDE), *weights, norm_gain.reshape(-1, 2 * LANES))
    scaled = scaled.reshape(members * sections, quarter, -1)
    scaled = lax.all_to_all(scaled, ("z", "section"), split_axis=0, concat_axis=0, tiled=True)
    sums = pl.pallas_call(
        term_kernel,
        out_shape=jax.ShapeDtypeStruct((prompt_count, width), BF16),
        scratch_shapes=[pltpu.VMEM((prompt_count, width), F32), pltpu.VMEM((sections, quarter, width), F32)],
        compiler_params=SMALL,
        cost_estimate=pl.CostEstimate(flops=10**8, bytes_accessed=10**6, transcendentals=0),
        name="norm_terms",
    )(scaled.reshape(members, prompt_count, -1), *hidden)
    sums = lax.all_to_all(sums.reshape(sections, quarter, width), "section", split_axis=0, concat_axis=0, tiled=True)
    return (upper_grad.astype(F32) + sums.reshape(prompt_count, width).astype(F32)).astype(BF16)


def turn(piece, axis, k):
    size = lax.axis_size(axis)
    return lax.ppermute(piece, axis, [(i, (i + k) % size) for i in range(size)])


def shift(rows, axis):
    size, here = rows.shape[0], lax.axis_index(axis)
    return [turn(lax.dynamic_index_in_dim(rows, lax.rem(here + k, size), keepdims=False), axis, k) for k in range(1, size)]


def body(queries, out_grad, resp_kv, prompt_kv, prompt_hidden, norm_gain, kv_weight, upper_grad, group_list, lengths, owner_map):
    prompt_count, devices = owner_map.shape
    sections = lax.axis_size("section")
    width = prompt_hidden.shape[-1]
    query_out, own_out, outgoing = attention(
        queries[0], out_grad[0], resp_kv[0], prompt_kv[0], group_list, lengths, owner_map
    )
    outgoing, weight = lax.optimization_barrier((outgoing, kv_weight[0]))
    outgoing = outgoing.reshape(devices, -1, WIDE // 2)
    incoming = lax.all_to_all(outgoing, RESP_AXES, split_axis=0, concat_axis=0, tiled=True)
    weights = [weight] + [turn(weight, "y", k) for k in range(1, lax.axis_size("y"))]
    weights = pl.pallas_call(
        collect_kernel,
        out_shape=jax.ShapeDtypeStruct((len(weights),) + weight.shape, BF16),
        compiler_params=SMALL,
        cost_estimate=pl.CostEstimate(flops=0, bytes_accessed=10**6, transcendentals=0),
        name="weight_rows",
    )(*weights)
    hidden = prompt_hidden[0].reshape(sections, prompt_count // sections, width)
    incoming, hidden, weights = lax.optimization_barrier((incoming, hidden, weights))
    pages = pl.pallas_call(
        page_kernel,
        out_shape=jax.ShapeDtypeStruct((lax.axis_size("z"), prompt_count, WIDE), BF16),
        compiler_params=SMALL,
        cost_estimate=pl.CostEstimate(flops=10**8, bytes_accessed=10**6, transcendentals=0),
        name="page_sum",
    )(jnp.repeat(group_list, 2)[None, :], incoming.reshape(-1, WIDE // 2))
    weights = weights.reshape(-1, WIDE)
    weights = [weights, lax.ppermute(weights, "core", [(0, 1), (1, 0)])]
    hidden = [hidden] + shift(hidden, "section")
    prompt_out = finish(pages, weights, hidden, norm_gain, upper_grad)
    return (query_out[None], own_out[None], prompt_out[None])


def solution(mesh):
    wide = jax.sharding.Mesh(mesh.devices.reshape(8, 8, 2, mesh.shape["section"]), RESP_AXES + ("section",))
    in_specs = (
        P("section", RESP_AXES, None),
        P("section", RESP_AXES, None),
        P("section", RESP_AXES, None),
        P("section", RESP_AXES, None, None),
        P("section", RESP_AXES, None),
        P("section", None),
        P("section", RESP_AXES, None),
        P(RESP_AXES, None),
        P(),
        P(RESP_AXES),
        P(),
    )
    out_specs = (P("section", RESP_AXES, None),) * 3
    return jax.shard_map(body, mesh=wide, in_specs=in_specs, out_specs=out_specs, check_vma=False)
```

time: 172 us -> 121 us (0.70)
  the two profiles are of different devices: /device:TPU:1 before, /device:TPU:64 now
where the time goes in v1:
time: 121 us; the launch traced here: 120 us
  starting transfers between devices  70.6 us (58%)
  waiting for transfers between devices  26.2 us (22%)
  blocking collectives  10.6 us (9%)
  Pallas kernels  10.2 us (8%)
    ppermute x10, starting transfers between devices, turn(): return lax.ppermute(piece, axis, [(i, (i + k) % size) for i in range(size)])  40 us
    all_to_all x1, starting transfers between devices, body(): lax.all_to_all(outgoing, RESP_AXES, split_axis=0, concat_axis=0, tiled=True)  16.7 us
    ppermute x10, waiting for transfers between devices, turn(): return lax.ppermute(piece, axis, [(i, (i + k) % size) for i in range(size)])  13.1 us
    all_to_all x1, waiting for transfers between devices, finish(): pages = lax.all_to_all(pages, 'z', split_axis=0, concat_axis=0, tiled=True)  12 us
    all_to_all x1, blocking collectives, finish(): lax.all_to_all(sums.reshape(sections, quarter, width), 'section', split_a...  10.6 us
    pallas_call x1, Pallas kernels, attention(): pl.pallas_call(attention_kernel, grid_spec=pltpu.PrefetchScalarGridSpec(n...  7.39 us
    all_to_all x1, starting transfers between devices, finish(): lax.all_to_all(scaled, ('z', 'section'), split_axis=0, concat_axis=0, til...  6.05 us
    all_to_all x1, starting transfers between devices, finish(): pages = lax.all_to_all(pages, 'z', split_axis=0, concat_axis=0, tiled=True)  5.91 us
  transfers between devices with their start and end apart: 14, of which 5 were waited for; matrix products, arithmetic and copies ran while one was open for 0% of the time, Pallas kernels for 0%

profile of v1, /device:TPU:64, one launch (start us, length us, event | category | flops | bytes accessed | tf_op | source)
XLA Modules:
  0.0 120.4 jit_solution(18027487642321815577)
XLA Ops:
  0.6 7.4 %attention_backward.1 = (bf16[128,4096]{1,0:T(8,128)(2,1)}, bf16[128,1024]{1,0:T(8,128)(2,1)}, bf16[1024,512]{1,0:T(8,128)(2,1)}) custom-call(s32[512]{0:T(512)} %groups.1, s32[4]{0:T(128)} %lengths.1, bf16[128,4096]{1,0:T(8,128)(2,1)} %bitcast.43, bf16[128,4096]{1,0:T(8,128)(2,1)} %bitcast.44, bf16[128,1024]{1,0:T(8,128)(2,1)} %bitcast.46, ...), custom_call_target="tpu_custom_call" | custom-call | flops 1000000000 | bytes 6000000 | tf_op jit(solution)/shard_map/attention_backward/pallas_call | solution.py:98
  8.0 0.0 copy-start.1
  8.0 0.0 copy-start.4
  8.0 16.7 %all-to-all-start = ((bf16[128,8,512]{2,1,0:T(8,128)(2,1)}), bf16[128,8,512]{2,1,0:T(8,128)(2,1)S(1)}, u32[]{:S(2)}, u32[]{:S(2)}) async-start(bf16[128,8,512]{2,1,0:T(8,128)(2,1)} %bitcast.42), calls=%async_computation | async-start | bytes 2097152 | tf_op jit(solution)/shard_map/all_to_all | solution.py:256
  24.8 3.4 %collective-permute-start = (bf16[32,1024]{1,0:T(8,128)(2,1)S(1)}, bf16[32,1024]{1,0:T(8,128)(2,1)S(1)}, u32[]{:S(2)}, u32[]{:S(2)}) collective-permute-start(bf16[32,1024]{1,0:T(8,128)(2,1)S(1)} %bitcast.34), channel_id=1, source_target_pairs={{0,8},{8,16},{16,24},{24,32},{32,40},{40,48},{48,56},{56,0},{1,9},... | collective-permute-start | bytes 196616 | tf_op jit(solution)/shard_map/ppermute | solution.py:239
  28.2 4.3 %collective-permute-start.1 = (bf16[32,1024]{1,0:T(8,128)(2,1)S(1)}, bf16[32,1024]{1,0:T(8,128)(2,1)S(1)}, u32[]{:S(2)}, u32[]{:S(2)}) collective-permute-start(bf16[32,1024]{1,0:T(8,128)(2,1)S(1)} %bitcast.35), channel_id=1, source_target_pairs={{0,16},{8,24},{16,32},{24,40},{32,48},{40,56},{48,0},{56,8},{1,17}... | collective-permute-start | bytes 196616 | tf_op jit(solution)/shard_map/ppermute | solution.py:239
  32.5 4.6 %collective-permute-start.2 = (bf16[32,1024]{1,0:T(8,128)(2,1)S(1)}, bf16[32,1024]{1,0:T(8,128)(2,1)S(1)}, u32[]{:S(2)}, u32[]{:S(2)}) collective-permute-start(bf16[32,1024]{1,0:T(8,128)(2,1)S(1)} %bitcast.36), channel_id=1, source_target_pairs={{0,24},{8,32},{16,40},{24,48},{32,56},{40,0},{48,8},{56,16},{1,25}... | collective-permute-start | bytes 196616 | tf_op jit(solution)/shard_map/ppermute | solution.py:239
  37.1 4.2 %collective-permute-start.3 = (bf16[32,1024]{1,0:T(8,128)(2,1)S(1)}, bf16[32,1024]{1,0:T(8,128)(2,1)S(1)}, u32[]{:S(2)}, u32[]{:S(2)}) collective-permute-start(bf16[32,1024]{1,0:T(8,128)(2,1)S(1)} %bitcast.37), channel_id=1, source_target_pairs={{0,32},{8,40},{16,48},{24,56},{32,0},{40,8},{48,16},{56,24},{1,33}... | collective-permute-start | bytes 196616 | tf_op jit(solution)/shard_map/ppermute | solution.py:239
  41.3 4.7 %collective-permute-start.4 = (bf16[32,1024]{1,0:T(8,128)(2,1)S(1)}, bf16[32,1024]{1,0:T(8,128)(2,1)S(1)}, u32[]{:S(2)}, u32[]{:S(2)}) collective-permute-start(bf16[32,1024]{1,0:T(8,128)(2,1)S(1)} %bitcast.38), channel_id=1, source_target_pairs={{0,40},{8,48},{16,56},{24,0},{32,8},{40,16},{48,24},{56,32},{1,41}... | collective-permute-start | bytes 196616 | tf_op jit(solution)/shard_map/ppermute | solution.py:239
  46.0 6.3 %collective-permute-done.refs_1_ = bf16[32,1024]{1,0:T(8,128)(2,1)S(1)} collective-permute-done((bf16[32,1024]{1,0:T(8,128)(2,1)S(1)}, bf16[32,1024]{1,0:T(8,128)(2,1)S(1)}, u32[]{:S(2)}, u32[]{:S(2)}) %collective-permute-start) | collective-permute-done | bytes 65568 | tf_op jit(solution)/shard_map/ppermute | solution.py:239
  52.3 4.1 %collective-permute-start.5 = (bf16[32,1024]{1,0:T(8,128)(2,1)S(1)}, bf16[32,1024]{1,0:T(8,128)(2,1)S(1)}, u32[]{:S(2)}, u32[]{:S(2)}) collective-permute-start(bf16[32,1024]{1,0:T(8,128)(2,1)S(1)} %bitcast.39), channel_id=1, source_target_pairs={{0,48},{8,56},{16,0},{24,8},{32,16},{40,24},{48,32},{56,40},{1,49}... | collective-permute-start | bytes 196616 | tf_op jit(solution)/shard_map/ppermute | solution.py:239
  56.5 3.4 %collective-permute-start.6 = (bf16[32,1024]{1,0:T(8,128)(2,1)S(1)}, bf16[32,1024]{1,0:T(8,128)(2,1)S(1)}, u32[]{:S(2)}, u32[]{:S(2)}) collective-permute-start(bf16[32,1024]{1,0:T(8,128)(2,1)S(1)} %bitcast.40), channel_id=1, source_target_pairs={{0,56},{8,0},{16,8},{24,16},{32,24},{40,32},{48,40},{56,48},{1,57}... | collective-permute-start | bytes 196616 | tf_op jit(solution)/shard_map/ppermute | solution.py:239
  59.9 0.1 broadcast_in_dim.14
  60.0 0.2 broadcast_in_dim_reshape.3.groups_ref
  60.2 4.0 %collective-permute-done.3.refs_4_ = bf16[32,1024]{1,0:T(8,128)(2,1)S(1)} collective-permute-done((bf16[32,1024]{1,0:T(8,128)(2,1)S(1)}, bf16[32,1024]{1,0:T(8,128)(2,1)S(1)}, u32[]{:S(2)}, u32[]{:S(2)}) %collective-permute-start.3) | collective-permute-done | bytes 65568 | tf_op jit(solution)/shard_map/ppermute | solution.py:239
  64.2 0.1 weight_rows.1
  64.3 1.1 page_sum.1
  65.4 5.9 %all-to-all-start.1 = ((bf16[8,32,1024]{2,1,0:T(8,128)(2,1)}), bf16[8,32,1024]{2,1,0:T(8,128)(2,1)S(1)}, u32[]{:S(2)}, u32[]{:S(2)}) async-start(bf16[8,32,1024]{2,1,0:T(8,128)(2,1)} %page_sum.1), calls=%async_computation.1 | async-start | bytes 1048576 | tf_op jit(solution)/shard_map/all_to_all | solution.py:214
  71.3 1.9 %collective-permute-start.7 = (bf16[256,1024]{1,0:T(8,128)(2,1)S(1)}, bf16[256,1024]{1,0:T(8,128)(2,1)S(1)}, u32[]{:S(2)}, u32[]{:S(2)}) collective-permute-start(bf16[256,1024]{1,0:T(8,128)(2,1)S(1)} %bitcast.27), channel_id=1, source_target_pairs={{0,4},{4,0},{1,5},{5,1},{2,6},{6,2},{3,7},{7,3},{8,12},{12,8},{9,1... | collective-permute-start | bytes 1572872 | tf_op jit(solution)/shard_map/ppermute | solution.py:275
  73.3 0.7 copy-done.3
  74.0 0.1 reduce
  74.1 1.1 collective-permute-done.7.other_ref
  75.1 12.0 %all-to-all-done.1 = bf16[8,32,1024]{2,1,0:T(8,128)(2,1)S(1)} async-done(((bf16[8,32,1024]{2,1,0:T(8,128)(2,1)}), bf16[8,32,1024]{2,1,0:T(8,128)(2,1)S(1)}, u32[]{:S(2)}, u32[]{:S(2)}) %all-to-all-start.1) | async-done | bytes 524320 | tf_op jit(solution)/shard_map/all_to_all | solution.py:214
  87.2 1.2 projection.1
  88.4 6.1 %all-to-all-start.2 = ((bf16[32,8,512]{2,1,0:T(8,128)(2,1)}), bf16[32,8,512]{2,1,0:T(8,128)(2,1)S(1)}, u32[]{:S(2)}, u32[]{:S(2)}) async-start(bf16[32,8,512]{2,1,0:T(8,128)(2,1)} %bitcast.12), calls=%async_computation.2 | async-start | bytes 524288 | tf_op jit(solution)/shard_map/all_to_all | solution.py:224
  94.5 3.4 %collective-permute-start.8 = (bf16[8,4096]{1,0:T(8,128)(2,1)S(1)}, bf16[8,4096]{1,0:T(8,128)(2,1)S(1)}, u32[]{:S(2)}, u32[]{:S(2)}) collective-permute-start(bf16[8,4096]{1,0:T(8,128)(2,1)S(1)} %get-tuple-element.21), channel_id=1, source_target_pairs={{0,1},{1,2},{2,3},{3,0},{4,5},{5,6},{6,7},{7,4},{8,9},{9,10},{10,1... | collective-permute-start | bytes 196616 | tf_op jit(solution)/shard_map/ppermute | solution.py:239
  97.8 4.6 %collective-permute-start.9 = (bf16[8,4096]{1,0:T(8,128)(2,1)S(1)}, bf16[8,4096]{1,0:T(8,128)(2,1)S(1)}, u32[]{:S(2)}, u32[]{:S(2)}) collective-permute-start(bf16[8,4096]{1,0:T(8,128)(2,1)S(1)} %get-tuple-element.20), channel_id=1, source_target_pairs={{0,2},{1,3},{2,0},{3,1},{4,6},{5,7},{6,4},{7,5},{8,10},{9,11},{10,... | collective-permute-start | bytes 196616 | tf_op jit(solution)/shard_map/ppermute | solution.py:239
  102.4 3.4 %collective-permute-start.10 = (bf16[8,4096]{1,0:T(8,128)(2,1)S(1)}, bf16[8,4096]{1,0:T(8,128)(2,1)S(1)}, u32[]{:S(2)}, u32[]{:S(2)}) collective-permute-start(bf16[8,4096]{1,0:T(8,128)(2,1)S(1)} %get-tuple-element.19), channel_id=1, source_target_pairs={{0,3},{1,0},{2,1},{3,2},{4,7},{5,4},{6,5},{7,6},{8,11},{9,8},{10,9... | collective-permute-start | bytes 196616 | tf_op jit(solution)/shard_map/ppermute | solution.py:239
  105.8 2.8 %collective-permute-done.10.refs_2_ = bf16[8,4096]{1,0:T(8,128)(2,1)S(1)} collective-permute-done((bf16[8,4096]{1,0:T(8,128)(2,1)S(1)}, bf16[8,4096]{1,0:T(8,128)(2,1)S(1)}, u32[]{:S(2)}, u32[]{:S(2)}) %collective-permute-start.10) | collective-permute-done | bytes 65568 | tf_op jit(solution)/shard_map/ppermute | solution.py:239
  108.6 0.4 norm_terms.1
  109.0 10.6 %all_to_all.20 = bf16[4,8,4096]{2,1,0:T(8,128)(2,1)S(1)} all-to-all(bf16[4,8,4096]{2,1,0:T(8,128)(2,1)S(1)} %bitcast.31), channel_id=1, replica_groups=mesh['z'=8,'y'=8,'core'=2,'section'=4] {'section'}, dimensions={0} | all-to-all | bytes 524288 | tf_op jit(solution)/shard_map/all_to_all | solution.py:233
  119.6 0.8 fusion.1
  (18 shorter events, 0.1 us)
Async XLA Ops:
  8.0 16.8 %copy-start.1 = (bf16[1,32,1024]{2,1,0:T(8,128)(2,1)S(1)}, bf16[1,32,1024]{2,1,0:T(8,128)(2,1)}, u32[]{:S(2)}) copy-start(bf16[1,32,1024]{2,1,0:T(8,128)(2,1)} %param.17) | copy-start | bytes 196612
  8.0 51.8 %copy-start.4 = (s32[512]{0:T(512)S(1)}, s32[512]{0:T(512)}, u32[]{:S(2)}) copy-start(s32[512]{0:T(512)} %groups.1) | copy-start | bytes 6148
  8.0 56.3 %all-to-all-start = ((bf16[128,8,512]{2,1,0:T(8,128)(2,1)}), bf16[128,8,512]{2,1,0:T(8,128)(2,1)S(1)}, u32[]{:S(2)}, u32[]{:S(2)}) async-start(bf16[128,8,512]{2,1,0:T(8,128)(2,1)} %bitcast.42), calls=%async_computation | async-start | bytes 2097152 | tf_op jit(solution)/shard_map/all_to_all | solution.py:256
  24.8 27.5 %collective-permute-start = (bf16[32,1024]{1,0:T(8,128)(2,1)S(1)}, bf16[32,1024]{1,0:T(8,128)(2,1)S(1)}, u32[]{:S(2)}, u32[]{:S(2)}) collective-permute-start(bf16[32,1024]{1,0:T(8,128)(2,1)S(1)} %bitcast.34), channel_id=1, source_target_pairs={{0,8},{8,16},{16,24},{24,32},{32,40},{40,48},{48,56},{56,0},{1,9},... | collective-permute-start | bytes 196616 | tf_op jit(solution)/shard_map/ppermute | solution.py:239
  28.2 28.3 %collective-permute-start.1 = (bf16[32,1024]{1,0:T(8,128)(2,1)S(1)}, bf16[32,1024]{1,0:T(8,128)(2,1)S(1)}, u32[]{:S(2)}, u32[]{:S(2)}) collective-permute-start(bf16[32,1024]{1,0:T(8,128)(2,1)S(1)} %bitcast.35), channel_id=1, source_target_pairs={{0,16},{8,24},{16,32},{24,40},{32,48},{40,56},{48,0},{56,8},{1,17}... | collective-permute-start | bytes 196616 | tf_op jit(solution)/shard_map/ppermute | solution.py:239
  32.5 27.7 %collective-permute-start.2 = (bf16[32,1024]{1,0:T(8,128)(2,1)S(1)}, bf16[32,1024]{1,0:T(8,128)(2,1)S(1)}, u32[]{:S(2)}, u32[]{:S(2)}) collective-permute-start(bf16[32,1024]{1,0:T(8,128)(2,1)S(1)} %bitcast.36), channel_id=1, source_target_pairs={{0,24},{8,32},{16,40},{24,48},{32,56},{40,0},{48,8},{56,16},{1,25}... | collective-permute-start | bytes 196616 | tf_op jit(solution)/shard_map/ppermute | solution.py:239
  37.1 27.1 %collective-permute-start.3 = (bf16[32,1024]{1,0:T(8,128)(2,1)S(1)}, bf16[32,1024]{1,0:T(8,128)(2,1)S(1)}, u32[]{:S(2)}, u32[]{:S(2)}) collective-permute-start(bf16[32,1024]{1,0:T(8,128)(2,1)S(1)} %bitcast.37), channel_id=1, source_target_pairs={{0,32},{8,40},{16,48},{24,56},{32,0},{40,8},{48,16},{56,24},{1,33}... | collective-permute-start | bytes 196616 | tf_op jit(solution)/shard_map/ppermute | solution.py:239
  41.3 22.9 %collective-permute-start.4 = (bf16[32,1024]{1,0:T(8,128)(2,1)S(1)}, bf16[32,1024]{1,0:T(8,128)(2,1)S(1)}, u32[]{:S(2)}, u32[]{:S(2)}) collective-permute-start(bf16[32,1024]{1,0:T(8,128)(2,1)S(1)} %bitcast.38), channel_id=1, source_target_pairs={{0,40},{8,48},{16,56},{24,0},{32,8},{40,16},{48,24},{56,32},{1,41}... | collective-permute-start | bytes 196616 | tf_op jit(solution)/shard_map/ppermute | solution.py:239
  52.3 11.9 %collective-permute-start.5 = (bf16[32,1024]{1,0:T(8,128)(2,1)S(1)}, bf16[32,1024]{1,0:T(8,128)(2,1)S(1)}, u32[]{:S(2)}, u32[]{:S(2)}) collective-permute-start(bf16[32,1024]{1,0:T(8,128)(2,1)S(1)} %bitcast.39), channel_id=1, source_target_pairs={{0,48},{8,56},{16,0},{24,8},{32,16},{40,24},{48,32},{56,40},{1,49}... | collective-permute-start | bytes 196616 | tf_op jit(solution)/shard_map/ppermute | solution.py:239
  56.5 7.8 %collective-permute-start.6 = (bf16[32,1024]{1,0:T(8,128)(2,1)S(1)}, bf16[32,1024]{1,0:T(8,128)(2,1)S(1)}, u32[]{:S(2)}, u32[]{:S(2)}) collective-permute-start(bf16[32,1024]{1,0:T(8,128)(2,1)S(1)} %bitcast.40), channel_id=1, source_target_pairs={{0,56},{8,0},{16,8},{24,16},{32,24},{40,32},{48,40},{56,48},{1,57}... | collective-permute-start | bytes 196616 | tf_op jit(solution)/shard_map/ppermute | solution.py:239
  65.4 21.7 %all-to-all-start.1 = ((bf16[8,32,1024]{2,1,0:T(8,128)(2,1)}), bf16[8,32,1024]{2,1,0:T(8,128)(2,1)S(1)}, u32[]{:S(2)}, u32[]{:S(2)}) async-start(bf16[8,32,1024]{2,1,0:T(8,128)(2,1)} %page_sum.1), calls=%async_computation.1 | async-start | bytes 1048576 | tf_op jit(solution)/shard_map/all_to_all | solution.py:214
  71.3 3.8 %collective-permute-start.7 = (bf16[256,1024]{1,0:T(8,128)(2,1)S(1)}, bf16[256,1024]{1,0:T(8,128)(2,1)S(1)}, u32[]{:S(2)}, u32[]{:S(2)}) collective-permute-start(bf16[256,1024]{1,0:T(8,128)(2,1)S(1)} %bitcast.27), channel_id=1, source_target_pairs={{0,4},{4,0},{1,5},{5,1},{2,6},{6,2},{3,7},{7,3},{8,12},{12,8},{9,1... | collective-permute-start | bytes 1572872 | tf_op jit(solution)/shard_map/ppermute | solution.py:275
  73.3 0.7 copy-start.3
  88.4 6.1 %copy-start = (bf16[1,32,4096]{2,1,0:T(8,128)(2,1)S(1)}, bf16[1,32,4096]{2,1,0:T(8,128)(2,1)}, u32[]{:S(2)}) copy-start(bf16[1,32,4096]{2,1,0:T(8,128)(2,1)} %param.15) | copy-start | bytes 786436
  88.4 20.2 %all-to-all-start.2 = ((bf16[32,8,512]{2,1,0:T(8,128)(2,1)}), bf16[32,8,512]{2,1,0:T(8,128)(2,1)S(1)}, u32[]{:S(2)}, u32[]{:S(2)}) async-start(bf16[32,8,512]{2,1,0:T(8,128)(2,1)} %bitcast.12), calls=%async_computation.2 | async-start | bytes 524288 | tf_op jit(solution)/shard_map/all_to_all | solution.py:224
  94.5 11.4 %collective-permute-start.8 = (bf16[8,4096]{1,0:T(8,128)(2,1)S(1)}, bf16[8,4096]{1,0:T(8,128)(2,1)S(1)}, u32[]{:S(2)}, u32[]{:S(2)}) collective-permute-start(bf16[8,4096]{1,0:T(8,128)(2,1)S(1)} %get-tuple-element.21), channel_id=1, source_target_pairs={{0,1},{1,2},{2,3},{3,0},{4,5},{5,6},{6,7},{7,4},{8,9},{9,10},{10,1... | collective-permute-start | bytes 196616 | tf_op jit(solution)/shard_map/ppermute | solution.py:239
  97.8 8.0 %collective-permute-start.9 = (bf16[8,4096]{1,0:T(8,128)(2,1)S(1)}, bf16[8,4096]{1,0:T(8,128)(2,1)S(1)}, u32[]{:S(2)}, u32[]{:S(2)}) collective-permute-start(bf16[8,4096]{1,0:T(8,128)(2,1)S(1)} %get-tuple-element.20), channel_id=1, source_target_pairs={{0,2},{1,3},{2,0},{3,1},{4,6},{5,7},{6,4},{7,5},{8,10},{9,11},{10,... | collective-permute-start | bytes 196616 | tf_op jit(solution)/shard_map/ppermute | solution.py:239
  102.4 6.2 %collective-permute-start.10 = (bf16[8,4096]{1,0:T(8,128)(2,1)S(1)}, bf16[8,4096]{1,0:T(8,128)(2,1)S(1)}, u32[]{:S(2)}, u32[]{:S(2)}) collective-permute-start(bf16[8,4096]{1,0:T(8,128)(2,1)S(1)} %get-tuple-element.19), channel_id=1, source_target_pairs={{0,3},{1,0},{2,1},{3,2},{4,7},{5,4},{6,5},{7,6},{8,11},{9,8},{10,9... | collective-permute-start | bytes 196616 | tf_op jit(solution)/shard_map/ppermute | solution.py:239
  109.0 10.6 %copy-start.2 = (bf16[32,4096]{1,0:T(8,128)(2,1)S(1)}, bf16[32,4096]{1,0:T(8,128)(2,1)}, u32[]{:S(2)}) copy-start(bf16[32,4096]{1,0:T(8,128)(2,1)} %param.18) | copy-start | bytes 786436

commit v2 on v1

--- a/solution.py
+++ b/solution.py
@@ -68,7 +68,7 @@
         expo = jnp.exp2((masked - jnp.max(masked, axis=0, keepdims=True)) * (scaling * LOG2E))
         probs = expo * (1.0 / jnp.sum(expo, axis=0, keepdims=True))
         low.append(probs.astype(BF16))
-        delta = jnp.sum(probs * prob_grad[k], axis=0, keepdims=True)
+        delta = jnp.sum(low[k].astype(F32) * prob_grad[k], axis=0, keepdims=True)
         score_grad.append((probs * ((prob_grad[k] - delta) * scaling)).astype(BF16))
     grads = []
     for k in each:
@@ -147,25 +147,44 @@
 
 def collect_kernel(*refs):
     out_ref, pieces = refs[-1], refs[:-1]
-    rows = len(pieces)
-    for k, ref in enumerate(pieces):
-        out_ref[lax.rem(lax.axis_index("y") + rows - k, rows)] = ref[...]
-
-
-def project_kernel(pages_ref, own_ref, other_ref, gain_ref, out_ref, gain_rows):
-    gain_rows[...] = dot(gain_ref[...], natural_order(True), ((1,), (0,)))
-    pairs = out_ref.shape[1] // (2 * LANES)
-    gain = [gain_rows[pl.ds(lax.axis_index("z") * pairs + pair, 1), :] for pair in range(pairs)]
-    first = lax.axis_index("core") == 0
-    own = dot(pages_ref[...], own_ref[...], ((1,), (1,)))
-    other = dot(pages_ref[...], other_ref[...], ((1,), (1,)))
-    for core in range(2):
-        normed = jnp.where(first, own, other) if core == 0 else jnp.where(first, other, own)
+    block, at = out_ref.shape[1], 0
+    for ref in pieces:
+        for start in range(0, ref.shape[0], block):
+            out_ref[at] = ref[start : start + block]
+            at += 1
+
+
+def project_kernel(pages_ref, own_ref, sibling_ref, near_ref, far_ref, gain_ref, out_ref, gain_rows, weight_ref):
+    span = 2 * LANES
+    gain = gain_ref[...].astype(F32)
+    gain = jnp.concatenate([gain[:, start : start + span] for start in range(0, gain.shape[1], span)], axis=0)
+    gain_rows[...] = dot(gain.astype(BF16), natural_order(True), ((1,), (0,)))
+    cores, rows, block, _ = weight_ref.shape
+    core, row = lax.axis_index("core"), lax.axis_index("y")
+    other = 1 - core
+    weight_ref[core, row] = own_ref[...]
+    weight_ref[other, row] = sibling_ref[...]
+    for j in range(1, rows // 2):
+        below = lax.rem(row + rows - j, rows)
+        above = lax.rem(row + j, rows)
+        near = jnp.where(core == 0, below, above)
+        far = jnp.where(core == 0, above, below)
+        weight_ref[core, near] = near_ref[2 * j - 2]
+        weight_ref[other, near] = near_ref[2 * j - 1]
+        weight_ref[other, far] = far_ref[2 * j - 2]
+        weight_ref[core, far] = far_ref[2 * j - 1]
+    middle = lax.rem(row + rows // 2, rows)
+    weight_ref[core, middle] = near_ref[rows - 2]
+    weight_ref[other, middle] = far_ref[rows - 2]
+    cols = rows * block
+    pairs = cols // LANES
+    scales = [gain_rows[pl.ds(lax.axis_index("z") * pairs + pair, 1), :] for pair in range(pairs)]
+    for c in range(cores):
+        normed = dot(pages_ref[...], weight_ref[c].reshape(cols, WIDE), ((1,), (1,)))
         for pair in range(pairs):
             at = slice(pair * LANES, (pair + 1) * LANES)
-            start = (core * pairs + pair) * LANES
-            scale = gain[pair][:, core * LANES : (core + 1) * LANES]
-            out_ref[:, start : start + LANES] = (normed[:, at] * scale).astype(BF16)
+            start = c * cols + pair * LANES
+            out_ref[:, start : start + LANES] = (normed[:, at] * scales[pair][:, c * LANES : (c + 1) * LANES]).astype(BF16)
 
 
 def term_kernel(scaled_ref, hidden_ref, *refs):
@@ -211,15 +230,17 @@
     prompt_count, width = upper_grad.shape
     sections, quarter, _ = hidden[0].shape
     members = pages.shape[0]
-    pages = lax.all_to_all(pages, "z", split_axis=0, concat_axis=0, tiled=True)
     scaled = pl.pallas_call(
         project_kernel,
         out_shape=jax.ShapeDtypeStruct((members * prompt_count, width // members), BF16),
-        scratch_shapes=[pltpu.VMEM((width // (2 * LANES), 2 * LANES), F32)],
+        scratch_shapes=[
+            pltpu.VMEM((width // (2 * LANES), 2 * LANES), F32),
+            pltpu.VMEM((2, lax.axis_size("y")) + weights[0].shape, BF16),
+        ],
         compiler_params=SMALL,
         cost_estimate=pl.CostEstimate(flops=3 * 10**8, bytes_accessed=2 * 10**6, transcendentals=0),
         name="projection",
-    )(pages.reshape(-1, WIDE), *weights, norm_gain.reshape(-1, 2 * LANES))
+    )(pages.reshape(-1, WIDE), *weights, norm_gain)
     scaled = scaled.reshape(members * sections, quarter, -1)
     scaled = lax.all_to_all(scaled, ("z", "section"), split_axis=0, concat_axis=0, tiled=True)
     sums = pl.pallas_call(
@@ -234,36 +255,55 @@
     return (upper_grad.astype(F32) + sums.reshape(prompt_count, width).astype(F32)).astype(BF16)
 
 
+def swap(piece):
+    return lax.ppermute(piece, "core", [(0, 1), (1, 0)])
+
+
 def turn(piece, axis, k):
     size = lax.axis_size(axis)
     return lax.ppermute(piece, axis, [(i, (i + k) % size) for i in range(size)])
 
 
-def shift(rows, axis):
-    size, here = rows.shape[0], lax.axis_index(axis)
-    return [turn(lax.dynamic_index_in_dim(rows, lax.rem(here + k, size), keepdims=False), axis, k) for k in range(1, size)]
+def part_ways(piece, j):
+    rows = lax.axis_size("y")
+    pairs = [(2 * y + c, (y + (j if c == 0 else rows - j)) % rows * 2 + c) for y in range(rows) for c in range(2)]
+    return lax.ppermute(piece, ("y", "core"), pairs)
+
+
+def hand_over(hidden, k):
+    size, here = hidden.shape[0], lax.axis_index("section")
+    return turn(lax.dynamic_index_in_dim(hidden, lax.rem(here + k, size), keepdims=False), "section", k)
+
+
+def gather_rows(weight, sibling):
+    rows = lax.axis_size("y")
+    both = jnp.concatenate([weight, sibling], axis=0)
+    pieces = [part_ways(both, j) for j in range(1, rows // 2)] + [turn(weight, "y", rows // 2)]
+    return pl.pallas_call(
+        collect_kernel,
+        out_shape=jax.ShapeDtypeStruct((rows - 1,) + weight.shape, BF16),
+        compiler_params=SMALL,
+        cost_estimate=pl.CostEstimate(flops=0, bytes_accessed=10**6, transcendentals=0),
+        name="weight_rows",
+    )(*pieces)
 
 
 def body(queries, out_grad, resp_kv, prompt_kv, prompt_hidden, norm_gain, kv_weight, upper_grad, group_list, lengths, owner_map):
     prompt_count, devices = owner_map.shape
     sections = lax.axis_size("section")
     width = prompt_hidden.shape[-1]
+    weight = kv_weight[0]
+    sibling = swap(weight)
+    hidden = prompt_hidden[0].reshape(sections, prompt_count // sections, width)
     query_out, own_out, outgoing = attention(
         queries[0], out_grad[0], resp_kv[0], prompt_kv[0], group_list, lengths, owner_map
     )
-    outgoing, weight = lax.optimization_barrier((outgoing, kv_weight[0]))
+    outgoing, weight, sibling, hidden = lax.optimization_barrier((outgoing, weight, sibling, hidden))
     outgoing = outgoing.reshape(devices, -1, WIDE // 2)
     incoming = lax.all_to_all(outgoing, RESP_AXES, split_axis=0, concat_axis=0, tiled=True)
-    weights = [weight] + [turn(weight, "y", k) for k in range(1, lax.axis_size("y"))]
-    weights = pl.pallas_call(
-        collect_kernel,
-        out_shape=jax.ShapeDtypeStruct((len(weights),) + weight.shape, BF16),
-        compiler_params=SMALL,
-        cost_estimate=pl.CostEstimate(flops=0, bytes_accessed=10**6, transcendentals=0),
-        name="weight_rows",
-    )(*weights)
-    hidden = prompt_hidden[0].reshape(sections, prompt_count // sections, width)
-    incoming, hidden, weights = lax.optimization_barrier((incoming, hidden, weights))
+    near = gather_rows(weight, sibling)
+    layers = [hidden, hand_over(hidden, 1)]
+    incoming, near, layers = lax.optimization_barrier((incoming, near, layers))
     pages = pl.pallas_call(
         page_kernel,
         out_shape=jax.ShapeDtypeStruct((lax.axis_size("z"), prompt_count, WIDE), BF16),
@@ -271,10 +311,11 @@
         cost_estimate=pl.CostEstimate(flops=10**8, bytes_accessed=10**6, transcendentals=0),
         name="page_sum",
     )(jnp.repeat(group_list, 2)[None, :], incoming.reshape(-1, WIDE // 2))
-    weights = weights.reshape(-1, WIDE)
-    weights = [weights, lax.ppermute(weights, "core", [(0, 1), (1, 0)])]
-    hidden = [hidden] + shift(hidden, "section")
-    prompt_out = finish(pages, weights, hidden, norm_gain, upper_grad)
+    pages = lax.all_to_all(pages, "z", split_axis=0, concat_axis=0, tiled=True)
+    far = swap(near)
+    layers += [hand_over(layers[0], k) for k in range(2, sections)]
+    pages, far, layers = lax.optimization_barrier((pages, far, layers))
+    prompt_out = finish(pages, [weight, sibling, near, far], layers, norm_gain, upper_grad)
     return (query_out[None], own_out[None], prompt_out[None])
 
 

time: 121 us -> 121 us (level)
  the two profiles are of different devices: /device:TPU:64 before, /device:TPU:2 now
where the time goes in v2:
time: 121 us; the launch traced here: 120 us
  starting transfers between devices  56 us (46%)
  blocking collectives  29.7 us (25%)
  waiting for transfers between devices  22.9 us (19%)
  Pallas kernels  9.5 us (8%)
    ppermute x4, waiting for transfers between devices, turn(): return lax.ppermute(piece, axis, [(i, (i + k) % size) for i in range(size)])  21.8 us
    all_to_all x1, blocking collectives, finish(): lax.all_to_all(scaled, ('z', 'section'), split_axis=0, concat_axis=0, til...  19.7 us
    all_to_all x1, starting transfers between devices, body(): lax.all_to_all(outgoing, RESP_AXES, split_axis=0, concat_axis=0, tiled=True)  18.1 us
    ppermute x4, starting transfers between devices, turn(): return lax.ppermute(piece, axis, [(i, (i + k) % size) for i in range(size)])  15 us
    ppermute x3, starting transfers between devices, part_ways(): return lax.ppermute(piece, ('y', 'core'), pairs)  12 us
    all_to_all x1, blocking collectives, finish(): lax.all_to_all(sums.reshape(sections, quarter, width), 'section', split_a...  9.96 us
    pallas_call x1, Pallas kernels, attention(): pl.pallas_call(attention_kernel, grid_spec=pltpu.PrefetchScalarGridSpec(n...  7.33 us
    all_to_all x1, starting transfers between devices, body(): pages = lax.all_to_all(pages, 'z', split_axis=0, concat_axis=0, tiled=True)  7.02 us
  transfers between devices with their start and end apart: 11, of which 4 were waited for; matrix products, arithmetic and copies ran while one was open for 0% of the time, Pallas kernels for 6%

profile of v2, /device:TPU:2, one launch (start us, length us, event | category | flops | bytes accessed | tf_op | source)
XLA Modules:
  0.0 120.1 jit_solution(15744311412527198099)
XLA Ops:
  0.6 1.9 %collective-permute-start = (bf16[32,1024]{1,0:T(8,128)(2,1)}, bf16[32,1024]{1,0:T(8,128)(2,1)S(1)}, u32[]{:S(2)}, u32[]{:S(2)}) collective-permute-start(bf16[32,1024]{1,0:T(8,128)(2,1)} %bitcast.33), channel_id=1, source_target_pairs={{0,4},{4,0},{1,5},{5,1},{2,6},{6,2},{3,7},{7,3},{8,12},{12,8},{9,1... | collective-permute-start | bytes 196616 | tf_op jit(solution)/shard_map/ppermute | solution.py:259
  2.6 7.3 %attention_backward.1 = (bf16[128,4096]{1,0:T(8,128)(2,1)}, bf16[128,1024]{1,0:T(8,128)(2,1)}, bf16[1024,512]{1,0:T(8,128)(2,1)}) custom-call(s32[512]{0:T(512)} %groups.1, s32[4]{0:T(128)} %lengths.1, bf16[128,4096]{1,0:T(8,128)(2,1)} %bitcast.38, bf16[128,4096]{1,0:T(8,128)(2,1)} %bitcast.39, bf16[128,1024]{1,0:T(8,128)(2,1)} %bitcast.41, ...), custom_call_target="tpu_custom_call" | custom-call | flops 1000000000 | bytes 6000000 | tf_op jit(solution)/shard_map/attention_backward/pallas_call | solution.py:98
  9.9 0.0 collective-permute-done.sibling_ref
  9.9 0.0 copy-start.1
  9.9 18.1 %all-to-all-start = ((bf16[128,8,512]{2,1,0:T(8,128)(2,1)}), bf16[128,8,512]{2,1,0:T(8,128)(2,1)S(1)}, u32[]{:S(2)}, u32[]{:S(2)}) async-start(bf16[128,8,512]{2,1,0:T(8,128)(2,1)} %bitcast.37), calls=%async_computation | async-start | bytes 2097152 | tf_op jit(solution)/shard_map/all_to_all | solution.py:303
  28.0 0.0 copy-start
  28.1 0.0 copy-start.4
  28.1 3.2 %collective-permute-start.1 = (bf16[64,1024]{1,0:T(8,128)(2,1)S(1)}, bf16[64,1024]{1,0:T(8,128)(2,1)S(1)}, u32[]{:S(2)}, u32[]{:S(2)}) collective-permute-start(bf16[64,1024]{1,0:T(8,128)(2,1)S(1)} %constant_dynamic-update-slice_fusion), channel_id=1, source_target_pairs={{0,8},{4,60},{8,16},{12,4},{16,24},{20,12},{24,32},{28,20},{32,40}... | collective-permute-start | bytes 393224 | tf_op jit(solution)/shard_map/ppermute | solution.py:270
  31.2 4.3 %collective-permute-start.2 = (bf16[64,1024]{1,0:T(8,128)(2,1)S(1)}, bf16[64,1024]{1,0:T(8,128)(2,1)S(1)}, u32[]{:S(2)}, u32[]{:S(2)}) collective-permute-start(bf16[64,1024]{1,0:T(8,128)(2,1)S(1)} %constant_dynamic-update-slice_fusion), channel_id=1, source_target_pairs={{0,16},{4,52},{8,24},{12,60},{16,32},{20,4},{24,40},{28,12},{32,48... | collective-permute-start | bytes 393224 | tf_op jit(solution)/shard_map/ppermute | solution.py:270
  35.5 4.6 %collective-permute-start.3 = (bf16[64,1024]{1,0:T(8,128)(2,1)S(1)}, bf16[64,1024]{1,0:T(8,128)(2,1)S(1)}, u32[]{:S(2)}, u32[]{:S(2)}) collective-permute-start(bf16[64,1024]{1,0:T(8,128)(2,1)S(1)} %constant_dynamic-update-slice_fusion), channel_id=1, source_target_pairs={{0,24},{4,44},{8,32},{12,52},{16,40},{20,60},{24,48},{28,4},{32,56... | collective-permute-start | bytes 393224 | tf_op jit(solution)/shard_map/ppermute | solution.py:270
  40.1 4.3 %collective-permute-start.4 = (bf16[32,1024]{1,0:T(8,128)(2,1)S(1)}, bf16[32,1024]{1,0:T(8,128)(2,1)S(1)}, u32[]{:S(2)}, u32[]{:S(2)}) collective-permute-start(bf16[32,1024]{1,0:T(8,128)(2,1)S(1)} %bitcast.35), channel_id=1, source_target_pairs={{0,32},{8,40},{16,48},{24,56},{32,0},{40,8},{48,16},{56,24},{1,33}... | collective-permute-start | bytes 196616 | tf_op jit(solution)/shard_map/ppermute | solution.py:264
  44.4 3.4 %collective-permute-start.5 = (bf16[8,4096]{1,0:T(8,128)(2,1)S(1)}, bf16[8,4096]{1,0:T(8,128)(2,1)S(1)}, u32[]{:S(2)}, u32[]{:S(2)}) collective-permute-start(bf16[8,4096]{1,0:T(8,128)(2,1)S(1)} %dynamic-slice_bitcast_fusion.2), channel_id=1, source_target_pairs={{0,1},{1,2},{2,3},{3,0},{4,5},{5,6},{6,7},{7,4},{8,9},{9,10},{10,1... | collective-permute-start | bytes 196616 | tf_op jit(solution)/shard_map/ppermute | solution.py:264
  47.8 0.1 broadcast_in_dim.14
  48.0 0.2 broadcast_in_dim_reshape.3.groups_ref
  48.2 19.0 %collective-permute-done.4.refs_3_ = bf16[32,1024]{1,0:T(8,128)(2,1)S(1)} collective-permute-done((bf16[32,1024]{1,0:T(8,128)(2,1)S(1)}, bf16[32,1024]{1,0:T(8,128)(2,1)S(1)}, u32[]{:S(2)}, u32[]{:S(2)}) %collective-permute-start.4) | collective-permute-done | bytes 65568 | tf_op jit(solution)/shard_map/ppermute | solution.py:264
  67.1 0.0 collective-permute-done.1.refs_0_
  67.1 0.0 collective-permute-done.2.refs_1_
  67.2 1.1 page_sum.1
  68.3 7.0 %all-to-all-start.1 = ((bf16[8,32,1024]{2,1,0:T(8,128)(2,1)}), bf16[8,32,1024]{2,1,0:T(8,128)(2,1)S(1)}, u32[]{:S(2)}, u32[]{:S(2)}) async-start(bf16[8,32,1024]{2,1,0:T(8,128)(2,1)} %page_sum.1), calls=%async_computation.1 | async-start | bytes 1048576 | tf_op jit(solution)/shard_map/all_to_all | solution.py:314
  75.3 1.9 %collective-permute-start.6 = (bf16[7,32,1024]{2,1,0:T(8,128)(2,1)S(1)}, bf16[7,32,1024]{2,1,0:T(8,128)(2,1)S(1)}, u32[]{:S(2)}, u32[]{:S(2)}) collective-permute-start(bf16[7,32,1024]{2,1,0:T(8,128)(2,1)S(1)} %weight_rows.1.near_ref), channel_id=1, source_target_pairs={{0,4},{4,0},{1,5},{5,1},{2,6},{6,2},{3,7},{7,3},{8,12},{12,8},{9,1... | collective-permute-start | bytes 1376264 | tf_op jit(solution)/shard_map/ppermute | solution.py:259
  77.3 0.0 copy-start.2
  77.3 4.0 %collective-permute-start.7 = (bf16[8,4096]{1,0:T(8,128)(2,1)S(1)}, bf16[8,4096]{1,0:T(8,128)(2,1)S(1)}, u32[]{:S(2)}, u32[]{:S(2)}) collective-permute-start(bf16[8,4096]{1,0:T(8,128)(2,1)S(1)} %get-tuple-element.38), channel_id=1, source_target_pairs={{0,2},{1,3},{2,0},{3,1},{4,6},{5,7},{6,4},{7,5},{8,10},{9,11},{10,... | collective-permute-start | bytes 196616 | tf_op jit(solution)/shard_map/ppermute | solution.py:264
  81.3 3.3 %collective-permute-start.8 = (bf16[8,4096]{1,0:T(8,128)(2,1)S(1)}, bf16[8,4096]{1,0:T(8,128)(2,1)S(1)}, u32[]{:S(2)}, u32[]{:S(2)}) collective-permute-start(bf16[8,4096]{1,0:T(8,128)(2,1)S(1)} %get-tuple-element.37), channel_id=1, source_target_pairs={{0,3},{1,0},{2,1},{3,2},{4,7},{5,4},{6,5},{7,6},{8,11},{9,8},{10,9... | collective-permute-start | bytes 196616 | tf_op jit(solution)/shard_map/ppermute | solution.py:264
  84.7 0.5 collective-permute-done.7.refs_1_
  85.2 2.3 %collective-permute-done.8.refs_2_ = bf16[8,4096]{1,0:T(8,128)(2,1)S(1)} collective-permute-done((bf16[8,4096]{1,0:T(8,128)(2,1)S(1)}, bf16[8,4096]{1,0:T(8,128)(2,1)S(1)}, u32[]{:S(2)}, u32[]{:S(2)}) %collective-permute-start.8) | collective-permute-done | bytes 65568 | tf_op jit(solution)/shard_map/ppermute | solution.py:264
  87.5 1.1 all-to-all-done.1
  88.6 0.6 projection.1
  89.2 19.7 %all_to_all.20 = bf16[32,8,512]{2,1,0:T(8,128)(2,1)S(1)} all-to-all(bf16[32,8,512]{2,1,0:T(8,128)(2,1)S(1)} %bitcast.27), channel_id=1, replica_groups=mesh['z'=8,'y'=8,'core'=2,'section'=4] {'z','section'}, dimensions={0} | all-to-all | bytes 524288 | tf_op jit(solution)/shard_map/all_to_all | solution.py:245
  108.9 0.4 norm_terms.1
  109.4 0.0 copy-start.3
  109.4 10.0 %all_to_all.21 = bf16[4,8,4096]{2,1,0:T(8,128)(2,1)S(1)} all-to-all(bf16[4,8,4096]{2,1,0:T(8,128)(2,1)S(1)} %bitcast.29), channel_id=1, replica_groups=mesh['z'=8,'y'=8,'core'=2,'section'=4] {'section'}, dimensions={0} | all-to-all | bytes 524288 | tf_op jit(solution)/shard_map/all_to_all | solution.py:254
  119.3 0.8 fusion.1
  (14 shorter events, 0.1 us)
Async XLA Ops:
  0.6 9.3 %collective-permute-start = (bf16[32,1024]{1,0:T(8,128)(2,1)}, bf16[32,1024]{1,0:T(8,128)(2,1)S(1)}, u32[]{:S(2)}, u32[]{:S(2)}) collective-permute-start(bf16[32,1024]{1,0:T(8,128)(2,1)} %bitcast.33), channel_id=1, source_target_pairs={{0,4},{4,0},{1,5},{5,1},{2,6},{6,2},{3,7},{7,3},{8,12},{12,8},{9,1... | collective-permute-start | bytes 196616 | tf_op jit(solution)/shard_map/ppermute | solution.py:259
  9.9 18.1 %copy-start.1 = (bf16[1,32,1024]{2,1,0:T(8,128)(2,1)S(1)}, bf16[1,32,1024]{2,1,0:T(8,128)(2,1)}, u32[]{:S(2)}) copy-start(bf16[1,32,1024]{2,1,0:T(8,128)(2,1)} %param.17) | copy-start | bytes 196612
  9.9 57.3 %all-to-all-start = ((bf16[128,8,512]{2,1,0:T(8,128)(2,1)}), bf16[128,8,512]{2,1,0:T(8,128)(2,1)S(1)}, u32[]{:S(2)}, u32[]{:S(2)}) async-start(bf16[128,8,512]{2,1,0:T(8,128)(2,1)} %bitcast.37), calls=%async_computation | async-start | bytes 2097152 | tf_op jit(solution)/shard_map/all_to_all | solution.py:303
  28.0 16.4 %copy-start = (bf16[1,32,4096]{2,1,0:T(8,128)(2,1)S(1)}, bf16[1,32,4096]{2,1,0:T(8,128)(2,1)}, u32[]{:S(2)}) copy-start(bf16[1,32,4096]{2,1,0:T(8,128)(2,1)} %param.15) | copy-start | bytes 786436
  28.1 19.8 %copy-start.4 = (s32[512]{0:T(512)S(1)}, s32[512]{0:T(512)}, u32[]{:S(2)}) copy-start(s32[512]{0:T(512)} %groups.1) | copy-start | bytes 6148
  28.1 39.1 %collective-permute-start.1 = (bf16[64,1024]{1,0:T(8,128)(2,1)S(1)}, bf16[64,1024]{1,0:T(8,128)(2,1)S(1)}, u32[]{:S(2)}, u32[]{:S(2)}) collective-permute-start(bf16[64,1024]{1,0:T(8,128)(2,1)S(1)} %constant_dynamic-update-slice_fusion), channel_id=1, source_target_pairs={{0,8},{4,60},{8,16},{12,4},{16,24},{20,12},{24,32},{28,20},{32,40}... | collective-permute-start | bytes 393224 | tf_op jit(solution)/shard_map/ppermute | solution.py:270
  31.2 35.9 %collective-permute-start.2 = (bf16[64,1024]{1,0:T(8,128)(2,1)S(1)}, bf16[64,1024]{1,0:T(8,128)(2,1)S(1)}, u32[]{:S(2)}, u32[]{:S(2)}) collective-permute-start(bf16[64,1024]{1,0:T(8,128)(2,1)S(1)} %constant_dynamic-update-slice_fusion), channel_id=1, source_target_pairs={{0,16},{4,52},{8,24},{12,60},{16,32},{20,4},{24,40},{28,12},{32,48... | collective-permute-start | bytes 393224 | tf_op jit(solution)/shard_map/ppermute | solution.py:270
  35.5 31.6 %collective-permute-start.3 = (bf16[64,1024]{1,0:T(8,128)(2,1)S(1)}, bf16[64,1024]{1,0:T(8,128)(2,1)S(1)}, u32[]{:S(2)}, u32[]{:S(2)}) collective-permute-start(bf16[64,1024]{1,0:T(8,128)(2,1)S(1)} %constant_dynamic-update-slice_fusion), channel_id=1, source_target_pairs={{0,24},{4,44},{8,32},{12,52},{16,40},{20,60},{24,48},{28,4},{32,56... | collective-permute-start | bytes 393224 | tf_op jit(solution)/shard_map/ppermute | solution.py:270
  40.1 27.0 %collective-permute-start.4 = (bf16[32,1024]{1,0:T(8,128)(2,1)S(1)}, bf16[32,1024]{1,0:T(8,128)(2,1)S(1)}, u32[]{:S(2)}, u32[]{:S(2)}) collective-permute-start(bf16[32,1024]{1,0:T(8,128)(2,1)S(1)} %bitcast.35), channel_id=1, source_target_pairs={{0,32},{8,40},{16,48},{24,56},{32,0},{40,8},{48,16},{56,24},{1,33}... | collective-permute-start | bytes 196616 | tf_op jit(solution)/shard_map/ppermute | solution.py:264
  44.4 22.8 %collective-permute-start.5 = (bf16[8,4096]{1,0:T(8,128)(2,1)S(1)}, bf16[8,4096]{1,0:T(8,128)(2,1)S(1)}, u32[]{:S(2)}, u32[]{:S(2)}) collective-permute-start(bf16[8,4096]{1,0:T(8,128)(2,1)S(1)} %dynamic-slice_bitcast_fusion.2), channel_id=1, source_target_pairs={{0,1},{1,2},{2,3},{3,0},{4,5},{5,6},{6,7},{7,4},{8,9},{9,10},{10,1... | collective-permute-start | bytes 196616 | tf_op jit(solution)/shard_map/ppermute | solution.py:264
  68.3 20.3 %all-to-all-start.1 = ((bf16[8,32,1024]{2,1,0:T(8,128)(2,1)}), bf16[8,32,1024]{2,1,0:T(8,128)(2,1)S(1)}, u32[]{:S(2)}, u32[]{:S(2)}) async-start(bf16[8,32,1024]{2,1,0:T(8,128)(2,1)} %page_sum.1), calls=%async_computation.1 | async-start | bytes 1048576 | tf_op jit(solution)/shard_map/all_to_all | solution.py:314
  75.3 12.2 %collective-permute-start.6 = (bf16[7,32,1024]{2,1,0:T(8,128)(2,1)S(1)}, bf16[7,32,1024]{2,1,0:T(8,128)(2,1)S(1)}, u32[]{:S(2)}, u32[]{:S(2)}) collective-permute-start(bf16[7,32,1024]{2,1,0:T(8,128)(2,1)S(1)} %weight_rows.1.near_ref), channel_id=1, source_target_pairs={{0,4},{4,0},{1,5},{5,1},{2,6},{6,2},{3,7},{7,3},{8,12},{12,8},{9,1... | collective-permute-start | bytes 1376264 | tf_op jit(solution)/shard_map/ppermute | solution.py:259
  77.3 11.4 %copy-start.2 = (bf16[1,4096]{1,0:T(2,128)(2,1)S(1)}, bf16[1,4096]{1,0:T(2,128)(2,1)}, u32[]{:S(2)}) copy-start(bf16[1,4096]{1,0:T(2,128)(2,1)} %gain_ref.1) | copy-start | bytes 24580
  77.3 7.9 %collective-permute-start.7 = (bf16[8,4096]{1,0:T(8,128)(2,1)S(1)}, bf16[8,4096]{1,0:T(8,128)(2,1)S(1)}, u32[]{:S(2)}, u32[]{:S(2)}) collective-permute-start(bf16[8,4096]{1,0:T(8,128)(2,1)S(1)} %get-tuple-element.38), channel_id=1, source_target_pairs={{0,2},{1,3},{2,0},{3,1},{4,6},{5,7},{6,4},{7,5},{8,10},{9,11},{10,... | collective-permute-start | bytes 196616 | tf_op jit(solution)/shard_map/ppermute | solution.py:264
  81.3 6.2 %collective-permute-start.8 = (bf16[8,4096]{1,0:T(8,128)(2,1)S(1)}, bf16[8,4096]{1,0:T(8,128)(2,1)S(1)}, u32[]{:S(2)}, u32[]{:S(2)}) collective-permute-start(bf16[8,4096]{1,0:T(8,128)(2,1)S(1)} %get-tuple-element.37), channel_id=1, source_target_pairs={{0,3},{1,0},{2,1},{3,2},{4,7},{5,4},{6,5},{7,6},{8,11},{9,8},{10,9... | collective-permute-start | bytes 196616 | tf_op jit(solution)/shard_map/ppermute | solution.py:264
  109.4 10.0 %copy-start.3 = (bf16[32,4096]{1,0:T(8,128)(2,1)S(1)}, bf16[32,4096]{1,0:T(8,128)(2,1)}, u32[]{:S(2)}) copy-start(bf16[32,4096]{1,0:T(8,128)(2,1)} %param.18) | copy-start | bytes 786436

commit v3 on v2

--- a/solution.py
+++ b/solution.py
@@ -275,9 +275,8 @@
     return turn(lax.dynamic_index_in_dim(hidden, lax.rem(here + k, size), keepdims=False), "section", k)
 
 
-def gather_rows(weight, sibling):
+def gather_rows(weight, both):
     rows = lax.axis_size("y")
-    both = jnp.concatenate([weight, sibling], axis=0)
     pieces = [part_ways(both, j) for j in range(1, rows // 2)] + [turn(weight, "y", rows // 2)]
     return pl.pallas_call(
         collect_kernel,
@@ -292,18 +291,17 @@
     prompt_count, devices = owner_map.shape
     sections = lax.axis_size("section")
     width = prompt_hidden.shape[-1]
-    weight = kv_weight[0]
-    sibling = swap(weight)
-    hidden = prompt_hidden[0].reshape(sections, prompt_count // sections, width)
     query_out, own_out, outgoing = attention(
         queries[0], out_grad[0], resp_kv[0], prompt_kv[0], group_list, lengths, owner_map
     )
-    outgoing, weight, sibling, hidden = lax.optimization_barrier((outgoing, weight, sibling, hidden))
+    hidden = prompt_hidden[0].reshape(sections, prompt_count // sections, width)
+    outgoing, weight, hidden = lax.optimization_barrier((outgoing, kv_weight[0], hidden))
     outgoing = outgoing.reshape(devices, -1, WIDE // 2)
     incoming = lax.all_to_all(outgoing, RESP_AXES, split_axis=0, concat_axis=0, tiled=True)
-    near = gather_rows(weight, sibling)
-    layers = [hidden, hand_over(hidden, 1)]
-    incoming, near, layers = lax.optimization_barrier((incoming, near, layers))
+    sibling = swap(weight)
+    both = jnp.concatenate([weight, sibling], axis=0)
+    layers = [hidden] + [hand_over(hidden, k) for k in range(1, sections)]
+    incoming, weight, sibling, both, layers = lax.optimization_barrier((incoming, weight, sibling, both, layers))
     pages = pl.pallas_call(
         page_kernel,
         out_shape=jax.ShapeDtypeStruct((lax.axis_size("z"), prompt_count, WIDE), BF16),
@@ -312,9 +310,8 @@
         name="page_sum",
     )(jnp.repeat(group_list, 2)[None, :], incoming.reshape(-1, WIDE // 2))
     pages = lax.all_to_all(pages, "z", split_axis=0, concat_axis=0, tiled=True)
+    near = gather_rows(weight, both)
     far = swap(near)
-    layers += [hand_over(layers[0], k) for k in range(2, sections)]
-    pages, far, layers = lax.optimization_barrier((pages, far, layers))
     prompt_out = finish(pages, [weight, sibling, near, far], layers, norm_gain, upper_grad)
     return (query_out[None], own_out[None], prompt_out[None])
 

time: 121 us -> 123 us (1.017)
  starting transfers between devices: 56 us -> 52.5 us
  waiting for transfers between devices: 22.9 us -> 26.3 us
  blocking collectives: 29.7 us -> 31.7 us
    all_to_all x1, waiting for transfers between devices: 0.01 us -> 15.7 us  [body(): lax.all_to_all(outgoing, RESP_AXES, split_axis=0, concat_axis=0, tiled=True)]
    ppermute x4, waiting for transfers between devices: 21.8 us -> 8.78 us  [turn(): return lax.ppermute(piece, axis, [(i, (i + k) % size) for i in range(size)])]
    all_to_all x1, starting transfers between devices: 7.02 us -> 3.49 us  [body(): pages = lax.all_to_all(pages, 'z', split_axis=0, concat_axis=0, tiled=True)]
    all_to_all x1, blocking collectives: 19.7 us -> 21.8 us  [finish(): lax.all_to_all(scaled, ('z', 'section'), split_axis=0, concat_axis=0, til...]
    ppermute x2, waiting for transfers between devices: 0.01 us -> 1.78 us  [swap(): return lax.ppermute(piece, 'core', [(0, 1), (1, 0)])]
    ppermute x4, starting transfers between devices: 15 us -> 16.6 us  [turn(): return lax.ppermute(piece, axis, [(i, (i + k) % size) for i in range(size)])]
    ppermute x3, starting transfers between devices: 12 us -> 10.5 us  [part_ways(): return lax.ppermute(piece, ('y', 'core'), pairs)]
  transfers between devices with their start and end apart: 11 -> 11, of which waited for: 4 -> 5; matrix products, arithmetic and copies ran while one was open for 0% -> 0% of each run, Pallas kernels for 6% -> 0%
where the time goes in v3:
time: 123 us; the launch traced here: 122 us
  starting transfers between devices  52.5 us (43%)
  blocking collectives  31.7 us (26%)
  waiting for transfers between devices  26.3 us (21%)
  Pallas kernels  9.5 us (8%)
    all_to_all x1, blocking collectives, finish(): lax.all_to_all(scaled, ('z', 'section'), split_axis=0, concat_axis=0, til...  21.8 us
    all_to_all x1, starting transfers between devices, body(): lax.all_to_all(outgoing, RESP_AXES, split_axis=0, concat_axis=0, tiled=True)  18 us
    ppermute x4, starting transfers between devices, turn(): return lax.ppermute(piece, axis, [(i, (i + k) % size) for i in range(size)])  16.6 us
    all_to_all x1, waiting for transfers between devices, body(): lax.all_to_all(outgoing, RESP_AXES, split_axis=0, concat_axis=0, tiled=True)  15.7 us
    ppermute x3, starting transfers between devices, part_ways(): return lax.ppermute(piece, ('y', 'core'), pairs)  10.5 us
    all_to_all x1, blocking collectives, finish(): lax.all_to_all(sums.reshape(sections, quarter, width), 'section', split_a...  9.95 us
    ppermute x4, waiting for transfers between devices, turn(): return lax.ppermute(piece, axis, [(i, (i + k) % size) for i in range(size)])  8.78 us
    pallas_call x1, Pallas kernels, attention(): pl.pallas_call(attention_kernel, grid_spec=pltpu.PrefetchScalarGridSpec(n...  7.34 us
  transfers between devices with their start and end apart: 11, of which 5 were waited for; matrix products, arithmetic and copies ran while one was open for 0% of the time, Pallas kernels for 0%

profile of v3, /device:TPU:2, one launch (start us, length us, event | category | flops | bytes accessed | tf_op | source)
XLA Modules:
  0.0 121.9 jit_solution(1226149126485191237)
XLA Ops:
  0.6 7.3 %attention_backward.1 = (bf16[128,4096]{1,0:T(8,128)(2,1)}, bf16[128,1024]{1,0:T(8,128)(2,1)}, bf16[1024,512]{1,0:T(8,128)(2,1)}) custom-call(s32[512]{0:T(512)} %groups.1, s32[4]{0:T(128)} %lengths.1, bf16[128,4096]{1,0:T(8,128)(2,1)} %bitcast.37, bf16[128,4096]{1,0:T(8,128)(2,1)} %bitcast.38, bf16[128,1024]{1,0:T(8,128)(2,1)} %bitcast.40, ...), custom_call_target="tpu_custom_call" | custom-call | flops 1000000000 | bytes 6000000 | tf_op jit(solution)/shard_map/attention_backward/pallas_call | solution.py:98
  8.0 0.0 copy-start.1
  8.0 0.0 copy-start
  8.0 18.0 %all-to-all-start = ((bf16[128,8,512]{2,1,0:T(8,128)(2,1)}), bf16[128,8,512]{2,1,0:T(8,128)(2,1)S(1)}, u32[]{:S(2)}, u32[]{:S(2)}) async-start(bf16[128,8,512]{2,1,0:T(8,128)(2,1)} %bitcast.36), calls=%async_computation | async-start | bytes 2097152 | tf_op jit(solution)/shard_map/all_to_all | solution.py:300
  26.0 1.9 %collective-permute-start = (bf16[32,1024]{1,0:T(8,128)(2,1)S(1)}, bf16[32,1024]{1,0:T(8,128)(2,1)S(1)}, u32[]{:S(2)}, u32[]{:S(2)}) collective-permute-start(bf16[32,1024]{1,0:T(8,128)(2,1)S(1)} %bitcast.32), channel_id=1, source_target_pairs={{0,4},{4,0},{1,5},{5,1},{2,6},{6,2},{3,7},{7,3},{8,12},{12,8},{9,1... | collective-permute-start | bytes 196616 | tf_op jit(solution)/shard_map/ppermute | solution.py:259
  28.0 0.0 copy-start.4
  28.0 3.4 %collective-permute-start.1 = (bf16[8,4096]{1,0:T(8,128)(2,1)S(1)}, bf16[8,4096]{1,0:T(8,128)(2,1)S(1)}, u32[]{:S(2)}, u32[]{:S(2)}) collective-permute-start(bf16[8,4096]{1,0:T(8,128)(2,1)S(1)} %get-tuple-element.33), channel_id=1, source_target_pairs={{0,1},{1,2},{2,3},{3,0},{4,5},{5,6},{6,7},{7,4},{8,9},{9,10},{10,1... | collective-permute-start | bytes 196616 | tf_op jit(solution)/shard_map/ppermute | solution.py:264
  31.4 3.0 %collective-permute-start.2 = (bf16[8,4096]{1,0:T(8,128)(2,1)S(1)}, bf16[8,4096]{1,0:T(8,128)(2,1)S(1)}, u32[]{:S(2)}, u32[]{:S(2)}) collective-permute-start(bf16[8,4096]{1,0:T(8,128)(2,1)S(1)} %get-tuple-element.32), channel_id=1, source_target_pairs={{0,2},{1,3},{2,0},{3,1},{4,6},{5,7},{6,4},{7,5},{8,10},{9,11},{10,... | collective-permute-start | bytes 196616 | tf_op jit(solution)/shard_map/ppermute | solution.py:264
  34.4 4.1 %collective-permute-start.3 = (bf16[8,4096]{1,0:T(8,128)(2,1)S(1)}, bf16[8,4096]{1,0:T(8,128)(2,1)S(1)}, u32[]{:S(2)}, u32[]{:S(2)}) collective-permute-start(bf16[8,4096]{1,0:T(8,128)(2,1)S(1)} %get-tuple-element.31), channel_id=1, source_target_pairs={{0,3},{1,0},{2,1},{3,2},{4,7},{5,4},{6,5},{7,6},{8,11},{9,8},{10,9... | collective-permute-start | bytes 196616 | tf_op jit(solution)/shard_map/ppermute | solution.py:264
  38.5 0.1 broadcast_in_dim.14
  38.6 0.2 broadcast_in_dim_reshape.3.groups_ref
  38.8 0.0 collective-permute-done.1.refs_0_
  38.8 0.2 collective-permute-done.2.refs_1_
  39.1 1.5 %collective-permute-done.3.refs_2_ = bf16[8,4096]{1,0:T(8,128)(2,1)S(1)} collective-permute-done((bf16[8,4096]{1,0:T(8,128)(2,1)S(1)}, bf16[8,4096]{1,0:T(8,128)(2,1)S(1)}, u32[]{:S(2)}, u32[]{:S(2)}) %collective-permute-start.3) | collective-permute-done | bytes 65568 | tf_op jit(solution)/shard_map/ppermute | solution.py:264
  40.6 15.7 %all-to-all-done = bf16[128,8,512]{2,1,0:T(8,128)(2,1)S(1)} async-done(((bf16[128,8,512]{2,1,0:T(8,128)(2,1)}), bf16[128,8,512]{2,1,0:T(8,128)(2,1)S(1)}, u32[]{:S(2)}, u32[]{:S(2)}) %all-to-all-start) | async-done | bytes 1048608 | tf_op jit(solution)/shard_map/all_to_all | solution.py:300
  56.2 1.1 page_sum.1
  57.4 3.5 %all-to-all-start.1 = ((bf16[8,32,1024]{2,1,0:T(8,128)(2,1)}), bf16[8,32,1024]{2,1,0:T(8,128)(2,1)S(1)}, u32[]{:S(2)}, u32[]{:S(2)}) async-start(bf16[8,32,1024]{2,1,0:T(8,128)(2,1)} %page_sum.1), calls=%async_computation.1 | async-start | bytes 1048576 | tf_op jit(solution)/shard_map/all_to_all | solution.py:312
  60.9 0.0 copy-start.2
  60.9 4.2 %collective-permute-start.4 = (bf16[64,1024]{1,0:T(8,128)(2,1)S(1)}, bf16[64,1024]{1,0:T(8,128)(2,1)S(1)}, u32[]{:S(2)}, u32[]{:S(2)}) collective-permute-start(bf16[64,1024]{1,0:T(8,128)(2,1)S(1)} %pad_maximum_fusion), channel_id=1, source_target_pairs={{0,8},{4,60},{8,16},{12,4},{16,24},{20,12},{24,32},{28,20},{32,40}... | collective-permute-start | bytes 393224 | tf_op jit(solution)/shard_map/ppermute | solution.py:270
  65.1 2.7 %collective-permute-start.5 = (bf16[64,1024]{1,0:T(8,128)(2,1)S(1)}, bf16[64,1024]{1,0:T(8,128)(2,1)S(1)}, u32[]{:S(2)}, u32[]{:S(2)}) collective-permute-start(bf16[64,1024]{1,0:T(8,128)(2,1)S(1)} %pad_maximum_fusion), channel_id=1, source_target_pairs={{0,16},{4,52},{8,24},{12,60},{16,32},{20,4},{24,40},{28,12},{32,48... | collective-permute-start | bytes 393224 | tf_op jit(solution)/shard_map/ppermute | solution.py:270
  67.8 3.6 %collective-permute-start.6 = (bf16[64,1024]{1,0:T(8,128)(2,1)S(1)}, bf16[64,1024]{1,0:T(8,128)(2,1)S(1)}, u32[]{:S(2)}, u32[]{:S(2)}) collective-permute-start(bf16[64,1024]{1,0:T(8,128)(2,1)S(1)} %pad_maximum_fusion), channel_id=1, source_target_pairs={{0,24},{4,44},{8,32},{12,52},{16,40},{20,60},{24,48},{28,4},{32,56... | collective-permute-start | bytes 393224 | tf_op jit(solution)/shard_map/ppermute | solution.py:270
  71.4 6.2 %collective-permute-start.7 = (bf16[32,1024]{1,0:T(8,128)(2,1)S(1)}, bf16[32,1024]{1,0:T(8,128)(2,1)S(1)}, u32[]{:S(2)}, u32[]{:S(2)}) collective-permute-start(bf16[32,1024]{1,0:T(8,128)(2,1)S(1)} %bitcast.34), channel_id=1, source_target_pairs={{0,32},{8,40},{16,48},{24,56},{32,0},{40,8},{48,16},{56,24},{1,33}... | collective-permute-start | bytes 196616 | tf_op jit(solution)/shard_map/ppermute | solution.py:264
  77.6 7.0 %collective-permute-done.7.refs_3_ = bf16[32,1024]{1,0:T(8,128)(2,1)S(1)} collective-permute-done((bf16[32,1024]{1,0:T(8,128)(2,1)S(1)}, bf16[32,1024]{1,0:T(8,128)(2,1)S(1)}, u32[]{:S(2)}, u32[]{:S(2)}) %collective-permute-start.7) | collective-permute-done | bytes 65568 | tf_op jit(solution)/shard_map/ppermute | solution.py:264
  84.7 0.0 collective-permute-done.4.refs_0_
  84.7 1.9 %collective-permute-start.8 = (bf16[7,32,1024]{2,1,0:T(8,128)(2,1)S(1)}, bf16[7,32,1024]{2,1,0:T(8,128)(2,1)S(1)}, u32[]{:S(2)}, u32[]{:S(2)}) collective-permute-start(bf16[7,32,1024]{2,1,0:T(8,128)(2,1)S(1)} %weight_rows.1.near_ref), channel_id=1, source_target_pairs={{0,4},{4,0},{1,5},{5,1},{2,6},{6,2},{3,7},{7,3},{8,12},{12,8},{9,1... | collective-permute-start | bytes 1376264 | tf_op jit(solution)/shard_map/ppermute | solution.py:259
  86.6 1.8 %collective-permute-done.8.far_ref = bf16[7,32,1024]{2,1,0:T(8,128)(2,1)S(1)} collective-permute-done((bf16[7,32,1024]{2,1,0:T(8,128)(2,1)S(1)}, bf16[7,32,1024]{2,1,0:T(8,128)(2,1)S(1)}, u32[]{:S(2)}, u32[]{:S(2)}) %collective-permute-start.8) | collective-permute-done | bytes 458784 | tf_op jit(solution)/shard_map/ppermute | solution.py:259
  88.4 0.6 projection.1
  89.0 21.8 %all_to_all.20 = bf16[32,8,512]{2,1,0:T(8,128)(2,1)S(1)} all-to-all(bf16[32,8,512]{2,1,0:T(8,128)(2,1)S(1)} %bitcast.27), channel_id=1, replica_groups=mesh['z'=8,'y'=8,'core'=2,'section'=4] {'z','section'}, dimensions={0} | all-to-all | bytes 524288 | tf_op jit(solution)/shard_map/all_to_all | solution.py:245
  110.8 0.4 norm_terms.1
  111.2 0.0 copy-start.3
  111.2 9.9 %all_to_all.21 = bf16[4,8,4096]{2,1,0:T(8,128)(2,1)S(1)} all-to-all(bf16[4,8,4096]{2,1,0:T(8,128)(2,1)S(1)} %bitcast.29), channel_id=1, replica_groups=mesh['z'=8,'y'=8,'core'=2,'section'=4] {'section'}, dimensions={0} | all-to-all | bytes 524288 | tf_op jit(solution)/shard_map/all_to_all | solution.py:254
  121.2 0.8 fusion.1
  (12 shorter events, 0.1 us)
Async XLA Ops:
  8.0 18.0 %copy-start.1 = (bf16[1,32,1024]{2,1,0:T(8,128)(2,1)S(1)}, bf16[1,32,1024]{2,1,0:T(8,128)(2,1)}, u32[]{:S(2)}) copy-start(bf16[1,32,1024]{2,1,0:T(8,128)(2,1)} %param.17) | copy-start | bytes 196612
  8.0 19.9 %copy-start = (bf16[1,32,4096]{2,1,0:T(8,128)(2,1)S(1)}, bf16[1,32,4096]{2,1,0:T(8,128)(2,1)}, u32[]{:S(2)}) copy-start(bf16[1,32,4096]{2,1,0:T(8,128)(2,1)} %param.15) | copy-start | bytes 786436
  8.0 48.3 %all-to-all-start = ((bf16[128,8,512]{2,1,0:T(8,128)(2,1)}), bf16[128,8,512]{2,1,0:T(8,128)(2,1)S(1)}, u32[]{:S(2)}, u32[]{:S(2)}) async-start(bf16[128,8,512]{2,1,0:T(8,128)(2,1)} %bitcast.36), calls=%async_computation | async-start | bytes 2097152 | tf_op jit(solution)/shard_map/all_to_all | solution.py:300
  26.0 12.8 %collective-permute-start = (bf16[32,1024]{1,0:T(8,128)(2,1)S(1)}, bf16[32,1024]{1,0:T(8,128)(2,1)S(1)}, u32[]{:S(2)}, u32[]{:S(2)}) collective-permute-start(bf16[32,1024]{1,0:T(8,128)(2,1)S(1)} %bitcast.32), channel_id=1, source_target_pairs={{0,4},{4,0},{1,5},{5,1},{2,6},{6,2},{3,7},{7,3},{8,12},{12,8},{9,1... | collective-permute-start | bytes 196616 | tf_op jit(solution)/shard_map/ppermute | solution.py:259
  28.0 10.5 %copy-start.4 = (s32[512]{0:T(512)S(1)}, s32[512]{0:T(512)}, u32[]{:S(2)}) copy-start(s32[512]{0:T(512)} %groups.1) | copy-start | bytes 6148
  28.0 10.9 %collective-permute-start.1 = (bf16[8,4096]{1,0:T(8,128)(2,1)S(1)}, bf16[8,4096]{1,0:T(8,128)(2,1)S(1)}, u32[]{:S(2)}, u32[]{:S(2)}) collective-permute-start(bf16[8,4096]{1,0:T(8,128)(2,1)S(1)} %get-tuple-element.33), channel_id=1, source_target_pairs={{0,1},{1,2},{2,3},{3,0},{4,5},{5,6},{6,7},{7,4},{8,9},{9,10},{10,1... | collective-permute-start | bytes 196616 | tf_op jit(solution)/shard_map/ppermute | solution.py:264
  31.4 7.7 %collective-permute-start.2 = (bf16[8,4096]{1,0:T(8,128)(2,1)S(1)}, bf16[8,4096]{1,0:T(8,128)(2,1)S(1)}, u32[]{:S(2)}, u32[]{:S(2)}) collective-permute-start(bf16[8,4096]{1,0:T(8,128)(2,1)S(1)} %get-tuple-element.32), channel_id=1, source_target_pairs={{0,2},{1,3},{2,0},{3,1},{4,6},{5,7},{6,4},{7,5},{8,10},{9,11},{10,... | collective-permute-start | bytes 196616 | tf_op jit(solution)/shard_map/ppermute | solution.py:264
  34.4 6.2 %collective-permute-start.3 = (bf16[8,4096]{1,0:T(8,128)(2,1)S(1)}, bf16[8,4096]{1,0:T(8,128)(2,1)S(1)}, u32[]{:S(2)}, u32[]{:S(2)}) collective-permute-start(bf16[8,4096]{1,0:T(8,128)(2,1)S(1)} %get-tuple-element.31), channel_id=1, source_target_pairs={{0,3},{1,0},{2,1},{3,2},{4,7},{5,4},{6,5},{7,6},{8,11},{9,8},{10,9... | collective-permute-start | bytes 196616 | tf_op jit(solution)/shard_map/ppermute | solution.py:264
  57.4 31.0 %all-to-all-start.1 = ((bf16[8,32,1024]{2,1,0:T(8,128)(2,1)}), bf16[8,32,1024]{2,1,0:T(8,128)(2,1)S(1)}, u32[]{:S(2)}, u32[]{:S(2)}) async-start(bf16[8,32,1024]{2,1,0:T(8,128)(2,1)} %page_sum.1), calls=%async_computation.1 | async-start | bytes 1048576 | tf_op jit(solution)/shard_map/all_to_all | solution.py:312
  60.9 27.6 %copy-start.2 = (bf16[1,4096]{1,0:T(2,128)(2,1)S(1)}, bf16[1,4096]{1,0:T(2,128)(2,1)}, u32[]{:S(2)}) copy-start(bf16[1,4096]{1,0:T(2,128)(2,1)} %gain_ref.1) | copy-start | bytes 24580
  60.9 23.8 %collective-permute-start.4 = (bf16[64,1024]{1,0:T(8,128)(2,1)S(1)}, bf16[64,1024]{1,0:T(8,128)(2,1)S(1)}, u32[]{:S(2)}, u32[]{:S(2)}) collective-permute-start(bf16[64,1024]{1,0:T(8,128)(2,1)S(1)} %pad_maximum_fusion), channel_id=1, source_target_pairs={{0,8},{4,60},{8,16},{12,4},{16,24},{20,12},{24,32},{28,20},{32,40}... | collective-permute-start | bytes 393224 | tf_op jit(solution)/shard_map/ppermute | solution.py:270
  65.1 19.6 %collective-permute-start.5 = (bf16[64,1024]{1,0:T(8,128)(2,1)S(1)}, bf16[64,1024]{1,0:T(8,128)(2,1)S(1)}, u32[]{:S(2)}, u32[]{:S(2)}) collective-permute-start(bf16[64,1024]{1,0:T(8,128)(2,1)S(1)} %pad_maximum_fusion), channel_id=1, source_target_pairs={{0,16},{4,52},{8,24},{12,60},{16,32},{20,4},{24,40},{28,12},{32,48... | collective-permute-start | bytes 393224 | tf_op jit(solution)/shard_map/ppermute | solution.py:270
  67.8 16.9 %collective-permute-start.6 = (bf16[64,1024]{1,0:T(8,128)(2,1)S(1)}, bf16[64,1024]{1,0:T(8,128)(2,1)S(1)}, u32[]{:S(2)}, u32[]{:S(2)}) collective-permute-start(bf16[64,1024]{1,0:T(8,128)(2,1)S(1)} %pad_maximum_fusion), channel_id=1, source_target_pairs={{0,24},{4,44},{8,32},{12,52},{16,40},{20,60},{24,48},{28,4},{32,56... | collective-permute-start | bytes 393224 | tf_op jit(solution)/shard_map/ppermute | solution.py:270
  71.4 13.2 %collective-permute-start.7 = (bf16[32,1024]{1,0:T(8,128)(2,1)S(1)}, bf16[32,1024]{1,0:T(8,128)(2,1)S(1)}, u32[]{:S(2)}, u32[]{:S(2)}) collective-permute-start(bf16[32,1024]{1,0:T(8,128)(2,1)S(1)} %bitcast.34), channel_id=1, source_target_pairs={{0,32},{8,40},{16,48},{24,56},{32,0},{40,8},{48,16},{56,24},{1,33}... | collective-permute-start | bytes 196616 | tf_op jit(solution)/shard_map/ppermute | solution.py:264
  84.7 3.7 %collective-permute-start.8 = (bf16[7,32,1024]{2,1,0:T(8,128)(2,1)S(1)}, bf16[7,32,1024]{2,1,0:T(8,128)(2,1)S(1)}, u32[]{:S(2)}, u32[]{:S(2)}) collective-permute-start(bf16[7,32,1024]{2,1,0:T(8,128)(2,1)S(1)} %weight_rows.1.near_ref), channel_id=1, source_target_pairs={{0,4},{4,0},{1,5},{5,1},{2,6},{6,2},{3,7},{7,3},{8,12},{12,8},{9,1... | collective-permute-start | bytes 1376264 | tf_op jit(solution)/shard_map/ppermute | solution.py:259
  111.2 10.0 %copy-start.3 = (bf16[32,4096]{1,0:T(8,128)(2,1)S(1)}, bf16[32,4096]{1,0:T(8,128)(2,1)}, u32[]{:S(2)}) copy-start(bf16[32,4096]{1,0:T(8,128)(2,1)} %param.18) | copy-start | bytes 786436

commit v4 on v3

--- a/solution.py
+++ b/solution.py
@@ -275,12 +275,11 @@
     return turn(lax.dynamic_index_in_dim(hidden, lax.rem(here + k, size), keepdims=False), "section", k)
 
 
-def gather_rows(weight, both):
-    rows = lax.axis_size("y")
-    pieces = [part_ways(both, j) for j in range(1, rows // 2)] + [turn(weight, "y", rows // 2)]
+def collect(pieces, block):
+    count = sum(piece.shape[0] for piece in pieces) // block
     return pl.pallas_call(
         collect_kernel,
-        out_shape=jax.ShapeDtypeStruct((rows - 1,) + weight.shape, BF16),
+        out_shape=jax.ShapeDtypeStruct((count, block, WIDE), BF16),
         compiler_params=SMALL,
         cost_estimate=pl.CostEstimate(flops=0, bytes_accessed=10**6, transcendentals=0),
         name="weight_rows",
@@ -291,17 +290,20 @@
     prompt_count, devices = owner_map.shape
     sections = lax.axis_size("section")
     width = prompt_hidden.shape[-1]
+    middle = turn(kv_weight[0], "y", lax.axis_size("y") // 2)
     query_out, own_out, outgoing = attention(
         queries[0], out_grad[0], resp_kv[0], prompt_kv[0], group_list, lengths, owner_map
     )
     hidden = prompt_hidden[0].reshape(sections, prompt_count // sections, width)
-    outgoing, weight, hidden = lax.optimization_barrier((outgoing, kv_weight[0], hidden))
+    outgoing, weight, hidden, middle = lax.optimization_barrier((outgoing, kv_weight[0], hidden, middle))
     outgoing = outgoing.reshape(devices, -1, WIDE // 2)
     incoming = lax.all_to_all(outgoing, RESP_AXES, split_axis=0, concat_axis=0, tiled=True)
+    layers = [hidden, hand_over(hidden, 1)]
     sibling = swap(weight)
-    both = jnp.concatenate([weight, sibling], axis=0)
-    layers = [hidden] + [hand_over(hidden, k) for k in range(1, sections)]
-    incoming, weight, sibling, both, layers = lax.optimization_barrier((incoming, weight, sibling, both, layers))
+    both, hidden = lax.optimization_barrier((jnp.concatenate([weight, sibling], axis=0), hidden))
+    near = [part_ways(both, 1), part_ways(both, 2)]
+    layers += [hand_over(hidden, k) for k in range(2, sections)]
+    incoming, both, near, layers = lax.optimization_barrier((incoming, both, near, layers))
     pages = pl.pallas_call(
         page_kernel,
         out_shape=jax.ShapeDtypeStruct((lax.axis_size("z"), prompt_count, WIDE), BF16),
@@ -310,7 +312,7 @@
         name="page_sum",
     )(jnp.repeat(group_list, 2)[None, :], incoming.reshape(-1, WIDE // 2))
     pages = lax.all_to_all(pages, "z", split_axis=0, concat_axis=0, tiled=True)
-    near = gather_rows(weight, both)
+    near = collect(near + [part_ways(both, 3), middle], weight.shape[0])
     far = swap(near)
     prompt_out = finish(pages, [weight, sibling, near, far], layers, norm_gain, upper_grad)
     return (query_out[None], own_out[None], prompt_out[None])

time: 123 us -> 118 us (0.959)
  waiting for transfers between devices: 26.3 us -> 22.1 us
    ppermute x3, waiting for transfers between devices: 0.01 us -> 15.2 us  [part_ways(): return lax.ppermute(piece, ('y', 'core'), pairs)]
    all_to_all x1, waiting for transfers between devices: 15.7 us -> 0.92 us  [body(): lax.all_to_all(outgoing, RESP_AXES, split_axis=0, concat_axis=0, tiled=True)]
    ppermute x4, waiting for transfers between devices: 8.78 us -> 3.45 us  [turn(): return lax.ppermute(piece, axis, [(i, (i + k) % size) for i in range(size)])]
    all_to_all x1, starting transfers between devices: 18 us -> 14.2 us  [body(): lax.all_to_all(outgoing, RESP_AXES, split_axis=0, concat_axis=0, tiled=True)]
    all_to_all x1, starting transfers between devices: 3.49 us -> 6.13 us  [body(): pages = lax.all_to_all(pages, 'z', split_axis=0, concat_axis=0, tiled=True)]
  transfers between devices with their start and end apart: 11 -> 11, of which waited for: 5 -> 7; matrix products, arithmetic and copies ran while one was open for 0% -> 0% of each run, Pallas kernels for 0% -> 6%
where the time goes in v4:
time: 118 us; the launch traced here: 117 us
  starting transfers between devices  52.3 us (44%)
  blocking collectives  31 us (26%)
  waiting for transfers between devices  22.1 us (19%)
  Pallas kernels  9.5 us (8%)
    all_to_all x1, blocking collectives, finish(): lax.all_to_all(scaled, ('z', 'section'), split_axis=0, concat_axis=0, til...  21 us
    ppermute x4, starting transfers between devices, turn(): return lax.ppermute(piece, axis, [(i, (i + k) % size) for i in range(size)])  17.6 us
    ppermute x3, waiting for transfers between devices, part_ways(): return lax.ppermute(piece, ('y', 'core'), pairs)  15.2 us
    all_to_all x1, starting transfers between devices, body(): lax.all_to_all(outgoing, RESP_AXES, split_axis=0, concat_axis=0, tiled=True)  14.2 us
    ppermute x3, starting transfers between devices, part_ways(): return lax.ppermute(piece, ('y', 'core'), pairs)  10.4 us
    all_to_all x1, blocking collectives, finish(): lax.all_to_all(sums.reshape(sections, quarter, width), 'section', split_a...  9.95 us
    pallas_call x1, Pallas kernels, attention(): pl.pallas_call(attention_kernel, grid_spec=pltpu.PrefetchScalarGridSpec(n...  7.35 us
    all_to_all x1, starting transfers between devices, body(): pages = lax.all_to_all(pages, 'z', split_axis=0, concat_axis=0, tiled=True)  6.13 us
  transfers between devices with their start and end apart: 11, of which 7 were waited for; matrix products, arithmetic and copies ran while one was open for 0% of the time, Pallas kernels for 6%

profile of v4, /device:TPU:2, one launch (start us, length us, event | category | flops | bytes accessed | tf_op | source)
XLA Modules:
  0.0 116.8 jit_solution(9348281645069956374)
XLA Ops:
  0.6 7.7 %collective-permute-start = (bf16[32,1024]{1,0:T(8,128)(2,1)}, bf16[32,1024]{1,0:T(8,128)(2,1)S(1)}, u32[]{:S(2)}, u32[]{:S(2)}) collective-permute-start(bf16[32,1024]{1,0:T(8,128)(2,1)} %bitcast.33), channel_id=1, source_target_pairs={{0,32},{8,40},{16,48},{24,56},{32,0},{40,8},{48,16},{56,24},{1,33}... | collective-permute-start | bytes 196616 | tf_op jit(solution)/shard_map/ppermute | solution.py:264
  8.4 7.3 %attention_backward.1 = (bf16[128,4096]{1,0:T(8,128)(2,1)}, bf16[128,1024]{1,0:T(8,128)(2,1)}, bf16[1024,512]{1,0:T(8,128)(2,1)}) custom-call(s32[512]{0:T(512)} %groups.1, s32[4]{0:T(128)} %lengths.1, bf16[128,4096]{1,0:T(8,128)(2,1)} %bitcast.38, bf16[128,4096]{1,0:T(8,128)(2,1)} %bitcast.39, bf16[128,1024]{1,0:T(8,128)(2,1)} %bitcast.41, ...), custom_call_target="tpu_custom_call" | custom-call | flops 1000000000 | bytes 6000000 | tf_op jit(solution)/shard_map/attention_backward/pallas_call | solution.py:98
  15.7 0.0 collective-permute-done.refs_3_
  15.7 0.0 copy-start.1
  15.7 0.0 copy-start
  15.8 14.2 %all-to-all-start = ((bf16[128,8,512]{2,1,0:T(8,128)(2,1)}), bf16[128,8,512]{2,1,0:T(8,128)(2,1)S(1)}, u32[]{:S(2)}, u32[]{:S(2)}) async-start(bf16[128,8,512]{2,1,0:T(8,128)(2,1)} %bitcast.37), calls=%async_computation | async-start | bytes 2097152 | tf_op jit(solution)/shard_map/all_to_all | solution.py:300
  30.0 1.9 %collective-permute-start.1 = (bf16[32,1024]{1,0:T(8,128)(2,1)S(1)}, bf16[32,1024]{1,0:T(8,128)(2,1)S(1)}, u32[]{:S(2)}, u32[]{:S(2)}) collective-permute-start(bf16[32,1024]{1,0:T(8,128)(2,1)S(1)} %bitcast.34), channel_id=1, source_target_pairs={{0,4},{4,0},{1,5},{5,1},{2,6},{6,2},{3,7},{7,3},{8,12},{12,8},{9,1... | collective-permute-start | bytes 196616 | tf_op jit(solution)/shard_map/ppermute | solution.py:259
  32.0 3.4 %collective-permute-start.4 = (bf16[8,4096]{1,0:T(8,128)(2,1)S(1)}, bf16[8,4096]{1,0:T(8,128)(2,1)S(1)}, u32[]{:S(2)}, u32[]{:S(2)}) collective-permute-start(bf16[8,4096]{1,0:T(8,128)(2,1)S(1)} %dynamic-slice_bitcast_fusion.2), channel_id=1, source_target_pairs={{0,1},{1,2},{2,3},{3,0},{4,5},{5,6},{6,7},{7,4},{8,9},{9,10},{10,1... | collective-permute-start | bytes 196616 | tf_op jit(solution)/shard_map/ppermute | solution.py:264
  35.4 4.1 %collective-permute-start.3 = (bf16[64,1024]{1,0:T(8,128)(2,1)S(1)}, bf16[64,1024]{1,0:T(8,128)(2,1)S(1)}, u32[]{:S(2)}, u32[]{:S(2)}) collective-permute-start(bf16[64,1024]{1,0:T(8,128)(2,1)S(1)} %pad_maximum_fusion), channel_id=1, source_target_pairs={{0,16},{4,52},{8,24},{12,60},{16,32},{20,4},{24,40},{28,12},{32,48... | collective-permute-start | bytes 393224 | tf_op jit(solution)/shard_map/ppermute | solution.py:270
  39.5 3.4 %collective-permute-start.2 = (bf16[64,1024]{1,0:T(8,128)(2,1)S(1)}, bf16[64,1024]{1,0:T(8,128)(2,1)S(1)}, u32[]{:S(2)}, u32[]{:S(2)}) collective-permute-start(bf16[64,1024]{1,0:T(8,128)(2,1)S(1)} %pad_maximum_fusion), channel_id=1, source_target_pairs={{0,8},{4,60},{8,16},{12,4},{16,24},{20,12},{24,32},{28,20},{32,40}... | collective-permute-start | bytes 393224 | tf_op jit(solution)/shard_map/ppermute | solution.py:270
  42.9 0.0 copy-start.4
  43.0 2.4 %collective-permute-start.6 = (bf16[8,4096]{1,0:T(8,128)(2,1)S(1)}, bf16[8,4096]{1,0:T(8,128)(2,1)S(1)}, u32[]{:S(2)}, u32[]{:S(2)}) collective-permute-start(bf16[8,4096]{1,0:T(8,128)(2,1)S(1)} %get-tuple-element.37), channel_id=1, source_target_pairs={{0,3},{1,0},{2,1},{3,2},{4,7},{5,4},{6,5},{7,6},{8,11},{9,8},{10,9... | collective-permute-start | bytes 196616 | tf_op jit(solution)/shard_map/ppermute | solution.py:264
  45.4 4.0 %collective-permute-start.5 = (bf16[8,4096]{1,0:T(8,128)(2,1)S(1)}, bf16[8,4096]{1,0:T(8,128)(2,1)S(1)}, u32[]{:S(2)}, u32[]{:S(2)}) collective-permute-start(bf16[8,4096]{1,0:T(8,128)(2,1)S(1)} %get-tuple-element.38), channel_id=1, source_target_pairs={{0,2},{1,3},{2,0},{3,1},{4,6},{5,7},{6,4},{7,5},{8,10},{9,11},{10,... | collective-permute-start | bytes 196616 | tf_op jit(solution)/shard_map/ppermute | solution.py:264
  49.5 0.1 broadcast_in_dim.14
  49.6 0.2 broadcast_in_dim_reshape.3.groups_ref
  49.8 3.4 %collective-permute-done.5.refs_1_ = bf16[8,4096]{1,0:T(8,128)(2,1)S(1)} collective-permute-done((bf16[8,4096]{1,0:T(8,128)(2,1)S(1)}, bf16[8,4096]{1,0:T(8,128)(2,1)S(1)}, u32[]{:S(2)}, u32[]{:S(2)}) %collective-permute-start.5) | collective-permute-done | bytes 65568 | tf_op jit(solution)/shard_map/ppermute | solution.py:264
  53.2 5.1 %collective-permute-done.3.refs_1_ = bf16[64,1024]{1,0:T(8,128)(2,1)S(1)} collective-permute-done((bf16[64,1024]{1,0:T(8,128)(2,1)S(1)}, bf16[64,1024]{1,0:T(8,128)(2,1)S(1)}, u32[]{:S(2)}, u32[]{:S(2)}) %collective-permute-start.3) | collective-permute-done | bytes 131104 | tf_op jit(solution)/shard_map/ppermute | solution.py:270
  58.3 1.0 collective-permute-done.2.refs_0_
  59.4 0.9 all-to-all-done
  60.3 1.1 page_sum.1
  61.4 6.1 %all-to-all-start.1 = ((bf16[8,32,1024]{2,1,0:T(8,128)(2,1)}), bf16[8,32,1024]{2,1,0:T(8,128)(2,1)S(1)}, u32[]{:S(2)}, u32[]{:S(2)}) async-start(bf16[8,32,1024]{2,1,0:T(8,128)(2,1)} %page_sum.1), calls=%async_computation.1 | async-start | bytes 1048576 | tf_op jit(solution)/shard_map/all_to_all | solution.py:314
  67.6 3.0 %collective-permute-start.7 = (bf16[64,1024]{1,0:T(8,128)(2,1)S(1)}, bf16[64,1024]{1,0:T(8,128)(2,1)S(1)}, u32[]{:S(2)}, u32[]{:S(2)}) collective-permute-start(bf16[64,1024]{1,0:T(8,128)(2,1)S(1)} %pad_maximum_fusion), channel_id=1, source_target_pairs={{0,24},{4,44},{8,32},{12,52},{16,40},{20,60},{24,48},{28,4},{32,56... | collective-permute-start | bytes 393224 | tf_op jit(solution)/shard_map/ppermute | solution.py:270
  70.5 9.0 %collective-permute-done.7.refs_2_ = bf16[64,1024]{1,0:T(8,128)(2,1)S(1)} collective-permute-done((bf16[64,1024]{1,0:T(8,128)(2,1)S(1)}, bf16[64,1024]{1,0:T(8,128)(2,1)S(1)}, u32[]{:S(2)}, u32[]{:S(2)}) %collective-permute-start.7) | collective-permute-done | bytes 131104 | tf_op jit(solution)/shard_map/ppermute | solution.py:270
  79.6 1.9 %collective-permute-start.8 = (bf16[7,32,1024]{2,1,0:T(8,128)(2,1)S(1)}, bf16[7,32,1024]{2,1,0:T(8,128)(2,1)S(1)}, u32[]{:S(2)}, u32[]{:S(2)}) collective-permute-start(bf16[7,32,1024]{2,1,0:T(8,128)(2,1)S(1)} %weight_rows.1.near_ref), channel_id=1, source_target_pairs={{0,4},{4,0},{1,5},{5,1},{2,6},{6,2},{3,7},{7,3},{8,12},{12,8},{9,1... | collective-permute-start | bytes 1376264 | tf_op jit(solution)/shard_map/ppermute | solution.py:259
  81.5 1.8 %collective-permute-done.8.far_ref = bf16[7,32,1024]{2,1,0:T(8,128)(2,1)S(1)} collective-permute-done((bf16[7,32,1024]{2,1,0:T(8,128)(2,1)S(1)}, bf16[7,32,1024]{2,1,0:T(8,128)(2,1)S(1)}, u32[]{:S(2)}, u32[]{:S(2)}) %collective-permute-start.8) | collective-permute-done | bytes 458784 | tf_op jit(solution)/shard_map/ppermute | solution.py:259
  83.3 0.7 all-to-all-done.1
  84.1 0.6 projection.1
  84.6 21.0 %all_to_all.20 = bf16[32,8,512]{2,1,0:T(8,128)(2,1)S(1)} all-to-all(bf16[32,8,512]{2,1,0:T(8,128)(2,1)S(1)} %bitcast.27), channel_id=1, replica_groups=mesh['z'=8,'y'=8,'core'=2,'section'=4] {'z','section'}, dimensions={0} | all-to-all | bytes 524288 | tf_op jit(solution)/shard_map/all_to_all | solution.py:245
  105.7 0.4 norm_terms.1
  106.1 0.0 copy-start.3
  106.1 10.0 %all_to_all.21 = bf16[4,8,4096]{2,1,0:T(8,128)(2,1)S(1)} all-to-all(bf16[4,8,4096]{2,1,0:T(8,128)(2,1)S(1)} %bitcast.29), channel_id=1, replica_groups=mesh['z'=8,'y'=8,'core'=2,'section'=4] {'section'}, dimensions={0} | all-to-all | bytes 524288 | tf_op jit(solution)/shard_map/all_to_all | solution.py:254
  116.1 0.8 fusion.1
  (13 shorter events, 0.1 us)
Async XLA Ops:
  0.6 15.1 %collective-permute-start = (bf16[32,1024]{1,0:T(8,128)(2,1)}, bf16[32,1024]{1,0:T(8,128)(2,1)S(1)}, u32[]{:S(2)}, u32[]{:S(2)}) collective-permute-start(bf16[32,1024]{1,0:T(8,128)(2,1)} %bitcast.33), channel_id=1, source_target_pairs={{0,32},{8,40},{16,48},{24,56},{32,0},{40,8},{48,16},{56,24},{1,33}... | collective-permute-start | bytes 196616 | tf_op jit(solution)/shard_map/ppermute | solution.py:264
  15.7 14.3 %copy-start.1 = (bf16[1,32,1024]{2,1,0:T(8,128)(2,1)S(1)}, bf16[1,32,1024]{2,1,0:T(8,128)(2,1)}, u32[]{:S(2)}) copy-start(bf16[1,32,1024]{2,1,0:T(8,128)(2,1)} %param.17) | copy-start | bytes 196612
  15.7 16.2 %copy-start = (bf16[1,32,4096]{2,1,0:T(8,128)(2,1)S(1)}, bf16[1,32,4096]{2,1,0:T(8,128)(2,1)}, u32[]{:S(2)}) copy-start(bf16[1,32,4096]{2,1,0:T(8,128)(2,1)} %param.15) | copy-start | bytes 786436
  15.8 44.6 %all-to-all-start = ((bf16[128,8,512]{2,1,0:T(8,128)(2,1)}), bf16[128,8,512]{2,1,0:T(8,128)(2,1)S(1)}, u32[]{:S(2)}, u32[]{:S(2)}) async-start(bf16[128,8,512]{2,1,0:T(8,128)(2,1)} %bitcast.37), calls=%async_computation | async-start | bytes 2097152 | tf_op jit(solution)/shard_map/all_to_all | solution.py:300
  30.0 5.4 %collective-permute-start.1 = (bf16[32,1024]{1,0:T(8,128)(2,1)S(1)}, bf16[32,1024]{1,0:T(8,128)(2,1)S(1)}, u32[]{:S(2)}, u32[]{:S(2)}) collective-permute-start(bf16[32,1024]{1,0:T(8,128)(2,1)S(1)} %bitcast.34), channel_id=1, source_target_pairs={{0,4},{4,0},{1,5},{5,1},{2,6},{6,2},{3,7},{7,3},{8,12},{12,8},{9,1... | collective-permute-start | bytes 196616 | tf_op jit(solution)/shard_map/ppermute | solution.py:259
  32.0 17.8 %collective-permute-start.4 = (bf16[8,4096]{1,0:T(8,128)(2,1)S(1)}, bf16[8,4096]{1,0:T(8,128)(2,1)S(1)}, u32[]{:S(2)}, u32[]{:S(2)}) collective-permute-start(bf16[8,4096]{1,0:T(8,128)(2,1)S(1)} %dynamic-slice_bitcast_fusion.2), channel_id=1, source_target_pairs={{0,1},{1,2},{2,3},{3,0},{4,5},{5,6},{6,7},{7,4},{8,9},{9,10},{10,1... | collective-permute-start | bytes 196616 | tf_op jit(solution)/shard_map/ppermute | solution.py:264
  35.4 22.9 %collective-permute-start.3 = (bf16[64,1024]{1,0:T(8,128)(2,1)S(1)}, bf16[64,1024]{1,0:T(8,128)(2,1)S(1)}, u32[]{:S(2)}, u32[]{:S(2)}) collective-permute-start(bf16[64,1024]{1,0:T(8,128)(2,1)S(1)} %pad_maximum_fusion), channel_id=1, source_target_pairs={{0,16},{4,52},{8,24},{12,60},{16,32},{20,4},{24,40},{28,12},{32,48... | collective-permute-start | bytes 393224 | tf_op jit(solution)/shard_map/ppermute | solution.py:270
  39.5 19.8 %collective-permute-start.2 = (bf16[64,1024]{1,0:T(8,128)(2,1)S(1)}, bf16[64,1024]{1,0:T(8,128)(2,1)S(1)}, u32[]{:S(2)}, u32[]{:S(2)}) collective-permute-start(bf16[64,1024]{1,0:T(8,128)(2,1)S(1)} %pad_maximum_fusion), channel_id=1, source_target_pairs={{0,8},{4,60},{8,16},{12,4},{16,24},{20,12},{24,32},{28,20},{32,40}... | collective-permute-start | bytes 393224 | tf_op jit(solution)/shard_map/ppermute | solution.py:270
  42.9 6.5 %copy-start.4 = (s32[512]{0:T(512)S(1)}, s32[512]{0:T(512)}, u32[]{:S(2)}) copy-start(s32[512]{0:T(512)} %groups.1) | copy-start | bytes 6148
  43.0 6.8 %collective-permute-start.6 = (bf16[8,4096]{1,0:T(8,128)(2,1)S(1)}, bf16[8,4096]{1,0:T(8,128)(2,1)S(1)}, u32[]{:S(2)}, u32[]{:S(2)}) collective-permute-start(bf16[8,4096]{1,0:T(8,128)(2,1)S(1)} %get-tuple-element.37), channel_id=1, source_target_pairs={{0,3},{1,0},{2,1},{3,2},{4,7},{5,4},{6,5},{7,6},{8,11},{9,8},{10,9... | collective-permute-start | bytes 196616 | tf_op jit(solution)/shard_map/ppermute | solution.py:264
  45.4 7.8 %collective-permute-start.5 = (bf16[8,4096]{1,0:T(8,128)(2,1)S(1)}, bf16[8,4096]{1,0:T(8,128)(2,1)S(1)}, u32[]{:S(2)}, u32[]{:S(2)}) collective-permute-start(bf16[8,4096]{1,0:T(8,128)(2,1)S(1)} %get-tuple-element.38), channel_id=1, source_target_pairs={{0,2},{1,3},{2,0},{3,1},{4,6},{5,7},{6,4},{7,5},{8,10},{9,11},{10,... | collective-permute-start | bytes 196616 | tf_op jit(solution)/shard_map/ppermute | solution.py:264
  61.4 22.6 %all-to-all-start.1 = ((bf16[8,32,1024]{2,1,0:T(8,128)(2,1)}), bf16[8,32,1024]{2,1,0:T(8,128)(2,1)S(1)}, u32[]{:S(2)}, u32[]{:S(2)}) async-start(bf16[8,32,1024]{2,1,0:T(8,128)(2,1)} %page_sum.1), calls=%async_computation.1 | async-start | bytes 1048576 | tf_op jit(solution)/shard_map/all_to_all | solution.py:314
  67.6 16.5 %copy-start.2 = (bf16[1,4096]{1,0:T(2,128)(2,1)S(1)}, bf16[1,4096]{1,0:T(2,128)(2,1)}, u32[]{:S(2)}) copy-start(bf16[1,4096]{1,0:T(2,128)(2,1)} %gain_ref.1) | copy-start | bytes 24580
  67.6 12.0 %collective-permute-start.7 = (bf16[64,1024]{1,0:T(8,128)(2,1)S(1)}, bf16[64,1024]{1,0:T(8,128)(2,1)S(1)}, u32[]{:S(2)}, u32[]{:S(2)}) collective-permute-start(bf16[64,1024]{1,0:T(8,128)(2,1)S(1)} %pad_maximum_fusion), channel_id=1, source_target_pairs={{0,24},{4,44},{8,32},{12,52},{16,40},{20,60},{24,48},{28,4},{32,56... | collective-permute-start | bytes 393224 | tf_op jit(solution)/shard_map/ppermute | solution.py:270
  79.6 3.7 %collective-permute-start.8 = (bf16[7,32,1024]{2,1,0:T(8,128)(2,1)S(1)}, bf16[7,32,1024]{2,1,0:T(8,128)(2,1)S(1)}, u32[]{:S(2)}, u32[]{:S(2)}) collective-permute-start(bf16[7,32,1024]{2,1,0:T(8,128)(2,1)S(1)} %weight_rows.1.near_ref), channel_id=1, source_target_pairs={{0,4},{4,0},{1,5},{5,1},{2,6},{6,2},{3,7},{7,3},{8,12},{12,8},{9,1... | collective-permute-start | bytes 1376264 | tf_op jit(solution)/shard_map/ppermute | solution.py:259
  106.1 10.0 %copy-start.3 = (bf16[32,4096]{1,0:T(8,128)(2,1)S(1)}, bf16[32,4096]{1,0:T(8,128)(2,1)}, u32[]{:S(2)}) copy-start(bf16[32,4096]{1,0:T(8,128)(2,1)} %param.18) | copy-start | bytes 786436

commit v5 on v4

--- a/solution.py
+++ b/solution.py
@@ -34,7 +34,7 @@
     return index
 
 
-def attention_kernel(groups, lengths, q_ref, do_ref, own_ref, cache_ref, owner_ref, dq_ref, down_ref, send_ref, mixed_ref):
+def attention_kernel(groups, lengths, q_ref, do_ref, own_ref, cache_ref, owner_ref, grad_ref, down_ref, send_ref, mixed_ref):
     b = pl.program_id(0)
     count = RESP_DEV
     length = lengths[b]
@@ -75,9 +75,7 @@
         grads.append((k, 1, value_cols[k], dot(low[k], do[k], ((1,), (0,)))))
         grads.append((k, 0, key_cols[k], dot(score_grad[k], q[k], ((1,), (0,)))))
     for k in each:
-        dq = dot(score_grad[k], keys[k], ((0,), (0,)))
-        for g, h in enumerate(heads[k * PER : (k + 1) * PER]):
-            dq_ref[:, h] = dq[g * rows : (g + 1) * rows].astype(BF16)
+        grad_ref[k] = score_grad[k]
     for k, half, at, grad in grads:
         down_ref[:, at] = grad[plen:].astype(BF16)
         part = dot(place, grad[:plen].astype(BF16), ((1,), (0,)))
@@ -94,6 +92,7 @@
     total = queries.shape[0]
     rows = total // count
     width = queries.shape[1]
+    keys, lanes = plen + rows, PER * rows
     by_resp = lambda w: pl.BlockSpec((rows, w), lambda b, *_: (b, 0))
     return pl.pallas_call(
         attention_kernel,
@@ -108,20 +107,51 @@
                 pl.BlockSpec(owner_map.shape, lambda b, *_: (0, 0)),
             ],
             out_specs=[
-                by_resp(width),
+                pl.BlockSpec((KVH, keys, lanes), lambda b, *_: (b, 0, 0)),
                 by_resp(WIDE),
                 pl.BlockSpec((2 * count * plen, WIDE // 2), lambda b, *_: (0, 0)),
             ],
             scratch_shapes=[pltpu.VMEM((KVH, 2 * count * plen, HD), F32)],
         ),
         out_shape=[
-            jax.ShapeDtypeStruct((total, width), BF16),
+            jax.ShapeDtypeStruct((count * KVH, keys, lanes), BF16),
             jax.ShapeDtypeStruct((total, WIDE), BF16),
             jax.ShapeDtypeStruct((2 * count * plen, WIDE // 2), BF16),
         ],
         cost_estimate=pl.CostEstimate(flops=10**9, bytes_accessed=6 * 10**6, transcendentals=700000),
         name="attention_backward",
     )(group_list, lengths, queries, out_grad, resp_kv, prompt_kv, owner_map)
+
+
+def query_kernel(grad_ref, own_ref, cache_ref, dq_ref):
+    rows = dq_ref.shape[0]
+    for k in range(KVH):
+        at = slice(k * HD, (k + 1) * HD)
+        keys = jnp.concatenate([cache_ref[:, at], own_ref[:, at]], axis=0)
+        dq = dot(grad_ref[k], keys, ((0,), (0,)))
+        for g in range(PER):
+            h = k * PER + g
+            dq_ref[:, h * HD : (h + 1) * HD] = dq[g * rows : (g + 1) * rows].astype(BF16)
+
+
+def query_gradient(score_grad, resp_kv, prompt_kv):
+    count, plen, _ = prompt_kv.shape
+    total = resp_kv.shape[0]
+    rows = total // count
+    half = KVH * HD
+    return pl.pallas_call(
+        query_kernel,
+        grid=(count,),
+        in_specs=[
+            pl.BlockSpec((KVH,) + score_grad.shape[1:], lambda b: (b, 0, 0)),
+            pl.BlockSpec((rows, half), lambda b: (b, 0)),
+            pl.BlockSpec((None, plen, half), lambda b: (b, 0, 0)),
+        ],
+        out_specs=pl.BlockSpec((rows, QH * HD), lambda b: (b, 0)),
+        out_shape=jax.ShapeDtypeStruct((total, QH * HD), BF16),
+        cost_estimate=pl.CostEstimate(flops=2 * 10**8, bytes_accessed=4 * 10**6, transcendentals=0),
+        name="query_gradient",
+    )(score_grad, resp_kv, prompt_kv)
 
 
 def page_kernel(groups_ref, arrived_ref, page_ref):
@@ -290,12 +320,11 @@
     prompt_count, devices = owner_map.shape
     sections = lax.axis_size("section")
     width = prompt_hidden.shape[-1]
-    middle = turn(kv_weight[0], "y", lax.axis_size("y") // 2)
-    query_out, own_out, outgoing = attention(
+    score_grad, own_out, outgoing = attention(
         queries[0], out_grad[0], resp_kv[0], prompt_kv[0], group_list, lengths, owner_map
     )
     hidden = prompt_hidden[0].reshape(sections, prompt_count // sections, width)
-    outgoing, weight, hidden, middle = lax.optimization_barrier((outgoing, kv_weight[0], hidden, middle))
+    outgoing, weight, hidden = lax.optimization_barrier((outgoing, kv_weight[0], hidden))
     outgoing = outgoing.reshape(devices, -1, WIDE // 2)
     incoming = lax.all_to_all(outgoing, RESP_AXES, split_axis=0, concat_axis=0, tiled=True)
     layers = [hidden, hand_over(hidden, 1)]
@@ -303,7 +332,10 @@
     both, hidden = lax.optimization_barrier((jnp.concatenate([weight, sibling], axis=0), hidden))
     near = [part_ways(both, 1), part_ways(both, 2)]
     layers += [hand_over(hidden, k) for k in range(2, sections)]
-    incoming, both, near, layers = lax.optimization_barrier((incoming, both, near, layers))
+    query_out = query_gradient(score_grad, resp_kv[0], prompt_kv[0])
+    incoming, both, near, layers, weight, query_out = lax.optimization_barrier(
+        (incoming, both, near, layers, weight, query_out)
+    )
     pages = pl.pallas_call(
         page_kernel,
         out_shape=jax.ShapeDtypeStruct((lax.axis_size("z"), prompt_count, WIDE), BF16),
@@ -312,7 +344,8 @@
         name="page_sum",
     )(jnp.repeat(group_list, 2)[None, :], incoming.reshape(-1, WIDE // 2))
     pages = lax.all_to_all(pages, "z", split_axis=0, concat_axis=0, tiled=True)
-    near = collect(near + [part_ways(both, 3), middle], weight.shape[0])
+    near += [part_ways(both, 3), turn(weight, "y", lax.axis_size("y") // 2)]
+    near = collect(near, weight.shape[0])
     far = swap(near)
     prompt_out = finish(pages, [weight, sibling, near, far], layers, norm_gain, upper_grad)
     return (query_out[None], own_out[None], prompt_out[None])

time: 118 us -> 117 us (level)
  the two profiles are of different devices: /device:TPU:2 before, /device:TPU:16 now
where the time goes in v5:
time: 117 us
  starting transfers between devices  55 us (47%)
  blocking collectives  32.5 us (28%)
  waiting for transfers between devices  13.6 us (12%)
  Pallas kernels  13.5 us (12%)
    all_to_all x1, blocking collectives, finish(): lax.all_to_all(scaled, ('z', 'section'), split_axis=0, concat_axis=0, til...  23.2 us
    all_to_all x1, starting transfers between devices, body(): lax.all_to_all(outgoing, RESP_AXES, split_axis=0, concat_axis=0, tiled=True)  17.4 us
    ppermute x4, starting transfers between devices, turn(): return lax.ppermute(piece, axis, [(i, (i + k) % size) for i in range(size)])  15.6 us
    ppermute x3, starting transfers between devices, part_ways(): return lax.ppermute(piece, ('y', 'core'), pairs)  14.4 us
    all_to_all x1, blocking collectives, finish(): lax.all_to_all(sums.reshape(sections, quarter, width), 'section', split_a...  9.33 us
    pallas_call x1, Pallas kernels, attention(): pl.pallas_call(attention_kernel, grid_spec=pltpu.PrefetchScalarGridSpec(n...  7.11 us
    ppermute x4, waiting for transfers between devices, turn(): return lax.ppermute(piece, axis, [(i, (i + k) % size) for i in range(size)])  6.91 us
    all_to_all x1, waiting for transfers between devices, body(): lax.all_to_all(outgoing, RESP_AXES, split_axis=0, concat_axis=0, tiled=True)  4.91 us
  transfers between devices with their start and end apart: 11, of which 3 were waited for; matrix products, arithmetic and copies ran while one was open for 0% of the time, Pallas kernels for 4%

profile of v5, /device:TPU:16, one launch (start us, length us, event | category | flops | bytes accessed | tf_op | source)
XLA Modules:
  0.0 116.6 jit_solution(18406358683532895742)
XLA Ops:
  0.6 7.1 %attention_backward.1 = (bf16[16,160,256]{2,1,0:T(8,128)(2,1)}, bf16[128,1024]{1,0:T(8,128)(2,1)}, bf16[1024,512]{1,0:T(8,128)(2,1)}) custom-call(s32[512]{0:T(512)} %groups.1, s32[4]{0:T(128)} %lengths.1, bf16[128,4096]{1,0:T(8,128)(2,1)} %bitcast.43, bf16[128,4096]{1,0:T(8,128)(2,1)} %bitcast.44, bf16[128,1024]{1,0:T(8,128)(2,1)} %bitcast.41, ...), custom_call_target="tpu_custom_call" | custom-call | flops 1000000000 | bytes 6000000 | tf_op jit(solution)/shard_map/attention_backward/pallas_call | solution.py:97
  7.7 0.0 copy-start.1
  7.8 0.0 copy-start
  7.8 0.0 copy-start.4
  7.8 17.4 %all-to-all-start = ((bf16[128,8,512]{2,1,0:T(8,128)(2,1)}), bf16[128,8,512]{2,1,0:T(8,128)(2,1)S(1)}, u32[]{:S(2)}, u32[]{:S(2)}) async-start(bf16[128,8,512]{2,1,0:T(8,128)(2,1)} %bitcast.40), calls=%async_computation | async-start | bytes 2097152 | tf_op jit(solution)/shard_map/all_to_all | solution.py:329
  25.2 2.1 %collective-permute-start = (bf16[32,1024]{1,0:T(8,128)(2,1)S(1)}, bf16[32,1024]{1,0:T(8,128)(2,1)S(1)}, u32[]{:S(2)}, u32[]{:S(2)}) collective-permute-start(bf16[32,1024]{1,0:T(8,128)(2,1)S(1)} %bitcast.33), channel_id=1, source_target_pairs={{0,4},{4,0},{1,5},{5,1},{2,6},{6,2},{3,7},{7,3},{8,12},{12,8},{9,1... | collective-permute-start | bytes 196616 | tf_op jit(solution)/shard_map/ppermute | solution.py:289
  27.3 3.4 %collective-permute-start.3 = (bf16[8,4096]{1,0:T(8,128)(2,1)S(1)}, bf16[8,4096]{1,0:T(8,128)(2,1)S(1)}, u32[]{:S(2)}, u32[]{:S(2)}) collective-permute-start(bf16[8,4096]{1,0:T(8,128)(2,1)S(1)} %dynamic-slice_bitcast_fusion.2), channel_id=1, source_target_pairs={{0,1},{1,2},{2,3},{3,0},{4,5},{5,6},{6,7},{7,4},{8,9},{9,10},{10,1... | collective-permute-start | bytes 196616 | tf_op jit(solution)/shard_map/ppermute | solution.py:294
  30.8 3.4 %collective-permute-start.1 = (bf16[64,1024]{1,0:T(8,128)(2,1)S(1)}, bf16[64,1024]{1,0:T(8,128)(2,1)S(1)}, u32[]{:S(2)}, u32[]{:S(2)}) collective-permute-start(bf16[64,1024]{1,0:T(8,128)(2,1)S(1)} %pad_maximum_fusion), channel_id=1, source_target_pairs={{0,8},{4,60},{8,16},{12,4},{16,24},{20,12},{24,32},{28,20},{32,40}... | collective-permute-start | bytes 393224 | tf_op jit(solution)/shard_map/ppermute | solution.py:300
  34.1 4.6 %collective-permute-start.2 = (bf16[64,1024]{1,0:T(8,128)(2,1)S(1)}, bf16[64,1024]{1,0:T(8,128)(2,1)S(1)}, u32[]{:S(2)}, u32[]{:S(2)}) collective-permute-start(bf16[64,1024]{1,0:T(8,128)(2,1)S(1)} %pad_maximum_fusion), channel_id=1, source_target_pairs={{0,16},{4,52},{8,24},{12,60},{16,32},{20,4},{24,40},{28,12},{32,48... | collective-permute-start | bytes 393224 | tf_op jit(solution)/shard_map/ppermute | solution.py:300
  38.8 4.6 %collective-permute-start.4 = (bf16[8,4096]{1,0:T(8,128)(2,1)S(1)}, bf16[8,4096]{1,0:T(8,128)(2,1)S(1)}, u32[]{:S(2)}, u32[]{:S(2)}) collective-permute-start(bf16[8,4096]{1,0:T(8,128)(2,1)S(1)} %get-tuple-element.40), channel_id=1, source_target_pairs={{0,2},{1,3},{2,0},{3,1},{4,6},{5,7},{6,4},{7,5},{8,10},{9,11},{10,... | collective-permute-start | bytes 196616 | tf_op jit(solution)/shard_map/ppermute | solution.py:294
  43.4 3.3 %collective-permute-start.5 = (bf16[8,4096]{1,0:T(8,128)(2,1)S(1)}, bf16[8,4096]{1,0:T(8,128)(2,1)S(1)}, u32[]{:S(2)}, u32[]{:S(2)}) collective-permute-start(bf16[8,4096]{1,0:T(8,128)(2,1)S(1)} %get-tuple-element.39), channel_id=1, source_target_pairs={{0,3},{1,0},{2,1},{3,2},{4,7},{5,4},{6,5},{7,6},{8,11},{9,8},{10,9... | collective-permute-start | bytes 196616 | tf_op jit(solution)/shard_map/ppermute | solution.py:294
  46.8 0.1 broadcast_in_dim.14
  46.9 0.2 broadcast_in_dim_reshape.3.groups_ref
  47.1 4.2 %query_gradient.1 = bf16[128,4096]{1,0:T(8,128)(2,1)} custom-call(bf16[16,160,256]{2,1,0:T(8,128)(2,1)} %get-tuple-element.27.grad_ref, bf16[128,1024]{1,0:T(8,128)(2,1)} %bitcast.42, bf16[4,128,1024]{2,1,0:T(8,128)(2,1)} %bitcast.38), custom_call_target="tpu_custom_call" | custom-call | flops 200000000 | bytes 4000000 | tf_op jit(solution)/shard_map/query_gradient/pallas_call | solution.py:142
  51.3 0.0 collective-permute-done.3.refs_0_
  51.3 0.0 collective-permute-done.5.refs_2_
  51.3 0.0 collective-permute-done.2.refs_1_
  51.3 4.9 %all-to-all-done = bf16[128,8,512]{2,1,0:T(8,128)(2,1)S(1)} async-done(((bf16[128,8,512]{2,1,0:T(8,128)(2,1)}), bf16[128,8,512]{2,1,0:T(8,128)(2,1)S(1)}, u32[]{:S(2)}, u32[]{:S(2)}) %all-to-all-start) | async-done | bytes 1048608 | tf_op jit(solution)/shard_map/all_to_all | solution.py:329
  56.2 1.1 page_sum.1
  57.4 3.6 %all-to-all-start.1 = ((bf16[8,32,1024]{2,1,0:T(8,128)(2,1)}), bf16[8,32,1024]{2,1,0:T(8,128)(2,1)S(1)}, u32[]{:S(2)}, u32[]{:S(2)}) async-start(bf16[8,32,1024]{2,1,0:T(8,128)(2,1)} %page_sum.1), calls=%async_computation.1 | async-start | bytes 1048576 | tf_op jit(solution)/shard_map/all_to_all | solution.py:346
  61.0 6.4 %collective-permute-start.6 = (bf16[64,1024]{1,0:T(8,128)(2,1)S(1)}, bf16[64,1024]{1,0:T(8,128)(2,1)S(1)}, u32[]{:S(2)}, u32[]{:S(2)}) collective-permute-start(bf16[64,1024]{1,0:T(8,128)(2,1)S(1)} %pad_maximum_fusion), channel_id=1, source_target_pairs={{0,24},{4,44},{8,32},{12,52},{16,40},{20,60},{24,48},{28,4},{32,56... | collective-permute-start | bytes 393224 | tf_op jit(solution)/shard_map/ppermute | solution.py:300
  67.4 4.2 %collective-permute-start.7 = (bf16[32,1024]{1,0:T(8,128)(2,1)S(1)}, bf16[32,1024]{1,0:T(8,128)(2,1)S(1)}, u32[]{:S(2)}, u32[]{:S(2)}) collective-permute-start(bf16[32,1024]{1,0:T(8,128)(2,1)S(1)} %bitcast.35), channel_id=1, source_target_pairs={{0,32},{8,40},{16,48},{24,56},{32,0},{40,8},{48,16},{56,24},{1,33}... | collective-permute-start | bytes 196616 | tf_op jit(solution)/shard_map/ppermute | solution.py:294
  71.6 6.9 %collective-permute-done.7.refs_3_ = bf16[32,1024]{1,0:T(8,128)(2,1)S(1)} collective-permute-done((bf16[32,1024]{1,0:T(8,128)(2,1)S(1)}, bf16[32,1024]{1,0:T(8,128)(2,1)S(1)}, u32[]{:S(2)}, u32[]{:S(2)}) %collective-permute-start.7) | collective-permute-done | bytes 65568 | tf_op jit(solution)/shard_map/ppermute | solution.py:294
  78.6 1.9 %collective-permute-start.8 = (bf16[7,32,1024]{2,1,0:T(8,128)(2,1)S(1)}, bf16[7,32,1024]{2,1,0:T(8,128)(2,1)S(1)}, u32[]{:S(2)}, u32[]{:S(2)}) collective-permute-start(bf16[7,32,1024]{2,1,0:T(8,128)(2,1)S(1)} %weight_rows.1.near_ref), channel_id=1, source_target_pairs={{0,4},{4,0},{1,5},{5,1},{2,6},{6,2},{3,7},{7,3},{8,12},{12,8},{9,1... | collective-permute-start | bytes 1376264 | tf_op jit(solution)/shard_map/ppermute | solution.py:289
  80.5 1.8 %collective-permute-done.8.far_ref = bf16[7,32,1024]{2,1,0:T(8,128)(2,1)S(1)} collective-permute-done((bf16[7,32,1024]{2,1,0:T(8,128)(2,1)S(1)}, bf16[7,32,1024]{2,1,0:T(8,128)(2,1)S(1)}, u32[]{:S(2)}, u32[]{:S(2)}) %collective-permute-start.8) | collective-permute-done | bytes 458784 | tf_op jit(solution)/shard_map/ppermute | solution.py:289
  82.3 0.0 all-to-all-done.1
  82.3 0.6 projection.1
  82.9 0.0 copy-start.3
  82.9 23.2 %all_to_all.20 = bf16[32,8,512]{2,1,0:T(8,128)(2,1)S(1)} all-to-all(bf16[32,8,512]{2,1,0:T(8,128)(2,1)S(1)} %bitcast.27), channel_id=1, replica_groups=mesh['z'=8,'y'=8,'core'=2,'section'=4] {'z','section'}, dimensions={0} | all-to-all | bytes 524288 | tf_op jit(solution)/shard_map/all_to_all | solution.py:275
  106.1 0.4 norm_terms.1
  106.5 9.3 %all_to_all.21 = bf16[4,8,4096]{2,1,0:T(8,128)(2,1)S(1)} all-to-all(bf16[4,8,4096]{2,1,0:T(8,128)(2,1)S(1)} %bitcast.29), channel_id=1, replica_groups=mesh['z'=8,'y'=8,'core'=2,'section'=4] {'section'}, dimensions={0} | all-to-all | bytes 524288 | tf_op jit(solution)/shard_map/all_to_all | solution.py:284
  115.9 0.8 fusion.1
  (14 shorter events, 0.1 us)
Async XLA Ops:
  7.7 17.4 %copy-start.1 = (bf16[1,32,1024]{2,1,0:T(8,128)(2,1)S(1)}, bf16[1,32,1024]{2,1,0:T(8,128)(2,1)}, u32[]{:S(2)}) copy-start(bf16[1,32,1024]{2,1,0:T(8,128)(2,1)} %param.17) | copy-start | bytes 196612
  7.8 19.5 %copy-start = (bf16[1,32,4096]{2,1,0:T(8,128)(2,1)S(1)}, bf16[1,32,4096]{2,1,0:T(8,128)(2,1)}, u32[]{:S(2)}) copy-start(bf16[1,32,4096]{2,1,0:T(8,128)(2,1)} %param.15) | copy-start | bytes 786436
  7.8 39.0 %copy-start.4 = (s32[512]{0:T(512)S(1)}, s32[512]{0:T(512)}, u32[]{:S(2)}) copy-start(s32[512]{0:T(512)} %groups.1) | copy-start | bytes 6148
  7.8 48.5 %all-to-all-start = ((bf16[128,8,512]{2,1,0:T(8,128)(2,1)}), bf16[128,8,512]{2,1,0:T(8,128)(2,1)S(1)}, u32[]{:S(2)}, u32[]{:S(2)}) async-start(bf16[128,8,512]{2,1,0:T(8,128)(2,1)} %bitcast.40), calls=%async_computation | async-start | bytes 2097152 | tf_op jit(solution)/shard_map/all_to_all | solution.py:329
  25.2 5.5 %collective-permute-start = (bf16[32,1024]{1,0:T(8,128)(2,1)S(1)}, bf16[32,1024]{1,0:T(8,128)(2,1)S(1)}, u32[]{:S(2)}, u32[]{:S(2)}) collective-permute-start(bf16[32,1024]{1,0:T(8,128)(2,1)S(1)} %bitcast.33), channel_id=1, source_target_pairs={{0,4},{4,0},{1,5},{5,1},{2,6},{6,2},{3,7},{7,3},{8,12},{12,8},{9,1... | collective-permute-start | bytes 196616 | tf_op jit(solution)/shard_map/ppermute | solution.py:289
  27.3 24.0 %collective-permute-start.3 = (bf16[8,4096]{1,0:T(8,128)(2,1)S(1)}, bf16[8,4096]{1,0:T(8,128)(2,1)S(1)}, u32[]{:S(2)}, u32[]{:S(2)}) collective-permute-start(bf16[8,4096]{1,0:T(8,128)(2,1)S(1)} %dynamic-slice_bitcast_fusion.2), channel_id=1, source_target_pairs={{0,1},{1,2},{2,3},{3,0},{4,5},{5,6},{6,7},{7,4},{8,9},{9,10},{10,1... | collective-permute-start | bytes 196616 | tf_op jit(solution)/shard_map/ppermute | solution.py:294
  30.8 20.6 %collective-permute-start.1 = (bf16[64,1024]{1,0:T(8,128)(2,1)S(1)}, bf16[64,1024]{1,0:T(8,128)(2,1)S(1)}, u32[]{:S(2)}, u32[]{:S(2)}) collective-permute-start(bf16[64,1024]{1,0:T(8,128)(2,1)S(1)} %pad_maximum_fusion), channel_id=1, source_target_pairs={{0,8},{4,60},{8,16},{12,4},{16,24},{20,12},{24,32},{28,20},{32,40}... | collective-permute-start | bytes 393224 | tf_op jit(solution)/shard_map/ppermute | solution.py:300
  34.1 17.2 %collective-permute-start.2 = (bf16[64,1024]{1,0:T(8,128)(2,1)S(1)}, bf16[64,1024]{1,0:T(8,128)(2,1)S(1)}, u32[]{:S(2)}, u32[]{:S(2)}) collective-permute-start(bf16[64,1024]{1,0:T(8,128)(2,1)S(1)} %pad_maximum_fusion), channel_id=1, source_target_pairs={{0,16},{4,52},{8,24},{12,60},{16,32},{20,4},{24,40},{28,12},{32,48... | collective-permute-start | bytes 393224 | tf_op jit(solution)/shard_map/ppermute | solution.py:300
  38.8 12.5 %collective-permute-start.4 = (bf16[8,4096]{1,0:T(8,128)(2,1)S(1)}, bf16[8,4096]{1,0:T(8,128)(2,1)S(1)}, u32[]{:S(2)}, u32[]{:S(2)}) collective-permute-start(bf16[8,4096]{1,0:T(8,128)(2,1)S(1)} %get-tuple-element.40), channel_id=1, source_target_pairs={{0,2},{1,3},{2,0},{3,1},{4,6},{5,7},{6,4},{7,5},{8,10},{9,11},{10,... | collective-permute-start | bytes 196616 | tf_op jit(solution)/shard_map/ppermute | solution.py:294
  43.4 7.9 %collective-permute-start.5 = (bf16[8,4096]{1,0:T(8,128)(2,1)S(1)}, bf16[8,4096]{1,0:T(8,128)(2,1)S(1)}, u32[]{:S(2)}, u32[]{:S(2)}) collective-permute-start(bf16[8,4096]{1,0:T(8,128)(2,1)S(1)} %get-tuple-element.39), channel_id=1, source_target_pairs={{0,3},{1,0},{2,1},{3,2},{4,7},{5,4},{6,5},{7,6},{8,11},{9,8},{10,9... | collective-permute-start | bytes 196616 | tf_op jit(solution)/shard_map/ppermute | solution.py:294
  57.4 24.9 %copy-start.2 = (bf16[1,4096]{1,0:T(2,128)(2,1)S(1)}, bf16[1,4096]{1,0:T(2,128)(2,1)}, u32[]{:S(2)}) copy-start(bf16[1,4096]{1,0:T(2,128)(2,1)} %gain_ref.1) | copy-start | bytes 24580
  57.4 24.9 %all-to-all-start.1 = ((bf16[8,32,1024]{2,1,0:T(8,128)(2,1)}), bf16[8,32,1024]{2,1,0:T(8,128)(2,1)S(1)}, u32[]{:S(2)}, u32[]{:S(2)}) async-start(bf16[8,32,1024]{2,1,0:T(8,128)(2,1)} %page_sum.1), calls=%async_computation.1 | async-start | bytes 1048576 | tf_op jit(solution)/shard_map/all_to_all | solution.py:346
  61.0 17.5 %collective-permute-start.6 = (bf16[64,1024]{1,0:T(8,128)(2,1)S(1)}, bf16[64,1024]{1,0:T(8,128)(2,1)S(1)}, u32[]{:S(2)}, u32[]{:S(2)}) collective-permute-start(bf16[64,1024]{1,0:T(8,128)(2,1)S(1)} %pad_maximum_fusion), channel_id=1, source_target_pairs={{0,24},{4,44},{8,32},{12,52},{16,40},{20,60},{24,48},{28,4},{32,56... | collective-permute-start | bytes 393224 | tf_op jit(solution)/shard_map/ppermute | solution.py:300
  67.4 11.1 %collective-permute-start.7 = (bf16[32,1024]{1,0:T(8,128)(2,1)S(1)}, bf16[32,1024]{1,0:T(8,128)(2,1)S(1)}, u32[]{:S(2)}, u32[]{:S(2)}) collective-permute-start(bf16[32,1024]{1,0:T(8,128)(2,1)S(1)} %bitcast.35), channel_id=1, source_target_pairs={{0,32},{8,40},{16,48},{24,56},{32,0},{40,8},{48,16},{56,24},{1,33}... | collective-permute-start | bytes 196616 | tf_op jit(solution)/shard_map/ppermute | solution.py:294
  78.6 3.7 %collective-permute-start.8 = (bf16[7,32,1024]{2,1,0:T(8,128)(2,1)S(1)}, bf16[7,32,1024]{2,1,0:T(8,128)(2,1)S(1)}, u32[]{:S(2)}, u32[]{:S(2)}) collective-permute-start(bf16[7,32,1024]{2,1,0:T(8,128)(2,1)S(1)} %weight_rows.1.near_ref), channel_id=1, source_target_pairs={{0,4},{4,0},{1,5},{5,1},{2,6},{6,2},{3,7},{7,3},{8,12},{12,8},{9,1... | collective-permute-start | bytes 1376264 | tf_op jit(solution)/shard_map/ppermute | solution.py:289
  82.9 33.0 %copy-start.3 = (bf16[32,4096]{1,0:T(8,128)(2,1)S(1)}, bf16[32,4096]{1,0:T(8,128)(2,1)}, u32[]{:S(2)}) copy-start(bf16[32,4096]{1,0:T(8,128)(2,1)} %param.18) | copy-start | bytes 786436

commit v6 on v5

--- a/solution.py
+++ b/solution.py
@@ -79,12 +79,17 @@
     for k, half, at, grad in grads:
         down_ref[:, at] = grad[plen:].astype(BF16)
         part = dot(place, grad[:plen].astype(BF16), ((1,), (0,)))
-        mixed_ref[k, pl.ds(2 * b + half, devices, stride=2 * count), :] = part
+        mixed_ref[2 * b + half, :, k * HD : (k + 1) * HD] = part.astype(BF16)
 
     @pl.when(b == count - 1)
     def _():
-        for k in range(KVH):
-            send_ref[:, k * HD : (k + 1) * HD] = mixed_ref[k].astype(BF16)
+        slots, step = 2 * count, 16
+        size = slots * step
+        row = lax.broadcasted_iota(jnp.int32, (size, size), 0)
+        order = (lax.broadcasted_iota(jnp.int32, (size, size), 1) == row % slots * step + row // slots).astype(BF16)
+        for start in range(0, devices, step):
+            block = mixed_ref[:, start : start + step, :].reshape(size, mixed_ref.shape[2])
+            send_ref[start * slots : start * slots + size, :] = dot(order, block, ((1,), (0,))).astype(BF16)
 
 
 def attention(queries, out_grad, resp_kv, prompt_kv, group_list, lengths, owner_map):
@@ -111,7 +116,7 @@
                 by_resp(WIDE),
                 pl.BlockSpec((2 * count * plen, WIDE // 2), lambda b, *_: (0, 0)),
             ],
-            scratch_shapes=[pltpu.VMEM((KVH, 2 * count * plen, HD), F32)],
+            scratch_shapes=[pltpu.VMEM((2 * count, plen, WIDE // 2), BF16)],
         ),
         out_shape=[
             jax.ShapeDtypeStruct((count * KVH, keys, lanes), BF16),

time: 117 us -> 118 us (level)
  no operation moved by 1% of the time
where the time goes in v6:
time: 118 us; the launch traced here: 117 us
  starting transfers between devices  55 us (47%)
  blocking collectives  32.5 us (28%)
  Pallas kernels  13.7 us (12%)
  waiting for transfers between devices  13.6 us (12%)
    all_to_all x1, blocking collectives, finish(): lax.all_to_all(scaled, ('z', 'section'), split_axis=0, concat_axis=0, til...  23.2 us
    all_to_all x1, starting transfers between devices, body(): lax.all_to_all(outgoing, RESP_AXES, split_axis=0, concat_axis=0, tiled=True)  17.4 us
    ppermute x4, starting transfers between devices, turn(): return lax.ppermute(piece, axis, [(i, (i + k) % size) for i in range(size)])  15.6 us
    ppermute x3, starting transfers between devices, part_ways(): return lax.ppermute(piece, ('y', 'core'), pairs)  14.4 us
    all_to_all x1, blocking collectives, finish(): lax.all_to_all(sums.reshape(sections, quarter, width), 'section', split_a...  9.33 us
    pallas_call x1, Pallas kernels, attention(): pl.pallas_call(attention_kernel, grid_spec=pltpu.PrefetchScalarGridSpec(n...  7.34 us
    ppermute x4, waiting for transfers between devices, turn(): return lax.ppermute(piece, axis, [(i, (i + k) % size) for i in range(size)])  6.91 us
    all_to_all x1, waiting for transfers between devices, body(): lax.all_to_all(outgoing, RESP_AXES, split_axis=0, concat_axis=0, tiled=True)  4.92 us
  transfers between devices with their start and end apart: 11, of which 3 were waited for; matrix products, arithmetic and copies ran while one was open for 0% of the time, Pallas kernels for 4%

profile of v6, /device:TPU:16, one launch (start us, length us, event | category | flops | bytes accessed | tf_op | source)
XLA Modules:
  0.0 116.9 jit_solution(12566963490604944836)
XLA Ops:
  0.6 7.3 %attention_backward.1 = (bf16[16,160,256]{2,1,0:T(8,128)(2,1)}, bf16[128,1024]{1,0:T(8,128)(2,1)}, bf16[1024,512]{1,0:T(8,128)(2,1)}) custom-call(s32[512]{0:T(512)} %groups.1, s32[4]{0:T(128)} %lengths.1, bf16[128,4096]{1,0:T(8,128)(2,1)} %bitcast.43, bf16[128,4096]{1,0:T(8,128)(2,1)} %bitcast.44, bf16[128,1024]{1,0:T(8,128)(2,1)} %bitcast.41, ...), custom_call_target="tpu_custom_call" | custom-call | flops 1000000000 | bytes 6000000 | tf_op jit(solution)/shard_map/attention_backward/pallas_call | solution.py:102
  8.0 0.0 copy-start.1
  8.0 0.0 copy-start
  8.0 0.0 copy-start.4
  8.0 17.4 %all-to-all-start = ((bf16[128,8,512]{2,1,0:T(8,128)(2,1)}), bf16[128,8,512]{2,1,0:T(8,128)(2,1)S(1)}, u32[]{:S(2)}, u32[]{:S(2)}) async-start(bf16[128,8,512]{2,1,0:T(8,128)(2,1)} %bitcast.40), calls=%async_computation | async-start | bytes 2097152 | tf_op jit(solution)/shard_map/all_to_all | solution.py:334
  25.4 2.1 %collective-permute-start = (bf16[32,1024]{1,0:T(8,128)(2,1)S(1)}, bf16[32,1024]{1,0:T(8,128)(2,1)S(1)}, u32[]{:S(2)}, u32[]{:S(2)}) collective-permute-start(bf16[32,1024]{1,0:T(8,128)(2,1)S(1)} %bitcast.33), channel_id=1, source_target_pairs={{0,4},{4,0},{1,5},{5,1},{2,6},{6,2},{3,7},{7,3},{8,12},{12,8},{9,1... | collective-permute-start | bytes 196616 | tf_op jit(solution)/shard_map/ppermute | solution.py:294
  27.5 3.4 %collective-permute-start.3 = (bf16[8,4096]{1,0:T(8,128)(2,1)S(1)}, bf16[8,4096]{1,0:T(8,128)(2,1)S(1)}, u32[]{:S(2)}, u32[]{:S(2)}) collective-permute-start(bf16[8,4096]{1,0:T(8,128)(2,1)S(1)} %dynamic-slice_bitcast_fusion.2), channel_id=1, source_target_pairs={{0,1},{1,2},{2,3},{3,0},{4,5},{5,6},{6,7},{7,4},{8,9},{9,10},{10,1... | collective-permute-start | bytes 196616 | tf_op jit(solution)/shard_map/ppermute | solution.py:299
  31.0 0.0 collective-permute-done.sibling_ref
  31.0 3.4 %collective-permute-start.1 = (bf16[64,1024]{1,0:T(8,128)(2,1)S(1)}, bf16[64,1024]{1,0:T(8,128)(2,1)S(1)}, u32[]{:S(2)}, u32[]{:S(2)}) collective-permute-start(bf16[64,1024]{1,0:T(8,128)(2,1)S(1)} %pad_maximum_fusion), channel_id=1, source_target_pairs={{0,8},{4,60},{8,16},{12,4},{16,24},{20,12},{24,32},{28,20},{32,40}... | collective-permute-start | bytes 393224 | tf_op jit(solution)/shard_map/ppermute | solution.py:305
  34.4 4.6 %collective-permute-start.2 = (bf16[64,1024]{1,0:T(8,128)(2,1)S(1)}, bf16[64,1024]{1,0:T(8,128)(2,1)S(1)}, u32[]{:S(2)}, u32[]{:S(2)}) collective-permute-start(bf16[64,1024]{1,0:T(8,128)(2,1)S(1)} %pad_maximum_fusion), channel_id=1, source_target_pairs={{0,16},{4,52},{8,24},{12,60},{16,32},{20,4},{24,40},{28,12},{32,48... | collective-permute-start | bytes 393224 | tf_op jit(solution)/shard_map/ppermute | solution.py:305
  39.0 4.6 %collective-permute-start.4 = (bf16[8,4096]{1,0:T(8,128)(2,1)S(1)}, bf16[8,4096]{1,0:T(8,128)(2,1)S(1)}, u32[]{:S(2)}, u32[]{:S(2)}) collective-permute-start(bf16[8,4096]{1,0:T(8,128)(2,1)S(1)} %get-tuple-element.40), channel_id=1, source_target_pairs={{0,2},{1,3},{2,0},{3,1},{4,6},{5,7},{6,4},{7,5},{8,10},{9,11},{10,... | collective-permute-start | bytes 196616 | tf_op jit(solution)/shard_map/ppermute | solution.py:299
  43.6 3.3 %collective-permute-start.5 = (bf16[8,4096]{1,0:T(8,128)(2,1)S(1)}, bf16[8,4096]{1,0:T(8,128)(2,1)S(1)}, u32[]{:S(2)}, u32[]{:S(2)}) collective-permute-start(bf16[8,4096]{1,0:T(8,128)(2,1)S(1)} %get-tuple-element.39), channel_id=1, source_target_pairs={{0,3},{1,0},{2,1},{3,2},{4,7},{5,4},{6,5},{7,6},{8,11},{9,8},{10,9... | collective-permute-start | bytes 196616 | tf_op jit(solution)/shard_map/ppermute | solution.py:299
  47.0 0.1 broadcast_in_dim.14
  47.1 0.2 broadcast_in_dim_reshape.3.groups_ref
  47.3 4.2 %query_gradient.1 = bf16[128,4096]{1,0:T(8,128)(2,1)} custom-call(bf16[16,160,256]{2,1,0:T(8,128)(2,1)} %get-tuple-element.27.grad_ref, bf16[128,1024]{1,0:T(8,128)(2,1)} %bitcast.42, bf16[4,128,1024]{2,1,0:T(8,128)(2,1)} %bitcast.38), custom_call_target="tpu_custom_call" | custom-call | flops 200000000 | bytes 4000000 | tf_op jit(solution)/shard_map/query_gradient/pallas_call | solution.py:147
  51.5 0.0 collective-permute-done.5.refs_2_
  51.5 0.0 collective-permute-done.1.refs_0_
  51.6 4.9 %all-to-all-done = bf16[128,8,512]{2,1,0:T(8,128)(2,1)S(1)} async-done(((bf16[128,8,512]{2,1,0:T(8,128)(2,1)}), bf16[128,8,512]{2,1,0:T(8,128)(2,1)S(1)}, u32[]{:S(2)}, u32[]{:S(2)}) %all-to-all-start) | async-done | bytes 1048608 | tf_op jit(solution)/shard_map/all_to_all | solution.py:334
  56.5 1.1 page_sum.1
  57.6 3.6 %all-to-all-start.1 = ((bf16[8,32,1024]{2,1,0:T(8,128)(2,1)}), bf16[8,32,1024]{2,1,0:T(8,128)(2,1)S(1)}, u32[]{:S(2)}, u32[]{:S(2)}) async-start(bf16[8,32,1024]{2,1,0:T(8,128)(2,1)} %page_sum.1), calls=%async_computation.1 | async-start | bytes 1048576 | tf_op jit(solution)/shard_map/all_to_all | solution.py:351
  61.2 6.4 %collective-permute-start.6 = (bf16[64,1024]{1,0:T(8,128)(2,1)S(1)}, bf16[64,1024]{1,0:T(8,128)(2,1)S(1)}, u32[]{:S(2)}, u32[]{:S(2)}) collective-permute-start(bf16[64,1024]{1,0:T(8,128)(2,1)S(1)} %pad_maximum_fusion), channel_id=1, source_target_pairs={{0,24},{4,44},{8,32},{12,52},{16,40},{20,60},{24,48},{28,4},{32,56... | collective-permute-start | bytes 393224 | tf_op jit(solution)/shard_map/ppermute | solution.py:305
  67.7 4.2 %collective-permute-start.7 = (bf16[32,1024]{1,0:T(8,128)(2,1)S(1)}, bf16[32,1024]{1,0:T(8,128)(2,1)S(1)}, u32[]{:S(2)}, u32[]{:S(2)}) collective-permute-start(bf16[32,1024]{1,0:T(8,128)(2,1)S(1)} %bitcast.35), channel_id=1, source_target_pairs={{0,32},{8,40},{16,48},{24,56},{32,0},{40,8},{48,16},{56,24},{1,33}... | collective-permute-start | bytes 196616 | tf_op jit(solution)/shard_map/ppermute | solution.py:299
  71.9 6.9 %collective-permute-done.7.refs_3_ = bf16[32,1024]{1,0:T(8,128)(2,1)S(1)} collective-permute-done((bf16[32,1024]{1,0:T(8,128)(2,1)S(1)}, bf16[32,1024]{1,0:T(8,128)(2,1)S(1)}, u32[]{:S(2)}, u32[]{:S(2)}) %collective-permute-start.7) | collective-permute-done | bytes 65568 | tf_op jit(solution)/shard_map/ppermute | solution.py:299
  78.8 1.9 %collective-permute-start.8 = (bf16[7,32,1024]{2,1,0:T(8,128)(2,1)S(1)}, bf16[7,32,1024]{2,1,0:T(8,128)(2,1)S(1)}, u32[]{:S(2)}, u32[]{:S(2)}) collective-permute-start(bf16[7,32,1024]{2,1,0:T(8,128)(2,1)S(1)} %weight_rows.1.near_ref), channel_id=1, source_target_pairs={{0,4},{4,0},{1,5},{5,1},{2,6},{6,2},{3,7},{7,3},{8,12},{12,8},{9,1... | collective-permute-start | bytes 1376264 | tf_op jit(solution)/shard_map/ppermute | solution.py:294
  80.7 1.8 %collective-permute-done.8.far_ref = bf16[7,32,1024]{2,1,0:T(8,128)(2,1)S(1)} collective-permute-done((bf16[7,32,1024]{2,1,0:T(8,128)(2,1)S(1)}, bf16[7,32,1024]{2,1,0:T(8,128)(2,1)S(1)}, u32[]{:S(2)}, u32[]{:S(2)}) %collective-permute-start.8) | collective-permute-done | bytes 458784 | tf_op jit(solution)/shard_map/ppermute | solution.py:294
  82.5 0.0 all-to-all-done.1
  82.5 0.6 projection.1
  83.1 0.0 copy-start.3
  83.1 23.2 %all_to_all.20 = bf16[32,8,512]{2,1,0:T(8,128)(2,1)S(1)} all-to-all(bf16[32,8,512]{2,1,0:T(8,128)(2,1)S(1)} %bitcast.27), channel_id=1, replica_groups=mesh['z'=8,'y'=8,'core'=2,'section'=4] {'z','section'}, dimensions={0} | all-to-all | bytes 524288 | tf_op jit(solution)/shard_map/all_to_all | solution.py:280
  106.3 0.4 norm_terms.1
  106.8 9.3 %all_to_all.21 = bf16[4,8,4096]{2,1,0:T(8,128)(2,1)S(1)} all-to-all(bf16[4,8,4096]{2,1,0:T(8,128)(2,1)S(1)} %bitcast.29), channel_id=1, replica_groups=mesh['z'=8,'y'=8,'core'=2,'section'=4] {'section'}, dimensions={0} | all-to-all | bytes 524288 | tf_op jit(solution)/shard_map/all_to_all | solution.py:289
  116.1 0.8 fusion.1
  (14 shorter events, 0.1 us)
Async XLA Ops:
  8.0 17.4 %copy-start.1 = (bf16[1,32,1024]{2,1,0:T(8,128)(2,1)S(1)}, bf16[1,32,1024]{2,1,0:T(8,128)(2,1)}, u32[]{:S(2)}) copy-start(bf16[1,32,1024]{2,1,0:T(8,128)(2,1)} %param.17) | copy-start | bytes 196612
  8.0 19.5 %copy-start = (bf16[1,32,4096]{2,1,0:T(8,128)(2,1)S(1)}, bf16[1,32,4096]{2,1,0:T(8,128)(2,1)}, u32[]{:S(2)}) copy-start(bf16[1,32,4096]{2,1,0:T(8,128)(2,1)} %param.15) | copy-start | bytes 786436
  8.0 39.0 %copy-start.4 = (s32[512]{0:T(512)S(1)}, s32[512]{0:T(512)}, u32[]{:S(2)}) copy-start(s32[512]{0:T(512)} %groups.1) | copy-start | bytes 6148
  8.0 48.5 %all-to-all-start = ((bf16[128,8,512]{2,1,0:T(8,128)(2,1)}), bf16[128,8,512]{2,1,0:T(8,128)(2,1)S(1)}, u32[]{:S(2)}, u32[]{:S(2)}) async-start(bf16[128,8,512]{2,1,0:T(8,128)(2,1)} %bitcast.40), calls=%async_computation | async-start | bytes 2097152 | tf_op jit(solution)/shard_map/all_to_all | solution.py:334
  25.4 5.5 %collective-permute-start = (bf16[32,1024]{1,0:T(8,128)(2,1)S(1)}, bf16[32,1024]{1,0:T(8,128)(2,1)S(1)}, u32[]{:S(2)}, u32[]{:S(2)}) collective-permute-start(bf16[32,1024]{1,0:T(8,128)(2,1)S(1)} %bitcast.33), channel_id=1, source_target_pairs={{0,4},{4,0},{1,5},{5,1},{2,6},{6,2},{3,7},{7,3},{8,12},{12,8},{9,1... | collective-permute-start | bytes 196616 | tf_op jit(solution)/shard_map/ppermute | solution.py:294
  27.5 24.0 %collective-permute-start.3 = (bf16[8,4096]{1,0:T(8,128)(2,1)S(1)}, bf16[8,4096]{1,0:T(8,128)(2,1)S(1)}, u32[]{:S(2)}, u32[]{:S(2)}) collective-permute-start(bf16[8,4096]{1,0:T(8,128)(2,1)S(1)} %dynamic-slice_bitcast_fusion.2), channel_id=1, source_target_pairs={{0,1},{1,2},{2,3},{3,0},{4,5},{5,6},{6,7},{7,4},{8,9},{9,10},{10,1... | collective-permute-start | bytes 196616 | tf_op jit(solution)/shard_map/ppermute | solution.py:299
  31.0 20.5 %collective-permute-start.1 = (bf16[64,1024]{1,0:T(8,128)(2,1)S(1)}, bf16[64,1024]{1,0:T(8,128)(2,1)S(1)}, u32[]{:S(2)}, u32[]{:S(2)}) collective-permute-start(bf16[64,1024]{1,0:T(8,128)(2,1)S(1)} %pad_maximum_fusion), channel_id=1, source_target_pairs={{0,8},{4,60},{8,16},{12,4},{16,24},{20,12},{24,32},{28,20},{32,40}... | collective-permute-start | bytes 393224 | tf_op jit(solution)/shard_map/ppermute | solution.py:305
  34.4 17.2 %collective-permute-start.2 = (bf16[64,1024]{1,0:T(8,128)(2,1)S(1)}, bf16[64,1024]{1,0:T(8,128)(2,1)S(1)}, u32[]{:S(2)}, u32[]{:S(2)}) collective-permute-start(bf16[64,1024]{1,0:T(8,128)(2,1)S(1)} %pad_maximum_fusion), channel_id=1, source_target_pairs={{0,16},{4,52},{8,24},{12,60},{16,32},{20,4},{24,40},{28,12},{32,48... | collective-permute-start | bytes 393224 | tf_op jit(solution)/shard_map/ppermute | solution.py:305
  39.0 12.5 %collective-permute-start.4 = (bf16[8,4096]{1,0:T(8,128)(2,1)S(1)}, bf16[8,4096]{1,0:T(8,128)(2,1)S(1)}, u32[]{:S(2)}, u32[]{:S(2)}) collective-permute-start(bf16[8,4096]{1,0:T(8,128)(2,1)S(1)} %get-tuple-element.40), channel_id=1, source_target_pairs={{0,2},{1,3},{2,0},{3,1},{4,6},{5,7},{6,4},{7,5},{8,10},{9,11},{10,... | collective-permute-start | bytes 196616 | tf_op jit(solution)/shard_map/ppermute | solution.py:299
  43.6 7.9 %collective-permute-start.5 = (bf16[8,4096]{1,0:T(8,128)(2,1)S(1)}, bf16[8,4096]{1,0:T(8,128)(2,1)S(1)}, u32[]{:S(2)}, u32[]{:S(2)}) collective-permute-start(bf16[8,4096]{1,0:T(8,128)(2,1)S(1)} %get-tuple-element.39), channel_id=1, source_target_pairs={{0,3},{1,0},{2,1},{3,2},{4,7},{5,4},{6,5},{7,6},{8,11},{9,8},{10,9... | collective-permute-start | bytes 196616 | tf_op jit(solution)/shard_map/ppermute | solution.py:299
  57.6 24.9 %copy-start.2 = (bf16[1,4096]{1,0:T(2,128)(2,1)S(1)}, bf16[1,4096]{1,0:T(2,128)(2,1)}, u32[]{:S(2)}) copy-start(bf16[1,4096]{1,0:T(2,128)(2,1)} %gain_ref.1) | copy-start | bytes 24580
  57.6 24.9 %all-to-all-start.1 = ((bf16[8,32,1024]{2,1,0:T(8,128)(2,1)}), bf16[8,32,1024]{2,1,0:T(8,128)(2,1)S(1)}, u32[]{:S(2)}, u32[]{:S(2)}) async-start(bf16[8,32,1024]{2,1,0:T(8,128)(2,1)} %page_sum.1), calls=%async_computation.1 | async-start | bytes 1048576 | tf_op jit(solution)/shard_map/all_to_all | solution.py:351
  61.2 17.5 %collective-permute-start.6 = (bf16[64,1024]{1,0:T(8,128)(2,1)S(1)}, bf16[64,1024]{1,0:T(8,128)(2,1)S(1)}, u32[]{:S(2)}, u32[]{:S(2)}) collective-permute-start(bf16[64,1024]{1,0:T(8,128)(2,1)S(1)} %pad_maximum_fusion), channel_id=1, source_target_pairs={{0,24},{4,44},{8,32},{12,52},{16,40},{20,60},{24,48},{28,4},{32,56... | collective-permute-start | bytes 393224 | tf_op jit(solution)/shard_map/ppermute | solution.py:305
  67.7 11.1 %collective-permute-start.7 = (bf16[32,1024]{1,0:T(8,128)(2,1)S(1)}, bf16[32,1024]{1,0:T(8,128)(2,1)S(1)}, u32[]{:S(2)}, u32[]{:S(2)}) collective-permute-start(bf16[32,1024]{1,0:T(8,128)(2,1)S(1)} %bitcast.35), channel_id=1, source_target_pairs={{0,32},{8,40},{16,48},{24,56},{32,0},{40,8},{48,16},{56,24},{1,33}... | collective-permute-start | bytes 196616 | tf_op jit(solution)/shard_map/ppermute | solution.py:299
  78.8 3.7 %collective-permute-start.8 = (bf16[7,32,1024]{2,1,0:T(8,128)(2,1)S(1)}, bf16[7,32,1024]{2,1,0:T(8,128)(2,1)S(1)}, u32[]{:S(2)}, u32[]{:S(2)}) collective-permute-start(bf16[7,32,1024]{2,1,0:T(8,128)(2,1)S(1)} %weight_rows.1.near_ref), channel_id=1, source_target_pairs={{0,4},{4,0},{1,5},{5,1},{2,6},{6,2},{3,7},{7,3},{8,12},{12,8},{9,1... | collective-permute-start | bytes 1376264 | tf_op jit(solution)/shard_map/ppermute | solution.py:294
  83.1 33.0 %copy-start.3 = (bf16[32,4096]{1,0:T(8,128)(2,1)S(1)}, bf16[32,4096]{1,0:T(8,128)(2,1)}, u32[]{:S(2)}) copy-start(bf16[32,4096]{1,0:T(8,128)(2,1)} %param.18) | copy-start | bytes 786436

commit v7 on v5

--- a/solution.py
+++ b/solution.py
@@ -320,6 +320,7 @@
     prompt_count, devices = owner_map.shape
     sections = lax.axis_size("section")
     width = prompt_hidden.shape[-1]
+    middle = turn(kv_weight[0], "y", lax.axis_size("y") // 2)
     score_grad, own_out, outgoing = attention(
         queries[0], out_grad[0], resp_kv[0], prompt_kv[0], group_list, lengths, owner_map
     )
@@ -327,14 +328,13 @@
     outgoing, weight, hidden = lax.optimization_barrier((outgoing, kv_weight[0], hidden))
     outgoing = outgoing.reshape(devices, -1, WIDE // 2)
     incoming = lax.all_to_all(outgoing, RESP_AXES, split_axis=0, concat_axis=0, tiled=True)
-    layers = [hidden, hand_over(hidden, 1)]
     sibling = swap(weight)
     both, hidden = lax.optimization_barrier((jnp.concatenate([weight, sibling], axis=0), hidden))
     near = [part_ways(both, 1), part_ways(both, 2)]
-    layers += [hand_over(hidden, k) for k in range(2, sections)]
+    layers = [hidden] + [hand_over(hidden, k) for k in range(1, sections)]
     query_out = query_gradient(score_grad, resp_kv[0], prompt_kv[0])
-    incoming, both, near, layers, weight, query_out = lax.optimization_barrier(
-        (incoming, both, near, layers, weight, query_out)
+    incoming, both, near, layers, middle, query_out = lax.optimization_barrier(
+        (incoming, both, near, layers, middle, query_out)
     )
     pages = pl.pallas_call(
         page_kernel,
@@ -344,8 +344,7 @@
         name="page_sum",
     )(jnp.repeat(group_list, 2)[None, :], incoming.reshape(-1, WIDE // 2))
     pages = lax.all_to_all(pages, "z", split_axis=0, concat_axis=0, tiled=True)
-    near += [part_ways(both, 3), turn(weight, "y", lax.axis_size("y") // 2)]
-    near = collect(near, weight.shape[0])
+    near = collect(near + [part_ways(both, 3), middle], weight.shape[0])
     far = swap(near)
     prompt_out = finish(pages, [weight, sibling, near, far], layers, norm_gain, upper_grad)
     return (query_out[None], own_out[None], prompt_out[None])

time: 117 us -> 121 us (1.034)
  the two profiles are of different devices: /device:TPU:16 before, /device:TPU:8 now
where the time goes in v7:
time: 121 us; the launch traced here: 120 us
  starting transfers between devices  54.7 us (45%)
  blocking collectives  28.1 us (23%)
  waiting for transfers between devices  21.7 us (18%)
  Pallas kernels  13.5 us (11%)
    ppermute x4, starting transfers between devices, turn(): return lax.ppermute(piece, axis, [(i, (i + k) % size) for i in range(size)])  19.1 us
    all_to_all x1, blocking collectives, finish(): lax.all_to_all(scaled, ('z', 'section'), split_axis=0, concat_axis=0, til...  18.8 us
    all_to_all x1, starting transfers between devices, body(): lax.all_to_all(outgoing, RESP_AXES, split_axis=0, concat_axis=0, tiled=True)  17.5 us
    all_to_all x1, blocking collectives, finish(): lax.all_to_all(sums.reshape(sections, quarter, width), 'section', split_a...  9.33 us
    ppermute x3, waiting for transfers between devices, part_ways(): return lax.ppermute(piece, ('y', 'core'), pairs)  8.95 us
    ppermute x4, waiting for transfers between devices, turn(): return lax.ppermute(piece, axis, [(i, (i + k) % size) for i in range(size)])  8.65 us
    all_to_all x1, starting transfers between devices, body(): pages = lax.all_to_all(pages, 'z', split_axis=0, concat_axis=0, tiled=True)  7.14 us
    pallas_call x1, Pallas kernels, attention(): pl.pallas_call(attention_kernel, grid_spec=pltpu.PrefetchScalarGridSpec(n...  7.1 us
  transfers between devices with their start and end apart: 11, of which 4 were waited for; matrix products, arithmetic and copies ran while one was open for 0% of the time, Pallas kernels for 4%

profile of v7, /device:TPU:8, one launch (start us, length us, event | category | flops | bytes accessed | tf_op | source)
XLA Modules:
  0.0 120.0 jit_solution(7839224256720017145)
XLA Ops:
  0.6 7.1 %attention_backward.1 = (bf16[16,160,256]{2,1,0:T(8,128)(2,1)}, bf16[128,1024]{1,0:T(8,128)(2,1)}, bf16[1024,512]{1,0:T(8,128)(2,1)}) custom-call(s32[512]{0:T(512)} %groups.1, s32[4]{0:T(128)} %lengths.1, bf16[128,4096]{1,0:T(8,128)(2,1)} %bitcast.42, bf16[128,4096]{1,0:T(8,128)(2,1)} %bitcast.43, bf16[128,1024]{1,0:T(8,128)(2,1)} %bitcast.40, ...), custom_call_target="tpu_custom_call" | custom-call | flops 1000000000 | bytes 6000000 | tf_op jit(solution)/shard_map/attention_backward/pallas_call | solution.py:97
  7.7 0.0 copy-start.1
  7.8 0.0 copy-start
  7.8 0.0 copy-start.4
  7.8 17.5 %all-to-all-start = ((bf16[128,8,512]{2,1,0:T(8,128)(2,1)}), bf16[128,8,512]{2,1,0:T(8,128)(2,1)S(1)}, u32[]{:S(2)}, u32[]{:S(2)}) async-start(bf16[128,8,512]{2,1,0:T(8,128)(2,1)} %bitcast.39), calls=%async_computation | async-start | bytes 2097152 | tf_op jit(solution)/shard_map/all_to_all | solution.py:330
  25.3 2.1 %collective-permute-start = (bf16[32,1024]{1,0:T(8,128)(2,1)S(1)}, bf16[32,1024]{1,0:T(8,128)(2,1)S(1)}, u32[]{:S(2)}, u32[]{:S(2)}) collective-permute-start(bf16[32,1024]{1,0:T(8,128)(2,1)S(1)} %bitcast.32), channel_id=1, source_target_pairs={{0,4},{4,0},{1,5},{5,1},{2,6},{6,2},{3,7},{7,3},{8,12},{12,8},{9,1... | collective-permute-start | bytes 196616 | tf_op jit(solution)/shard_map/ppermute | solution.py:289
  27.4 6.4 %collective-permute-start.6 = (bf16[32,1024]{1,0:T(8,128)(2,1)S(1)}, bf16[32,1024]{1,0:T(8,128)(2,1)S(1)}, u32[]{:S(2)}, u32[]{:S(2)}) collective-permute-start(bf16[32,1024]{1,0:T(8,128)(2,1)S(1)} %bitcast.33), channel_id=1, source_target_pairs={{0,32},{8,40},{16,48},{24,56},{32,0},{40,8},{48,16},{56,24},{1,33}... | collective-permute-start | bytes 196616 | tf_op jit(solution)/shard_map/ppermute | solution.py:294
  33.8 2.5 %collective-permute-start.1 = (bf16[64,1024]{1,0:T(8,128)(2,1)S(1)}, bf16[64,1024]{1,0:T(8,128)(2,1)S(1)}, u32[]{:S(2)}, u32[]{:S(2)}) collective-permute-start(bf16[64,1024]{1,0:T(8,128)(2,1)S(1)} %pad_maximum_fusion), channel_id=1, source_target_pairs={{0,8},{4,60},{8,16},{12,4},{16,24},{20,12},{24,32},{28,20},{32,40}... | collective-permute-start | bytes 393224 | tf_op jit(solution)/shard_map/ppermute | solution.py:300
  36.3 2.6 %collective-permute-start.2 = (bf16[64,1024]{1,0:T(8,128)(2,1)S(1)}, bf16[64,1024]{1,0:T(8,128)(2,1)S(1)}, u32[]{:S(2)}, u32[]{:S(2)}) collective-permute-start(bf16[64,1024]{1,0:T(8,128)(2,1)S(1)} %pad_maximum_fusion), channel_id=1, source_target_pairs={{0,16},{4,52},{8,24},{12,60},{16,32},{20,4},{24,40},{28,12},{32,48... | collective-permute-start | bytes 393224 | tf_op jit(solution)/shard_map/ppermute | solution.py:300
  39.0 3.4 %collective-permute-start.3 = (bf16[8,4096]{1,0:T(8,128)(2,1)S(1)}, bf16[8,4096]{1,0:T(8,128)(2,1)S(1)}, u32[]{:S(2)}, u32[]{:S(2)}) collective-permute-start(bf16[8,4096]{1,0:T(8,128)(2,1)S(1)} %get-tuple-element.41), channel_id=1, source_target_pairs={{0,1},{1,2},{2,3},{3,0},{4,5},{5,6},{6,7},{7,4},{8,9},{9,10},{10,1... | collective-permute-start | bytes 196616 | tf_op jit(solution)/shard_map/ppermute | solution.py:294
  42.4 4.6 %collective-permute-start.4 = (bf16[8,4096]{1,0:T(8,128)(2,1)S(1)}, bf16[8,4096]{1,0:T(8,128)(2,1)S(1)}, u32[]{:S(2)}, u32[]{:S(2)}) collective-permute-start(bf16[8,4096]{1,0:T(8,128)(2,1)S(1)} %get-tuple-element.40), channel_id=1, source_target_pairs={{0,2},{1,3},{2,0},{3,1},{4,6},{5,7},{6,4},{7,5},{8,10},{9,11},{10,... | collective-permute-start | bytes 196616 | tf_op jit(solution)/shard_map/ppermute | solution.py:294
  47.1 8.6 %collective-permute-done.6.refs_3_ = bf16[32,1024]{1,0:T(8,128)(2,1)S(1)} collective-permute-done((bf16[32,1024]{1,0:T(8,128)(2,1)S(1)}, bf16[32,1024]{1,0:T(8,128)(2,1)S(1)}, u32[]{:S(2)}, u32[]{:S(2)}) %collective-permute-start.6) | collective-permute-done | bytes 65568 | tf_op jit(solution)/shard_map/ppermute | solution.py:294
  55.7 4.7 %collective-permute-start.5 = (bf16[8,4096]{1,0:T(8,128)(2,1)S(1)}, bf16[8,4096]{1,0:T(8,128)(2,1)S(1)}, u32[]{:S(2)}, u32[]{:S(2)}) collective-permute-start(bf16[8,4096]{1,0:T(8,128)(2,1)S(1)} %get-tuple-element.39), channel_id=1, source_target_pairs={{0,3},{1,0},{2,1},{3,2},{4,7},{5,4},{6,5},{7,6},{8,11},{9,8},{10,9... | collective-permute-start | bytes 196616 | tf_op jit(solution)/shard_map/ppermute | solution.py:294
  60.4 0.1 broadcast_in_dim.14
  60.5 0.2 broadcast_in_dim_reshape.3.groups_ref
  60.7 4.2 %query_gradient.1 = bf16[128,4096]{1,0:T(8,128)(2,1)} custom-call(bf16[16,160,256]{2,1,0:T(8,128)(2,1)} %get-tuple-element.27.grad_ref, bf16[128,1024]{1,0:T(8,128)(2,1)} %bitcast.41, bf16[4,128,1024]{2,1,0:T(8,128)(2,1)} %bitcast.37), custom_call_target="tpu_custom_call" | custom-call | flops 200000000 | bytes 4000000 | tf_op jit(solution)/shard_map/query_gradient/pallas_call | solution.py:142
  64.9 0.0 collective-permute-done.5.refs_2_
  64.9 0.0 collective-permute-done.1.refs_0_
  64.9 0.0 all-to-all-done
  64.9 1.1 page_sum.1
  66.1 7.1 %all-to-all-start.1 = ((bf16[8,32,1024]{2,1,0:T(8,128)(2,1)}), bf16[8,32,1024]{2,1,0:T(8,128)(2,1)S(1)}, u32[]{:S(2)}, u32[]{:S(2)}) async-start(bf16[8,32,1024]{2,1,0:T(8,128)(2,1)} %page_sum.1), calls=%async_computation.1 | async-start | bytes 1048576 | tf_op jit(solution)/shard_map/all_to_all | solution.py:346
  73.2 1.9 %collective-permute-start.7 = (bf16[64,1024]{1,0:T(8,128)(2,1)S(1)}, bf16[64,1024]{1,0:T(8,128)(2,1)S(1)}, u32[]{:S(2)}, u32[]{:S(2)}) collective-permute-start(bf16[64,1024]{1,0:T(8,128)(2,1)S(1)} %pad_maximum_fusion), channel_id=1, source_target_pairs={{0,24},{4,44},{8,32},{12,52},{16,40},{20,60},{24,48},{28,4},{32,56... | collective-permute-start | bytes 393224 | tf_op jit(solution)/shard_map/ppermute | solution.py:300
  75.1 8.9 %collective-permute-done.7.refs_2_ = bf16[64,1024]{1,0:T(8,128)(2,1)S(1)} collective-permute-done((bf16[64,1024]{1,0:T(8,128)(2,1)S(1)}, bf16[64,1024]{1,0:T(8,128)(2,1)S(1)}, u32[]{:S(2)}, u32[]{:S(2)}) %collective-permute-start.7) | collective-permute-done | bytes 131104 | tf_op jit(solution)/shard_map/ppermute | solution.py:300
  84.1 1.9 %collective-permute-start.8 = (bf16[7,32,1024]{2,1,0:T(8,128)(2,1)S(1)}, bf16[7,32,1024]{2,1,0:T(8,128)(2,1)S(1)}, u32[]{:S(2)}, u32[]{:S(2)}) collective-permute-start(bf16[7,32,1024]{2,1,0:T(8,128)(2,1)S(1)} %weight_rows.1.near_ref), channel_id=1, source_target_pairs={{0,4},{4,0},{1,5},{5,1},{2,6},{6,2},{3,7},{7,3},{8,12},{12,8},{9,1... | collective-permute-start | bytes 1376264 | tf_op jit(solution)/shard_map/ppermute | solution.py:289
  86.0 1.8 %collective-permute-done.8.far_ref = bf16[7,32,1024]{2,1,0:T(8,128)(2,1)S(1)} collective-permute-done((bf16[7,32,1024]{2,1,0:T(8,128)(2,1)S(1)}, bf16[7,32,1024]{2,1,0:T(8,128)(2,1)S(1)}, u32[]{:S(2)}, u32[]{:S(2)}) %collective-permute-start.8) | collective-permute-done | bytes 458784 | tf_op jit(solution)/shard_map/ppermute | solution.py:289
  87.8 2.3 %all-to-all-done.1 = bf16[8,32,1024]{2,1,0:T(8,128)(2,1)S(1)} async-done(((bf16[8,32,1024]{2,1,0:T(8,128)(2,1)}), bf16[8,32,1024]{2,1,0:T(8,128)(2,1)S(1)}, u32[]{:S(2)}, u32[]{:S(2)}) %all-to-all-start.1) | async-done | bytes 524320 | tf_op jit(solution)/shard_map/all_to_all | solution.py:346
  90.1 0.6 projection.1
  90.7 0.0 copy-start.3
  90.7 18.8 %all_to_all.20 = bf16[32,8,512]{2,1,0:T(8,128)(2,1)S(1)} all-to-all(bf16[32,8,512]{2,1,0:T(8,128)(2,1)S(1)} %bitcast.27), channel_id=1, replica_groups=mesh['z'=8,'y'=8,'core'=2,'section'=4] {'z','section'}, dimensions={0} | all-to-all | bytes 524288 | tf_op jit(solution)/shard_map/all_to_all | solution.py:275
  109.5 0.4 norm_terms.1
  109.9 9.3 %all_to_all.21 = bf16[4,8,4096]{2,1,0:T(8,128)(2,1)S(1)} all-to-all(bf16[4,8,4096]{2,1,0:T(8,128)(2,1)S(1)} %bitcast.29), channel_id=1, replica_groups=mesh['z'=8,'y'=8,'core'=2,'section'=4] {'section'}, dimensions={0} | all-to-all | bytes 524288 | tf_op jit(solution)/shard_map/all_to_all | solution.py:284
  119.3 0.8 fusion.1
  (13 shorter events, 0.1 us)
Async XLA Ops:
  7.7 17.6 %copy-start.1 = (bf16[1,32,1024]{2,1,0:T(8,128)(2,1)S(1)}, bf16[1,32,1024]{2,1,0:T(8,128)(2,1)}, u32[]{:S(2)}) copy-start(bf16[1,32,1024]{2,1,0:T(8,128)(2,1)} %param.17) | copy-start | bytes 196612
  7.8 31.2 %copy-start = (bf16[1,32,4096]{2,1,0:T(8,128)(2,1)S(1)}, bf16[1,32,4096]{2,1,0:T(8,128)(2,1)}, u32[]{:S(2)}) copy-start(bf16[1,32,4096]{2,1,0:T(8,128)(2,1)} %param.15) | copy-start | bytes 786436
  7.8 52.6 %copy-start.4 = (s32[512]{0:T(512)S(1)}, s32[512]{0:T(512)}, u32[]{:S(2)}) copy-start(s32[512]{0:T(512)} %groups.1) | copy-start | bytes 6148
  7.8 57.2 %all-to-all-start = ((bf16[128,8,512]{2,1,0:T(8,128)(2,1)}), bf16[128,8,512]{2,1,0:T(8,128)(2,1)S(1)}, u32[]{:S(2)}, u32[]{:S(2)}) async-start(bf16[128,8,512]{2,1,0:T(8,128)(2,1)} %bitcast.39), calls=%async_computation | async-start | bytes 2097152 | tf_op jit(solution)/shard_map/all_to_all | solution.py:330
  25.3 8.5 %collective-permute-start = (bf16[32,1024]{1,0:T(8,128)(2,1)S(1)}, bf16[32,1024]{1,0:T(8,128)(2,1)S(1)}, u32[]{:S(2)}, u32[]{:S(2)}) collective-permute-start(bf16[32,1024]{1,0:T(8,128)(2,1)S(1)} %bitcast.32), channel_id=1, source_target_pairs={{0,4},{4,0},{1,5},{5,1},{2,6},{6,2},{3,7},{7,3},{8,12},{12,8},{9,1... | collective-permute-start | bytes 196616 | tf_op jit(solution)/shard_map/ppermute | solution.py:289
  27.4 28.3 %collective-permute-start.6 = (bf16[32,1024]{1,0:T(8,128)(2,1)S(1)}, bf16[32,1024]{1,0:T(8,128)(2,1)S(1)}, u32[]{:S(2)}, u32[]{:S(2)}) collective-permute-start(bf16[32,1024]{1,0:T(8,128)(2,1)S(1)} %bitcast.33), channel_id=1, source_target_pairs={{0,32},{8,40},{16,48},{24,56},{32,0},{40,8},{48,16},{56,24},{1,33}... | collective-permute-start | bytes 196616 | tf_op jit(solution)/shard_map/ppermute | solution.py:294
  33.8 31.1 %collective-permute-start.1 = (bf16[64,1024]{1,0:T(8,128)(2,1)S(1)}, bf16[64,1024]{1,0:T(8,128)(2,1)S(1)}, u32[]{:S(2)}, u32[]{:S(2)}) collective-permute-start(bf16[64,1024]{1,0:T(8,128)(2,1)S(1)} %pad_maximum_fusion), channel_id=1, source_target_pairs={{0,8},{4,60},{8,16},{12,4},{16,24},{20,12},{24,32},{28,20},{32,40}... | collective-permute-start | bytes 393224 | tf_op jit(solution)/shard_map/ppermute | solution.py:300
  36.3 28.6 %collective-permute-start.2 = (bf16[64,1024]{1,0:T(8,128)(2,1)S(1)}, bf16[64,1024]{1,0:T(8,128)(2,1)S(1)}, u32[]{:S(2)}, u32[]{:S(2)}) collective-permute-start(bf16[64,1024]{1,0:T(8,128)(2,1)S(1)} %pad_maximum_fusion), channel_id=1, source_target_pairs={{0,16},{4,52},{8,24},{12,60},{16,32},{20,4},{24,40},{28,12},{32,48... | collective-permute-start | bytes 393224 | tf_op jit(solution)/shard_map/ppermute | solution.py:300
  39.0 25.9 %collective-permute-start.3 = (bf16[8,4096]{1,0:T(8,128)(2,1)S(1)}, bf16[8,4096]{1,0:T(8,128)(2,1)S(1)}, u32[]{:S(2)}, u32[]{:S(2)}) collective-permute-start(bf16[8,4096]{1,0:T(8,128)(2,1)S(1)} %get-tuple-element.41), channel_id=1, source_target_pairs={{0,1},{1,2},{2,3},{3,0},{4,5},{5,6},{6,7},{7,4},{8,9},{9,10},{10,1... | collective-permute-start | bytes 196616 | tf_op jit(solution)/shard_map/ppermute | solution.py:294
  42.4 22.5 %collective-permute-start.4 = (bf16[8,4096]{1,0:T(8,128)(2,1)S(1)}, bf16[8,4096]{1,0:T(8,128)(2,1)S(1)}, u32[]{:S(2)}, u32[]{:S(2)}) collective-permute-start(bf16[8,4096]{1,0:T(8,128)(2,1)S(1)} %get-tuple-element.40), channel_id=1, source_target_pairs={{0,2},{1,3},{2,0},{3,1},{4,6},{5,7},{6,4},{7,5},{8,10},{9,11},{10,... | collective-permute-start | bytes 196616 | tf_op jit(solution)/shard_map/ppermute | solution.py:294
  55.7 9.2 %collective-permute-start.5 = (bf16[8,4096]{1,0:T(8,128)(2,1)S(1)}, bf16[8,4096]{1,0:T(8,128)(2,1)S(1)}, u32[]{:S(2)}, u32[]{:S(2)}) collective-permute-start(bf16[8,4096]{1,0:T(8,128)(2,1)S(1)} %get-tuple-element.39), channel_id=1, source_target_pairs={{0,3},{1,0},{2,1},{3,2},{4,7},{5,4},{6,5},{7,6},{8,11},{9,8},{10,9... | collective-permute-start | bytes 196616 | tf_op jit(solution)/shard_map/ppermute | solution.py:294
  66.1 24.1 %copy-start.2 = (bf16[1,4096]{1,0:T(2,128)(2,1)S(1)}, bf16[1,4096]{1,0:T(2,128)(2,1)}, u32[]{:S(2)}) copy-start(bf16[1,4096]{1,0:T(2,128)(2,1)} %gain_ref.1) | copy-start | bytes 24580
  66.1 24.1 %all-to-all-start.1 = ((bf16[8,32,1024]{2,1,0:T(8,128)(2,1)}), bf16[8,32,1024]{2,1,0:T(8,128)(2,1)S(1)}, u32[]{:S(2)}, u32[]{:S(2)}) async-start(bf16[8,32,1024]{2,1,0:T(8,128)(2,1)} %page_sum.1), calls=%async_computation.1 | async-start | bytes 1048576 | tf_op jit(solution)/shard_map/all_to_all | solution.py:346
  73.2 10.9 %collective-permute-start.7 = (bf16[64,1024]{1,0:T(8,128)(2,1)S(1)}, bf16[64,1024]{1,0:T(8,128)(2,1)S(1)}, u32[]{:S(2)}, u32[]{:S(2)}) collective-permute-start(bf16[64,1024]{1,0:T(8,128)(2,1)S(1)} %pad_maximum_fusion), channel_id=1, source_target_pairs={{0,24},{4,44},{8,32},{12,52},{16,40},{20,60},{24,48},{28,4},{32,56... | collective-permute-start | bytes 393224 | tf_op jit(solution)/shard_map/ppermute | solution.py:300
  84.1 3.7 %collective-permute-start.8 = (bf16[7,32,1024]{2,1,0:T(8,128)(2,1)S(1)}, bf16[7,32,1024]{2,1,0:T(8,128)(2,1)S(1)}, u32[]{:S(2)}, u32[]{:S(2)}) collective-permute-start(bf16[7,32,1024]{2,1,0:T(8,128)(2,1)S(1)} %weight_rows.1.near_ref), channel_id=1, source_target_pairs={{0,4},{4,0},{1,5},{5,1},{2,6},{6,2},{3,7},{7,3},{8,12},{12,8},{9,1... | collective-permute-start | bytes 1376264 | tf_op jit(solution)/shard_map/ppermute | solution.py:289
  90.7 28.5 %copy-start.3 = (bf16[32,4096]{1,0:T(8,128)(2,1)S(1)}, bf16[32,4096]{1,0:T(8,128)(2,1)}, u32[]{:S(2)}) copy-start(bf16[32,4096]{1,0:T(8,128)(2,1)} %param.18) | copy-start | bytes 786436

commit v8 on v5

--- a/solution.py
+++ b/solution.py
@@ -327,11 +327,10 @@
     outgoing, weight, hidden = lax.optimization_barrier((outgoing, kv_weight[0], hidden))
     outgoing = outgoing.reshape(devices, -1, WIDE // 2)
     incoming = lax.all_to_all(outgoing, RESP_AXES, split_axis=0, concat_axis=0, tiled=True)
-    layers = [hidden, hand_over(hidden, 1)]
     sibling = swap(weight)
     both, hidden = lax.optimization_barrier((jnp.concatenate([weight, sibling], axis=0), hidden))
     near = [part_ways(both, 1), part_ways(both, 2)]
-    layers += [hand_over(hidden, k) for k in range(2, sections)]
+    layers = [hidden] + [hand_over(hidden, k) for k in range(1, sections)]
     query_out = query_gradient(score_grad, resp_kv[0], prompt_kv[0])
     incoming, both, near, layers, weight, query_out = lax.optimization_barrier(
         (incoming, both, near, layers, weight, query_out)

time: 117 us -> 117 us (level)
  transfers between devices with their start and end apart: 11 -> 11, of which waited for: 3 -> 4; matrix products, arithmetic and copies ran while one was open for 0% -> 0% of each run, Pallas kernels for 4% -> 4%
where the time goes in v8:
time: 117 us
  starting transfers between devices  54.9 us (47%)
  blocking collectives  32.5 us (28%)
  waiting for transfers between devices  13.7 us (12%)
  Pallas kernels  13.5 us (12%)
    all_to_all x1, blocking collectives, finish(): lax.all_to_all(scaled, ('z', 'section'), split_axis=0, concat_axis=0, til...  23.2 us
    all_to_all x1, starting transfers between devices, body(): lax.all_to_all(outgoing, RESP_AXES, split_axis=0, concat_axis=0, tiled=True)  17.4 us
    ppermute x4, starting transfers between devices, turn(): return lax.ppermute(piece, axis, [(i, (i + k) % size) for i in range(size)])  15.6 us
    ppermute x3, starting transfers between devices, part_ways(): return lax.ppermute(piece, ('y', 'core'), pairs)  14.4 us
    all_to_all x1, blocking collectives, finish(): lax.all_to_all(sums.reshape(sections, quarter, width), 'section', split_a...  9.33 us
    pallas_call x1, Pallas kernels, attention(): pl.pallas_call(attention_kernel, grid_spec=pltpu.PrefetchScalarGridSpec(n...  7.11 us
    ppermute x4, waiting for transfers between devices, turn(): return lax.ppermute(piece, axis, [(i, (i + k) % size) for i in range(size)])  6.91 us
    pallas_call x1, Pallas kernels, query_gradient(): pl.pallas_call(query_kernel, grid=(count,), in_specs=[pl.BlockSpec((KVH,)...  4.21 us
  transfers between devices with their start and end apart: 11, of which 4 were waited for; matrix products, arithmetic and copies ran while one was open for 0% of the time, Pallas kernels for 4%

profile of v8, /device:TPU:16, one launch (start us, length us, event | category | flops | bytes accessed | tf_op | source)
XLA Modules:
  0.0 116.6 jit_solution(1375991618057598867)
XLA Ops:
  0.6 7.1 %attention_backward.1 = (bf16[16,160,256]{2,1,0:T(8,128)(2,1)}, bf16[128,1024]{1,0:T(8,128)(2,1)}, bf16[1024,512]{1,0:T(8,128)(2,1)}) custom-call(s32[512]{0:T(512)} %groups.1, s32[4]{0:T(128)} %lengths.1, bf16[128,4096]{1,0:T(8,128)(2,1)} %bitcast.42, bf16[128,4096]{1,0:T(8,128)(2,1)} %bitcast.43, bf16[128,1024]{1,0:T(8,128)(2,1)} %bitcast.40, ...), custom_call_target="tpu_custom_call" | custom-call | flops 1000000000 | bytes 6000000 | tf_op jit(solution)/shard_map/attention_backward/pallas_call | solution.py:97
  7.7 0.0 copy-start.1
  7.8 0.0 copy-start
  7.8 0.0 copy-start.4
  7.8 17.4 %all-to-all-start = ((bf16[128,8,512]{2,1,0:T(8,128)(2,1)}), bf16[128,8,512]{2,1,0:T(8,128)(2,1)S(1)}, u32[]{:S(2)}, u32[]{:S(2)}) async-start(bf16[128,8,512]{2,1,0:T(8,128)(2,1)} %bitcast.39), calls=%async_computation | async-start | bytes 2097152 | tf_op jit(solution)/shard_map/all_to_all | solution.py:329
  25.2 2.1 %collective-permute-start = (bf16[32,1024]{1,0:T(8,128)(2,1)S(1)}, bf16[32,1024]{1,0:T(8,128)(2,1)S(1)}, u32[]{:S(2)}, u32[]{:S(2)}) collective-permute-start(bf16[32,1024]{1,0:T(8,128)(2,1)S(1)} %bitcast.32), channel_id=1, source_target_pairs={{0,4},{4,0},{1,5},{5,1},{2,6},{6,2},{3,7},{7,3},{8,12},{12,8},{9,1... | collective-permute-start | bytes 196616 | tf_op jit(solution)/shard_map/ppermute | solution.py:289
  27.3 1.1 collective-permute-done.sibling_ref
  28.4 3.4 %collective-permute-start.1 = (bf16[64,1024]{1,0:T(8,128)(2,1)S(1)}, bf16[64,1024]{1,0:T(8,128)(2,1)S(1)}, u32[]{:S(2)}, u32[]{:S(2)}) collective-permute-start(bf16[64,1024]{1,0:T(8,128)(2,1)S(1)} %pad_maximum_fusion), channel_id=1, source_target_pairs={{0,8},{4,60},{8,16},{12,4},{16,24},{20,12},{24,32},{28,20},{32,40}... | collective-permute-start | bytes 393224 | tf_op jit(solution)/shard_map/ppermute | solution.py:300
  31.7 4.6 %collective-permute-start.2 = (bf16[64,1024]{1,0:T(8,128)(2,1)S(1)}, bf16[64,1024]{1,0:T(8,128)(2,1)S(1)}, u32[]{:S(2)}, u32[]{:S(2)}) collective-permute-start(bf16[64,1024]{1,0:T(8,128)(2,1)S(1)} %pad_maximum_fusion), channel_id=1, source_target_pairs={{0,16},{4,52},{8,24},{12,60},{16,32},{20,4},{24,40},{28,12},{32,48... | collective-permute-start | bytes 393224 | tf_op jit(solution)/shard_map/ppermute | solution.py:300
  36.4 3.4 %collective-permute-start.3 = (bf16[8,4096]{1,0:T(8,128)(2,1)S(1)}, bf16[8,4096]{1,0:T(8,128)(2,1)S(1)}, u32[]{:S(2)}, u32[]{:S(2)}) collective-permute-start(bf16[8,4096]{1,0:T(8,128)(2,1)S(1)} %get-tuple-element.41), channel_id=1, source_target_pairs={{0,1},{1,2},{2,3},{3,0},{4,5},{5,6},{6,7},{7,4},{8,9},{9,10},{10,1... | collective-permute-start | bytes 196616 | tf_op jit(solution)/shard_map/ppermute | solution.py:294
  39.8 4.6 %collective-permute-start.4 = (bf16[8,4096]{1,0:T(8,128)(2,1)S(1)}, bf16[8,4096]{1,0:T(8,128)(2,1)S(1)}, u32[]{:S(2)}, u32[]{:S(2)}) collective-permute-start(bf16[8,4096]{1,0:T(8,128)(2,1)S(1)} %get-tuple-element.40), channel_id=1, source_target_pairs={{0,2},{1,3},{2,0},{3,1},{4,6},{5,7},{6,4},{7,5},{8,10},{9,11},{10,... | collective-permute-start | bytes 196616 | tf_op jit(solution)/shard_map/ppermute | solution.py:294
  44.4 3.3 %collective-permute-start.5 = (bf16[8,4096]{1,0:T(8,128)(2,1)S(1)}, bf16[8,4096]{1,0:T(8,128)(2,1)S(1)}, u32[]{:S(2)}, u32[]{:S(2)}) collective-permute-start(bf16[8,4096]{1,0:T(8,128)(2,1)S(1)} %get-tuple-element.39), channel_id=1, source_target_pairs={{0,3},{1,0},{2,1},{3,2},{4,7},{5,4},{6,5},{7,6},{8,11},{9,8},{10,9... | collective-permute-start | bytes 196616 | tf_op jit(solution)/shard_map/ppermute | solution.py:294
  47.8 0.1 broadcast_in_dim.14
  47.9 0.2 broadcast_in_dim_reshape.3.groups_ref
  48.1 4.2 %query_gradient.1 = bf16[128,4096]{1,0:T(8,128)(2,1)} custom-call(bf16[16,160,256]{2,1,0:T(8,128)(2,1)} %get-tuple-element.27.grad_ref, bf16[128,1024]{1,0:T(8,128)(2,1)} %bitcast.41, bf16[4,128,1024]{2,1,0:T(8,128)(2,1)} %bitcast.37), custom_call_target="tpu_custom_call" | custom-call | flops 200000000 | bytes 4000000 | tf_op jit(solution)/shard_map/query_gradient/pallas_call | solution.py:142
  52.3 0.0 collective-permute-done.3.refs_0_
  52.3 0.0 collective-permute-done.4.refs_1_
  52.3 0.0 collective-permute-done.2.refs_1_
  52.3 3.9 %all-to-all-done = bf16[128,8,512]{2,1,0:T(8,128)(2,1)S(1)} async-done(((bf16[128,8,512]{2,1,0:T(8,128)(2,1)}), bf16[128,8,512]{2,1,0:T(8,128)(2,1)S(1)}, u32[]{:S(2)}, u32[]{:S(2)}) %all-to-all-start) | async-done | bytes 1048608 | tf_op jit(solution)/shard_map/all_to_all | solution.py:329
  56.2 1.1 page_sum.1
  57.4 3.6 %all-to-all-start.1 = ((bf16[8,32,1024]{2,1,0:T(8,128)(2,1)}), bf16[8,32,1024]{2,1,0:T(8,128)(2,1)S(1)}, u32[]{:S(2)}, u32[]{:S(2)}) async-start(bf16[8,32,1024]{2,1,0:T(8,128)(2,1)} %page_sum.1), calls=%async_computation.1 | async-start | bytes 1048576 | tf_op jit(solution)/shard_map/all_to_all | solution.py:345
  61.0 6.4 %collective-permute-start.6 = (bf16[64,1024]{1,0:T(8,128)(2,1)S(1)}, bf16[64,1024]{1,0:T(8,128)(2,1)S(1)}, u32[]{:S(2)}, u32[]{:S(2)}) collective-permute-start(bf16[64,1024]{1,0:T(8,128)(2,1)S(1)} %pad_maximum_fusion), channel_id=1, source_target_pairs={{0,24},{4,44},{8,32},{12,52},{16,40},{20,60},{24,48},{28,4},{32,56... | collective-permute-start | bytes 393224 | tf_op jit(solution)/shard_map/ppermute | solution.py:300
  67.4 4.2 %collective-permute-start.7 = (bf16[32,1024]{1,0:T(8,128)(2,1)S(1)}, bf16[32,1024]{1,0:T(8,128)(2,1)S(1)}, u32[]{:S(2)}, u32[]{:S(2)}) collective-permute-start(bf16[32,1024]{1,0:T(8,128)(2,1)S(1)} %bitcast.34), channel_id=1, source_target_pairs={{0,32},{8,40},{16,48},{24,56},{32,0},{40,8},{48,16},{56,24},{1,33}... | collective-permute-start | bytes 196616 | tf_op jit(solution)/shard_map/ppermute | solution.py:294
  71.6 6.9 %collective-permute-done.7.refs_3_ = bf16[32,1024]{1,0:T(8,128)(2,1)S(1)} collective-permute-done((bf16[32,1024]{1,0:T(8,128)(2,1)S(1)}, bf16[32,1024]{1,0:T(8,128)(2,1)S(1)}, u32[]{:S(2)}, u32[]{:S(2)}) %collective-permute-start.7) | collective-permute-done | bytes 65568 | tf_op jit(solution)/shard_map/ppermute | solution.py:294
  78.6 1.9 %collective-permute-start.8 = (bf16[7,32,1024]{2,1,0:T(8,128)(2,1)S(1)}, bf16[7,32,1024]{2,1,0:T(8,128)(2,1)S(1)}, u32[]{:S(2)}, u32[]{:S(2)}) collective-permute-start(bf16[7,32,1024]{2,1,0:T(8,128)(2,1)S(1)} %weight_rows.1.near_ref), channel_id=1, source_target_pairs={{0,4},{4,0},{1,5},{5,1},{2,6},{6,2},{3,7},{7,3},{8,12},{12,8},{9,1... | collective-permute-start | bytes 1376264 | tf_op jit(solution)/shard_map/ppermute | solution.py:289
  80.5 1.8 %collective-permute-done.8.far_ref = bf16[7,32,1024]{2,1,0:T(8,128)(2,1)S(1)} collective-permute-done((bf16[7,32,1024]{2,1,0:T(8,128)(2,1)S(1)}, bf16[7,32,1024]{2,1,0:T(8,128)(2,1)S(1)}, u32[]{:S(2)}, u32[]{:S(2)}) %collective-permute-start.8) | collective-permute-done | bytes 458784 | tf_op jit(solution)/shard_map/ppermute | solution.py:289
  82.3 0.6 projection.1
  82.9 0.0 copy-start.3
  82.9 23.2 %all_to_all.20 = bf16[32,8,512]{2,1,0:T(8,128)(2,1)S(1)} all-to-all(bf16[32,8,512]{2,1,0:T(8,128)(2,1)S(1)} %bitcast.27), channel_id=1, replica_groups=mesh['z'=8,'y'=8,'core'=2,'section'=4] {'z','section'}, dimensions={0} | all-to-all | bytes 524288 | tf_op jit(solution)/shard_map/all_to_all | solution.py:275
  106.1 0.4 norm_terms.1
  106.5 9.3 %all_to_all.21 = bf16[4,8,4096]{2,1,0:T(8,128)(2,1)S(1)} all-to-all(bf16[4,8,4096]{2,1,0:T(8,128)(2,1)S(1)} %bitcast.29), channel_id=1, replica_groups=mesh['z'=8,'y'=8,'core'=2,'section'=4] {'section'}, dimensions={0} | all-to-all | bytes 524288 | tf_op jit(solution)/shard_map/all_to_all | solution.py:284
  115.9 0.8 fusion.1
  (13 shorter events, 0.1 us)
Async XLA Ops:
  7.7 17.4 %copy-start.1 = (bf16[1,32,1024]{2,1,0:T(8,128)(2,1)S(1)}, bf16[1,32,1024]{2,1,0:T(8,128)(2,1)}, u32[]{:S(2)}) copy-start(bf16[1,32,1024]{2,1,0:T(8,128)(2,1)} %param.17) | copy-start | bytes 196612
  7.8 28.6 %copy-start = (bf16[1,32,4096]{2,1,0:T(8,128)(2,1)S(1)}, bf16[1,32,4096]{2,1,0:T(8,128)(2,1)}, u32[]{:S(2)}) copy-start(bf16[1,32,4096]{2,1,0:T(8,128)(2,1)} %param.15) | copy-start | bytes 786436
  7.8 40.0 %copy-start.4 = (s32[512]{0:T(512)S(1)}, s32[512]{0:T(512)}, u32[]{:S(2)}) copy-start(s32[512]{0:T(512)} %groups.1) | copy-start | bytes 6148
  7.8 48.5 %all-to-all-start = ((bf16[128,8,512]{2,1,0:T(8,128)(2,1)}), bf16[128,8,512]{2,1,0:T(8,128)(2,1)S(1)}, u32[]{:S(2)}, u32[]{:S(2)}) async-start(bf16[128,8,512]{2,1,0:T(8,128)(2,1)} %bitcast.39), calls=%async_computation | async-start | bytes 2097152 | tf_op jit(solution)/shard_map/all_to_all | solution.py:329
  25.2 3.1 %collective-permute-start = (bf16[32,1024]{1,0:T(8,128)(2,1)S(1)}, bf16[32,1024]{1,0:T(8,128)(2,1)S(1)}, u32[]{:S(2)}, u32[]{:S(2)}) collective-permute-start(bf16[32,1024]{1,0:T(8,128)(2,1)S(1)} %bitcast.32), channel_id=1, source_target_pairs={{0,4},{4,0},{1,5},{5,1},{2,6},{6,2},{3,7},{7,3},{8,12},{12,8},{9,1... | collective-permute-start | bytes 196616 | tf_op jit(solution)/shard_map/ppermute | solution.py:289
  28.4 24.0 %collective-permute-start.1 = (bf16[64,1024]{1,0:T(8,128)(2,1)S(1)}, bf16[64,1024]{1,0:T(8,128)(2,1)S(1)}, u32[]{:S(2)}, u32[]{:S(2)}) collective-permute-start(bf16[64,1024]{1,0:T(8,128)(2,1)S(1)} %pad_maximum_fusion), channel_id=1, source_target_pairs={{0,8},{4,60},{8,16},{12,4},{16,24},{20,12},{24,32},{28,20},{32,40}... | collective-permute-start | bytes 393224 | tf_op jit(solution)/shard_map/ppermute | solution.py:300
  31.7 20.6 %collective-permute-start.2 = (bf16[64,1024]{1,0:T(8,128)(2,1)S(1)}, bf16[64,1024]{1,0:T(8,128)(2,1)S(1)}, u32[]{:S(2)}, u32[]{:S(2)}) collective-permute-start(bf16[64,1024]{1,0:T(8,128)(2,1)S(1)} %pad_maximum_fusion), channel_id=1, source_target_pairs={{0,16},{4,52},{8,24},{12,60},{16,32},{20,4},{24,40},{28,12},{32,48... | collective-permute-start | bytes 393224 | tf_op jit(solution)/shard_map/ppermute | solution.py:300
  36.4 15.9 %collective-permute-start.3 = (bf16[8,4096]{1,0:T(8,128)(2,1)S(1)}, bf16[8,4096]{1,0:T(8,128)(2,1)S(1)}, u32[]{:S(2)}, u32[]{:S(2)}) collective-permute-start(bf16[8,4096]{1,0:T(8,128)(2,1)S(1)} %get-tuple-element.41), channel_id=1, source_target_pairs={{0,1},{1,2},{2,3},{3,0},{4,5},{5,6},{6,7},{7,4},{8,9},{9,10},{10,1... | collective-permute-start | bytes 196616 | tf_op jit(solution)/shard_map/ppermute | solution.py:294
  39.8 12.5 %collective-permute-start.4 = (bf16[8,4096]{1,0:T(8,128)(2,1)S(1)}, bf16[8,4096]{1,0:T(8,128)(2,1)S(1)}, u32[]{:S(2)}, u32[]{:S(2)}) collective-permute-start(bf16[8,4096]{1,0:T(8,128)(2,1)S(1)} %get-tuple-element.40), channel_id=1, source_target_pairs={{0,2},{1,3},{2,0},{3,1},{4,6},{5,7},{6,4},{7,5},{8,10},{9,11},{10,... | collective-permute-start | bytes 196616 | tf_op jit(solution)/shard_map/ppermute | solution.py:294
  44.4 7.9 %collective-permute-start.5 = (bf16[8,4096]{1,0:T(8,128)(2,1)S(1)}, bf16[8,4096]{1,0:T(8,128)(2,1)S(1)}, u32[]{:S(2)}, u32[]{:S(2)}) collective-permute-start(bf16[8,4096]{1,0:T(8,128)(2,1)S(1)} %get-tuple-element.39), channel_id=1, source_target_pairs={{0,3},{1,0},{2,1},{3,2},{4,7},{5,4},{6,5},{7,6},{8,11},{9,8},{10,9... | collective-permute-start | bytes 196616 | tf_op jit(solution)/shard_map/ppermute | solution.py:294
  57.4 24.9 %copy-start.2 = (bf16[1,4096]{1,0:T(2,128)(2,1)S(1)}, bf16[1,4096]{1,0:T(2,128)(2,1)}, u32[]{:S(2)}) copy-start(bf16[1,4096]{1,0:T(2,128)(2,1)} %gain_ref.1) | copy-start | bytes 24580
  57.4 24.9 %all-to-all-start.1 = ((bf16[8,32,1024]{2,1,0:T(8,128)(2,1)}), bf16[8,32,1024]{2,1,0:T(8,128)(2,1)S(1)}, u32[]{:S(2)}, u32[]{:S(2)}) async-start(bf16[8,32,1024]{2,1,0:T(8,128)(2,1)} %page_sum.1), calls=%async_computation.1 | async-start | bytes 1048576 | tf_op jit(solution)/shard_map/all_to_all | solution.py:345
  61.0 17.5 %collective-permute-start.6 = (bf16[64,1024]{1,0:T(8,128)(2,1)S(1)}, bf16[64,1024]{1,0:T(8,128)(2,1)S(1)}, u32[]{:S(2)}, u32[]{:S(2)}) collective-permute-start(bf16[64,1024]{1,0:T(8,128)(2,1)S(1)} %pad_maximum_fusion), channel_id=1, source_target_pairs={{0,24},{4,44},{8,32},{12,52},{16,40},{20,60},{24,48},{28,4},{32,56... | collective-permute-start | bytes 393224 | tf_op jit(solution)/shard_map/ppermute | solution.py:300
  67.4 11.1 %collective-permute-start.7 = (bf16[32,1024]{1,0:T(8,128)(2,1)S(1)}, bf16[32,1024]{1,0:T(8,128)(2,1)S(1)}, u32[]{:S(2)}, u32[]{:S(2)}) collective-permute-start(bf16[32,1024]{1,0:T(8,128)(2,1)S(1)} %bitcast.34), channel_id=1, source_target_pairs={{0,32},{8,40},{16,48},{24,56},{32,0},{40,8},{48,16},{56,24},{1,33}... | collective-permute-start | bytes 196616 | tf_op jit(solution)/shard_map/ppermute | solution.py:294
  78.6 3.7 %collective-permute-start.8 = (bf16[7,32,1024]{2,1,0:T(8,128)(2,1)S(1)}, bf16[7,32,1024]{2,1,0:T(8,128)(2,1)S(1)}, u32[]{:S(2)}, u32[]{:S(2)}) collective-permute-start(bf16[7,32,1024]{2,1,0:T(8,128)(2,1)S(1)} %weight_rows.1.near_ref), channel_id=1, source_target_pairs={{0,4},{4,0},{1,5},{5,1},{2,6},{6,2},{3,7},{7,3},{8,12},{12,8},{9,1... | collective-permute-start | bytes 1376264 | tf_op jit(solution)/shard_map/ppermute | solution.py:289
  82.9 33.0 %copy-start.3 = (bf16[32,4096]{1,0:T(8,128)(2,1)S(1)}, bf16[32,4096]{1,0:T(8,128)(2,1)}, u32[]{:S(2)}) copy-start(bf16[32,4096]{1,0:T(8,128)(2,1)} %param.18) | copy-start | bytes 786436
